TPU v7x, 32 devices: a whole 2x2x4 slice. The times are simulated.
32 devices in a mesh: orig: 8 (over y, x, core), dest: 4 (over z).
Axes of the slice: x: 2, y: 2, z: 4, core: 2. Of those that a mesh axis runs over, the one named last changes fastest.
Arguments:
- pair_field: bfloat16 [64, 64, 128], P('orig', 'dest'), may hold values from -6 to 6
- region_mask: int32 [64], replicated, may hold values 0 or 1
- region_count: int32 [1], replicated, may hold values from 1 to 64
- row_query: bfloat16 [1, 128, 128], replicated, may hold values from -17.5 to 17.5, as said below
- row_key: bfloat16 [1, 128, 128], replicated, may hold values from -0.36 to 0.36, as said below
- row_value: bfloat16 [1, 128, 128], replicated, may hold values from -0.5 to 0.5
- row_gate: bfloat16 [1, 128, 128], replicated, may hold values from -0.5 to 0.5
- row_gate_bias: float32 [1, 128], replicated, may hold values from -4 to 4
- row_out: bfloat16 [1, 128, 128], replicated, may hold values from -1.5 to 1.5
- col_query: bfloat16 [1, 128, 128], replicated, may hold values from -17.5 to 17.5, as said below
- col_key: bfloat16 [1, 128, 128], replicated, may hold values from -0.36 to 0.36, as said below
- col_value: bfloat16 [1, 128, 128], replicated, may hold values from -0.5 to 0.5
- col_gate: bfloat16 [1, 128, 128], replicated, may hold values from -0.5 to 0.5
- col_gate_bias: float32 [1, 128], replicated, may hold values from -4 to 4
- col_out: bfloat16 [1, 128, 128], replicated, may hold values from -1.5 to 1.5
Outputs:
- new_pair: bfloat16 [64, 64, 128], P('orig', 'dest')
Inputs may be any that keep to these rules, and one draw needn't show every extreme that they name: `row_query`: row attention query weights. `row_key`: row attention key weights. `col_query`: column attention query weights. `col_key`: column attention key weights.
All inputs are finite; a program needn't handle non-finite values.
Results may differ from a plain program's by a relative error of at most 0.012.
Values may be sent and summed in bfloat16 or wider, within the bound.
No kernel may reach another device: no remote copies, remote signals or barrier semaphores. Data moves between devices by JAX's collectives and lax.ppermute only.
A program may use at most 64 MiB of HBM per device.

v0:
```python
import math

import jax
import jax.numpy as jnp
from jax import lax
from jax.sharding import PartitionSpec as P

H = 4


epsilon = 1e-05
masked_score = -1e30


def normalize(pair_rows):
    widened = pair_rows.astype(jnp.float32)
    centered = widened - jnp.mean(widened, axis=-1, keepdims=True)
    variance = jnp.mean(centered * centered, axis=-1, keepdims=True)
    return (centered * lax.rsqrt(variance + epsilon)).astype(jnp.bfloat16)


def attend_heads(queries, key_rows, value_rows, valid_keys):
    items, length, channels = queries.shape
    head_size = channels // H
    block = min(512, length)
    count = length // block

    def heads_first(values):
        return jnp.transpose(values.reshape(items, length, H, head_size), (0, 2, 1, 3))

    query_heads = heads_first(queries).reshape(items * H, count, block, head_size)
    key_heads = heads_first(key_rows).reshape(items * H, length, head_size)
    value_heads = heads_first(value_rows).reshape(items * H, length, head_size)

    def one_head(operands):
        head_queries, head_keys, head_values = operands

        def one_block(block_queries):
            scores = jnp.einsum(
                "qd,kd->qk", block_queries, head_keys, preferred_element_type=jnp.float32
            ) / math.sqrt(head_size)
            scores = jnp.where(valid_keys[None, :], scores, masked_score)
            maximum = jnp.max(scores, axis=1, keepdims=True)
            expanded = jnp.exp(scores - maximum)
            weights = (expanded / jnp.sum(expanded, axis=1, keepdims=True)).astype(jnp.bfloat16)
            return jnp.dot(weights, head_values, preferred_element_type=jnp.float32).astype(
                jnp.bfloat16
            )

        return lax.map(one_block, head_queries)

    results = lax.map(one_head, (query_heads, key_heads, value_heads))
    return jnp.transpose(results.reshape(items, H, length, head_size), (0, 2, 1, 3)).reshape(
        items, length, channels
    )


def finish(pair_tile, normed, attended, w_gate, gate_bias, w_out, gate_form, out_form):
    gate_values = jax.nn.sigmoid(
        jnp.einsum(gate_form, normed, w_gate, preferred_element_type=jnp.float32) + gate_bias
    )
    gated = (gate_values * attended.astype(jnp.float32)).astype(jnp.bfloat16)
    update = jnp.einsum(out_form, gated, w_out, preferred_element_type=jnp.float32)
    return (pair_tile.astype(jnp.float32) + update).astype(jnp.bfloat16)


def attend_pairs(pair_rows, weights, valid_keys):
    w_query, w_key, w_value, w_gate, gate_bias, w_out = weights
    normed = normalize(pair_rows)
    stacked = jnp.stack((w_query, w_key, w_value))
    projected = jnp.einsum(
        "nrc,scm->snrm", normed, stacked, preferred_element_type=jnp.float32
    ).astype(jnp.bfloat16)
    attended = attend_heads(projected[0], projected[1], projected[2], valid_keys)
    return finish(
        pair_rows, normed, attended, w_gate, gate_bias, w_out, "nrc,cm->nrm", "nrm,mc->nrc"
    )


def body(
    pair_field,
    region_mask,
    region_count,
    row_query,
    row_key,
    row_value,
    row_gate,
    row_gate_bias,
    row_out,
    col_query,
    col_key,
    col_value,
    col_gate,
    col_gate_bias,
    col_out,
):
    tile_rows, tile_cols, channels = pair_field.shape
    dest_size = lax.axis_size("dest")
    orig_size = lax.axis_size("orig")
    region_total = region_mask.shape[0]
    row_part = tile_rows // dest_size
    col_part = tile_cols // orig_size
    positions = jnp.arange(region_total, dtype=jnp.int32)
    valid_keys = ((region_mask == 1) | (positions == 0)) & (positions < region_count[0])
    current = pair_field
    row_weights = (
        row_query[0],
        row_key[0],
        row_value[0],
        row_gate[0],
        row_gate_bias[0],
        row_out[0],
    )
    col_weights = (
        col_query[0],
        col_key[0],
        col_value[0],
        col_gate[0],
        col_gate_bias[0],
        col_out[0],
    )
    pieces = current.reshape(dest_size, row_part, tile_cols, channels)
    rows_whole = attend_pairs(
        lax.all_to_all(pieces, "dest", split_axis=0, concat_axis=2, tiled=True)[0],
        row_weights,
        valid_keys,
    )[None]
    spread = rows_whole.reshape(1, 1, row_part, dest_size, orig_size, col_part, channels)
    columns = lax.all_to_all(
        lax.all_to_all(spread, "orig", split_axis=4, concat_axis=0, tiled=True),
        "dest",
        split_axis=3,
        concat_axis=1,
        tiled=True,
    )
    column_columns = columns.reshape(region_total, col_part, channels)
    updated = jnp.swapaxes(
        attend_pairs(jnp.swapaxes(column_columns, 0, 1), col_weights, valid_keys), 0, 1
    )
    back = lax.all_to_all(
        updated.reshape(region_total, 1, col_part, channels),
        "orig",
        split_axis=0,
        concat_axis=1,
        tiled=True,
    )
    current = back.reshape(tile_rows, tile_cols, channels)
    return current


def solution(mesh):
    in_specs = (
        P("orig", "dest", None),
        P(),
        P(),
        P(),
        P(),
        P(),
        P(),
        P(),
        P(),
        P(),
        P(),
        P(),
        P(),
        P(),
        P(),
    )
    out_specs = P("orig", "dest", None)
    return jax.shard_map(body, mesh=mesh, in_specs=in_specs, out_specs=out_specs, check_vma=False)
```

profile of v0, /device:TPU:0, one launch (start us, length us, event | category | flops | bytes accessed | tf_op | source)
XLA Modules:
  0.0 48.8 jit_solution(6063122225269515832)
XLA Ops:
  0.0 6.4 %all-to-all-start = ((bf16[4,2,16,128]{3,2,1,0:T(8,128)(2,1)}), bf16[4,2,16,128]{3,2,1,0:T(8,128)(2,1)S(1)}, u32[]{:S(2)}, u32[]{:S(2)}) async-start(bf16[4,2,16,128]{3,2,1,0:T(8,128)(2,1)} %bitcast.207), calls=%async_computation | async-start | bytes 65536 | tf_op jit(solution)/shard_map/all_to_all | solution.py:124
  7.1 0.6 %copy-done.10 = s32[64]{0:T(128)S(1)} copy-done((s32[64]{0:T(128)S(1)}, s32[64]{0:T(128)}, u32[]{:S(2)}) %copy-start.10) | copy-done | bytes 280
  7.8 4.3 %all-to-all-done = bf16[4,2,16,128]{3,2,1,0:T(8,128)(2,1)S(1)} async-done(((bf16[4,2,16,128]{3,2,1,0:T(8,128)(2,1)}), bf16[4,2,16,128]{3,2,1,0:T(8,128)(2,1)S(1)}, u32[]{:S(2)}, u32[]{:S(2)}) %all-to-all-start) | async-done | bytes 32800 | tf_op jit(solution)/shard_map/all_to_all | solution.py:124
  12.3 0.2 multiply_reduce_fusion.1
  12.6 0.7 %copy-done.1 = bf16[1,128,128]{2,1,0:T(8,128)(2,1)S(1)} copy-done((bf16[1,128,128]{2,1,0:T(8,128)(2,1)S(1)}, bf16[1,128,128]{2,1,0:T(8,128)(2,1)}, u32[]{:S(2)}) %copy-start.1) | copy-done | bytes 32792
  13.4 0.2 fusion.28
  14.0 3.2 %while.20 = (s32[]{:T(128)}, bf16[8,1,64,32]{2,3,1,0:T(8,128)(2,1)S(1)}, pred[64]{0:T(512)(128)(4,1)S(1)}, bf16[8,1,64,32]{2,3,0,1:T(8,128)(2,1)S(1)}, bf16[8,64...) while((s32[]{:T(128)}, bf16[8,1,64,32]{2,3,1,0:T(8,128)(2,1)S(1)}, ...), condition=%wide.region_5.6_spmd, body=%wide.region_2.5_spmd.sunk | while | flops 558978 | bytes 102733 | solution.py:52
  14.0 0.2 fusion.87
  14.3 0.1 fusion.89
  14.4 0.2 fusion.87
  14.7 0.1 fusion.89
  14.8 0.2 fusion.87
  15.1 0.1 fusion.89
  15.2 0.2 fusion.87
  15.5 0.1 fusion.89
  15.6 0.2 fusion.87
  15.9 0.1 fusion.89
  16.1 0.2 fusion.87
  16.3 0.1 fusion.89
  16.5 0.2 fusion.87
  16.7 0.1 fusion.89
  16.9 0.2 fusion.87
  17.5 0.6 %copy-done.4 = bf16[1,128,128]{2,1,0:T(8,128)(2,1)S(1)} copy-done((bf16[1,128,128]{2,1,0:T(8,128)(2,1)S(1)}, bf16[1,128,128]{2,1,0:T(8,128)(2,1)}, u32[]{:S(2)}) %copy-start.4) | copy-done | bytes 32792
  18.2 0.3 fusion.42
  18.5 8.4 %all_to_all.51 = bf16[1,1,2,4,8,2,128]{6,5,3,2,1,0,4:T(2,128)(2,1)S(1)} all-to-all(bf16[1,1,2,4,8,2,128]{6,5,3,2,1,0,4:T(2,128)(2,1)S(1)} %copy.74), channel_id=1, replica_groups=mesh['orig'=8,'dest'=4] {'orig'}, dimensions={4} | all-to-all | bytes 65536 | tf_op jit(solution)/shard_map/all_to_all | solution.py:130
  26.9 8.0 %all_to_all.52 = bf16[8,1,2,4,1,2,128]{6,5,0,2,4,1,3:T(2,128)(2,1)S(1)} all-to-all(bf16[8,1,2,4,1,2,128]{6,5,0,2,4,1,3:T(2,128)(2,1)S(1)} %copy.75), channel_id=1, replica_groups=mesh['orig'=8,'dest'=4] {'dest'}, dimensions={3} | all-to-all | bytes 65536 | tf_op jit(solution)/shard_map/all_to_all | solution.py:129
  35.1 0.2 multiply_reduce_fusion
  35.3 0.4 copy-done.7
  35.8 0.2 fusion.29
  36.5 3.2 %while.21 = (s32[]{:T(128)}, bf16[8,1,64,32]{2,3,1,0:T(8,128)(2,1)S(1)}, pred[64]{0:T(512)(128)(4,1)S(1)}, bf16[8,1,64,32]{2,3,0,1:T(8,128)(2,1)S(1)}, bf16[8,64...) while((s32[]{:T(128)}, bf16[8,1,64,32]{2,3,1,0:T(8,128)(2,1)S(1)}, ...), condition=%wide.region_11.12_spmd, body=%wide.region_8.11_spmd.sunk | while | flops 558978 | bytes 102733 | solution.py:52
  36.5 0.2 fusion.91
  36.8 0.1 fusion.93
  36.9 0.2 fusion.91
  37.2 0.1 fusion.93
  37.3 0.2 fusion.91
  37.6 0.1 fusion.93
  37.7 0.2 fusion.91
  38.0 0.1 fusion.93
  38.1 0.2 fusion.91
  38.4 0.1 fusion.93
  38.5 0.2 fusion.91
  38.8 0.1 fusion.93
  38.9 0.2 fusion.91
  39.3 0.2 fusion.91
  39.9 0.6 %copy-done.8 = bf16[1,128,128]{2,1,0:T(8,128)(2,1)S(1)} copy-done((bf16[1,128,128]{2,1,0:T(8,128)(2,1)S(1)}, bf16[1,128,128]{2,1,0:T(8,128)(2,1)}, u32[]{:S(2)}) %copy-start.8) | copy-done | bytes 32792
  40.5 0.3 fusion.45
  40.9 7.2 %all_to_all.53 = bf16[64,1,2,128]{3,2,1,0:T(2,128)(2,1)S(1)} all-to-all(bf16[64,1,2,128]{3,2,1,0:T(2,128)(2,1)S(1)} %copy.84), channel_id=1, replica_groups=mesh['orig'=8,'dest'=4] {'orig'}, dimensions={0} | all-to-all | bytes 65536 | tf_op jit(solution)/shard_map/all_to_all | solution.py:140
  48.1 0.6 %copy.85 = bf16[8,8,1,2,128]{4,3,1,0,2:T(2,128)(2,1)} copy(bf16[8,8,1,2,128]{4,3,0,1,2:T(2,128)(2,1)S(1)} %bitcast.198) | data formatting | bytes 65536 | tf_op jit(solution)/shard_map/all_to_all | solution.py:140
  (70 shorter events, 2.8 us)
Async XLA Ops:
  0.0 17.5 %copy-start = (bf16[1,128,128]{2,1,0:T(8,128)(2,1)S(1)}, bf16[1,128,128]{2,1,0:T(8,128)(2,1)}, u32[]{:S(2)}) copy-start(bf16[1,128,128]{2,1,0:T(8,128)(2,1)} %param.27) | copy-start | bytes 98308
  0.0 12.1 %all-to-all-start = ((bf16[4,2,16,128]{3,2,1,0:T(8,128)(2,1)}), bf16[4,2,16,128]{3,2,1,0:T(8,128)(2,1)S(1)}, u32[]{:S(2)}, u32[]{:S(2)}) async-start(bf16[4,2,16,128]{3,2,1,0:T(8,128)(2,1)} %bitcast.207), calls=%async_computation | async-start | bytes 65536 | tf_op jit(solution)/shard_map/all_to_all | solution.py:124
  7.1 0.7 %copy-start.10 = (s32[64]{0:T(128)S(1)}, s32[64]{0:T(128)}, u32[]{:S(2)}) copy-start(s32[64]{0:T(128)} %param.20) | copy-start | bytes 772
  12.6 0.8 %copy-start.1 = (bf16[1,128,128]{2,1,0:T(8,128)(2,1)S(1)}, bf16[1,128,128]{2,1,0:T(8,128)(2,1)}, u32[]{:S(2)}) copy-start(bf16[1,128,128]{2,1,0:T(8,128)(2,1)} %param.24) | copy-start | bytes 98308
  12.6 0.8 %copy-start.2 = (bf16[1,128,128]{2,1,0:T(8,128)(2,1)S(1)}, bf16[1,128,128]{2,1,0:T(8,128)(2,1)}, u32[]{:S(2)}) copy-start(bf16[1,128,128]{2,1,0:T(8,128)(2,1)} %param.23) | copy-start | bytes 98308
  12.6 0.8 %copy-start.3 = (bf16[1,128,128]{2,1,0:T(8,128)(2,1)S(1)}, bf16[1,128,128]{2,1,0:T(8,128)(2,1)}, u32[]{:S(2)}) copy-start(bf16[1,128,128]{2,1,0:T(8,128)(2,1)} %param.22) | copy-start | bytes 98308
  17.4 0.8 %copy-start.4 = (bf16[1,128,128]{2,1,0:T(8,128)(2,1)S(1)}, bf16[1,128,128]{2,1,0:T(8,128)(2,1)}, u32[]{:S(2)}) copy-start(bf16[1,128,128]{2,1,0:T(8,128)(2,1)} %param.25) | copy-start | bytes 98308
  17.5 0.7 %copy-start.11 = (f32[1,128]{1,0:T(1,128)S(1)}, f32[1,128]{1,0:T(1,128)}, u32[]{:S(2)}) copy-start(f32[1,128]{1,0:T(1,128)} %param.26) | copy-start | bytes 1540
  34.9 0.8 %copy-start.7 = (bf16[1,128,128]{2,1,0:T(8,128)(2,1)S(1)}, bf16[1,128,128]{2,1,0:T(8,128)(2,1)}, u32[]{:S(2)}) copy-start(bf16[1,128,128]{2,1,0:T(8,128)(2,1)} %param.28) | copy-start | bytes 98308
  35.1 0.8 %copy-start.5 = (bf16[1,128,128]{2,1,0:T(8,128)(2,1)S(1)}, bf16[1,128,128]{2,1,0:T(8,128)(2,1)}, u32[]{:S(2)}) copy-start(bf16[1,128,128]{2,1,0:T(8,128)(2,1)} %param.30) | copy-start | bytes 98308
  35.1 0.8 %copy-start.6 = (bf16[1,128,128]{2,1,0:T(8,128)(2,1)S(1)}, bf16[1,128,128]{2,1,0:T(8,128)(2,1)}, u32[]{:S(2)}) copy-start(bf16[1,128,128]{2,1,0:T(8,128)(2,1)} %param.29) | copy-start | bytes 98308
  39.8 0.8 %copy-start.8 = (bf16[1,128,128]{2,1,0:T(8,128)(2,1)S(1)}, bf16[1,128,128]{2,1,0:T(8,128)(2,1)}, u32[]{:S(2)}) copy-start(bf16[1,128,128]{2,1,0:T(8,128)(2,1)} %param.33) | copy-start | bytes 98308
  39.8 0.8 %copy-start.9 = (bf16[1,128,128]{2,1,0:T(8,128)(2,1)S(1)}, bf16[1,128,128]{2,1,0:T(8,128)(2,1)}, u32[]{:S(2)}) copy-start(bf16[1,128,128]{2,1,0:T(8,128)(2,1)} %param.31) | copy-start | bytes 98308
  39.9 0.7 %copy-start.12 = (f32[1,128]{1,0:T(1,128)S(1)}, f32[1,128]{1,0:T(1,128)}, u32[]{:S(2)}) copy-start(f32[1,128]{1,0:T(1,128)} %param.32) | copy-start | bytes 1540
where the time goes:
time: 49.4 us; the launch traced here: 48.8 us
  blocking collectives  23.6 us (48%)
  matrix products  6.91 us (14%)
  starting transfers between devices  6.45 us (13%)
  local copies, waits for them, and re-layouts  5.2 us (11%)
  waiting for transfers between devices  4.34 us (9%)
  other arithmetic  1.28 us (3%)
  between operations  0.96 us (2%)
    all_to_all x1, blocking collectives, body(): lax.all_to_all(spread, 'orig', split_axis=4, concat_axis=0, tiled=True)  8.36 us
    all_to_all x1, blocking collectives, body(): lax.all_to_all(lax.all_to_all(spread, 'orig', split_axis=4, concat_axis=0...  8.01 us
    all_to_all x1, blocking collectives, body(): lax.all_to_all(updated.reshape(region_total, 1, col_part, channels), 'ori...  7.22 us
    all_to_all x1, starting transfers between devices, body(): lax.all_to_all(pieces, 'dest', split_axis=0, concat_axis=2, tiled=True)[0]  6.45 us
    all_to_all x1, waiting for transfers between devices, body(): lax.all_to_all(pieces, 'dest', split_axis=0, concat_axis=2, tiled=True)[0]  4.34 us
    dot_general x16, matrix products, one_block(): jnp.einsum('qd,kd->qk', block_queries, head_keys, preferred_element_type=...  3.58 us
    unnamed x26, local copies, waits for them, and re-layouts  3.34 us
    dot_general x16, matrix products, one_block(): jnp.dot(weights, head_values, preferred_element_type=jnp.float32)  2.27 us
  transfers between devices with their start and end apart: 1, of which 1 were waited for; matrix products, arithmetic and copies ran while one was open for 0% of the time, Pallas kernels for 0%

commit v1 on v0

v1 whole, which is shorter than its diff:
```python
import functools
import math

import jax
import jax.numpy as jnp
from jax import lax
from jax.experimental import pallas as pl
from jax.experimental.pallas import tpu as pltpu
from jax.sharding import PartitionSpec as P

H = 4

epsilon = 1e-05
masked_score = -1e30
lanes = 128
group_rows = 1024

vmem = pl.BlockSpec(memory_space=pltpu.VMEM)


def packing(items, length):
    pack = max(p for p in range(1, items + 1) if items % p == 0 and (p == 1 or p * length <= lanes))
    group = max(
        g
        for g in range(pack, items + 1, pack)
        if items % g == 0 and (g == pack or g * length <= group_rows)
    )
    return pack, group


def prepare_kernel(axes, steps, parts, packs, mask_ref, count_ref, *refs):
    weights, gate_biases, outs, sem = refs[:10], refs[10:12], refs[12:18], refs[18]
    channels = weights[0].shape[1]
    copies = []
    for a in range(2):
        for w in range(5):
            copies.append(
                pltpu.make_async_copy(
                    weights[5 * a + w].at[0],
                    outs[3 * a].at[:, pl.ds(w * channels, channels)],
                    sem.at[len(copies)],
                )
            )
        copies.append(pltpu.make_async_copy(gate_biases[a], outs[3 * a + 1], sem.at[len(copies)]))
    for copy in copies:
        copy.start()
    regions = mask_ref.shape[1]
    place = lax.broadcasted_iota(jnp.int32, (8, regions), 1)
    valid = ((mask_ref[...] == 1) | (place == 0)) & (place < count_ref[0])
    valid = jnp.where(valid, 1.0, 0.0).astype(jnp.bfloat16)
    for a in range(2):
        me = lax.axis_index(axes[a])
        part, pack = parts[a], packs[a]
        shape = (regions, pack * regions)
        lane = lax.broadcasted_iota(jnp.int32, (1, shape[1]), 1)
        block = lane // (part * pack)
        odd = me % 2 == 1
        step = jnp.zeros_like(lane)
        for b, (for_even, for_odd) in enumerate(steps[a]):
            step = jnp.where(block == b, jnp.where(odd, for_odd, for_even), step)
        region = (step ^ me) * part + lane % part
        hit = lax.broadcasted_iota(jnp.int32, shape, 0) == region
        found = jnp.dot(
            valid, jnp.where(hit, 1.0, 0.0).astype(jnp.bfloat16), preferred_element_type=jnp.float32
        )
        outs[3 * a + 2][...] = jnp.where(found[:1] > 0.5, 0.0, masked_score)
    for copy in copies:
        copy.wait()


def prepare(axes, steps, parts, packs, region_mask, region_count, weights, gate_biases):
    regions = region_mask.shape[0]
    channels = weights[0].shape[-1]
    outs = []
    for pack in packs:
        outs += [
            pltpu.VMEM((channels, 5 * channels), jnp.bfloat16),
            pltpu.VMEM((1, channels), jnp.float32),
            pltpu.VMEM((1, pack * regions), jnp.float32),
        ]
    return pl.pallas_call(
        functools.partial(prepare_kernel, axes, steps, parts, packs),
        out_shape=tuple(outs),
        in_specs=[vmem, pl.BlockSpec(memory_space=pltpu.SMEM)]
        + [pl.BlockSpec(memory_space=pltpu.HBM)] * 12,
        out_specs=(vmem,) * 6,
        scratch_shapes=[pltpu.SemaphoreType.DMA((12,))],
        compiler_params=pltpu.CompilerParams(vmem_limit_bytes=16 * 2**20),
        cost_estimate=pl.CostEstimate(flops=2**20, bytes_accessed=2**20, transcendentals=0),
    )(
        region_mask.reshape(1, regions),
        region_count,
        *(pltpu.with_memory_space_constraint(w, pltpu.HBM) for w in (*weights, *gate_biases)),
    )


def attend_kernel(counts, items, pack, group, *refs):
    block_refs = refs[: len(counts)]
    weight_ref, gate_bias_ref, bias_ref, out_ref, turned_ref = refs[len(counts) :]
    channels = weight_ref.shape[0]
    head_size = channels // H
    rows = out_ref.shape[0]
    part = rows // items
    step_rows, pack_rows = group * part, pack * part
    blocks = sum(counts)
    scale = math.log2(math.e) / math.sqrt(head_size)
    head_of = lax.broadcasted_iota(jnp.int32, (1, channels), 1) // head_size
    shape = (H * pack_rows, blocks * pack_rows)
    row_item = lax.broadcasted_iota(jnp.int32, shape, 0) // part % pack
    key_item = lax.broadcasted_iota(jnp.int32, shape, 1) // part % pack
    bias = jnp.where(row_item == key_item, bias_ref[...], masked_score)

    def step(start):
        x = jnp.concatenate(
            [
                ref[pl.ds(b * rows + start, step_rows), :]
                for ref, count in zip(block_refs, counts)
                for b in range(count)
            ],
            0,
        ).astype(jnp.float32)
        centered = x - jnp.mean(x, axis=1, keepdims=True)
        variance = jnp.mean(centered * centered, axis=1, keepdims=True)
        normed = (centered * lax.rsqrt(variance + epsilon)).astype(jnp.bfloat16)
        own_products = jnp.dot(
            normed[:step_rows], weight_ref[:, : 2 * channels], preferred_element_type=jnp.float32
        )
        queries = own_products[:, :channels]
        gate = jax.nn.sigmoid(own_products[:, channels:] + gate_bias_ref[...])
        products = jnp.dot(
            normed, weight_ref[:, 2 * channels : 4 * channels], preferred_element_type=jnp.float32
        ).astype(jnp.bfloat16)
        attended = []
        for i in range(group // pack):
            at = [b * step_rows + i * pack_rows for b in range(blocks)]
            both = jnp.concatenate([products[a : a + pack_rows] for a in at], 0)
            q = queries[i * pack_rows : (i + 1) * pack_rows]
            stacked = jnp.concatenate(
                [jnp.where(head_of == h, q, 0.0) for h in range(H)], 0
            ).astype(jnp.bfloat16)
            scores = (
                lax.dot_general(
                    stacked,
                    both[:, :channels],
                    (((1,), (1,)), ((), ())),
                    preferred_element_type=jnp.float32,
                )
                * scale
                + bias
            )
            expanded = jnp.exp2(scores - jnp.max(scores, axis=1, keepdims=True))
            weights = expanded * (1.0 / jnp.sum(expanded, axis=1, keepdims=True))
            heads = jnp.dot(
                weights.astype(jnp.bfloat16), both[:, channels:], preferred_element_type=jnp.float32
            )
            picked = heads[:pack_rows]
            for h in range(1, H):
                picked = jnp.where(
                    head_of == h, heads[h * pack_rows : (h + 1) * pack_rows], picked
                )
            attended.append(picked)
        attended = jnp.concatenate(attended, 0).astype(jnp.bfloat16).astype(jnp.float32)
        gated = (gate * attended).astype(jnp.bfloat16)
        return x[:step_rows] + jnp.dot(
            gated, weight_ref[:, 4 * channels :], preferred_element_type=jnp.float32
        )

    def one_group(g, start):
        result = step(start)
        for i in range(group):
            turned_ref[pl.ds(g * group + i, part, stride=items), :] = result[
                i * part : (i + 1) * part
            ]

    if group == items:
        one_group(0, 0)
    else:

        def body(g, carry):
            one_group(g, pl.multiple_of(g * step_rows, step_rows))
            return carry

        lax.fori_loop(0, items // group, body, 0)
    out_ref[...] = turned_ref[...].astype(out_ref.dtype)


def attend(blocks, counts, items, pack, group, prepared):
    rows, channels = blocks[0].shape[0] // counts[0], blocks[0].shape[1]
    held = sum(b.size * b.dtype.itemsize for b in blocks)
    return pl.pallas_call(
        functools.partial(attend_kernel, counts, items, pack, group),
        out_shape=jax.ShapeDtypeStruct((rows, channels), jnp.bfloat16),
        in_specs=[vmem] * (len(blocks) + len(prepared)),
        out_specs=vmem,
        scratch_shapes=[pltpu.VMEM((rows, channels), jnp.float32)],
        compiler_params=pltpu.CompilerParams(vmem_limit_bytes=held + 16 * 2**20),
    )(*blocks, *prepared)


def meet(size, step):
    return [(i, i ^ step) for i in range(size)]


def body(
    pair_field,
    region_mask,
    region_count,
    row_query,
    row_key,
    row_value,
    row_gate,
    row_gate_bias,
    row_out,
    col_query,
    col_key,
    col_value,
    col_gate,
    col_gate_bias,
    col_out,
):
    tile_rows, tile_cols, channels = pair_field.shape
    dest_size = lax.axis_size("dest")
    orig_size = lax.axis_size("orig")
    regions = region_mask.shape[0]
    row_steps = list(range(dest_size))
    near = list(range(0, orig_size, 2))
    col_steps = near + [s ^ 1 for s in near]
    row_packing = packing(tile_rows, regions)
    col_packing = packing(tile_cols, regions)
    prepared = prepare(
        ("dest", "orig"),
        ([(s, s) for s in row_steps], [(s, s) for s in col_steps]),
        (tile_cols, tile_rows),
        (row_packing[0], col_packing[0]),
        region_mask,
        region_count,
        (row_query, row_gate, row_key, row_value, row_out)
        + (col_query, col_gate, col_key, col_value, col_out),
        (row_gate_bias, col_gate_bias),
    )

    tile = pair_field.reshape(tile_rows * tile_cols, channels)
    blocks = [tile] + [lax.ppermute(tile, "dest", meet(dest_size, s)) for s in row_steps[1:]]
    turned = attend(blocks, [1] * dest_size, tile_rows, *row_packing, prepared[:3])

    held = jnp.concatenate(
        [turned] + [lax.ppermute(turned, "orig", meet(orig_size, s)) for s in near[1:]], 0
    )
    other = lax.ppermute(held, "orig", meet(orig_size, 1))
    result = attend([held, other], [len(near)] * 2, tile_cols, *col_packing, prepared[3:])
    return result.reshape(tile_rows, tile_cols, channels)


def solution(mesh):
    tile = P("orig", "dest", None)
    in_specs = (tile,) + (P(),) * 14
    return jax.shard_map(body, mesh=mesh, in_specs=in_specs, out_specs=tile, check_vma=False)
```

time: 49.4 us -> 24.2 us (0.49)
  blocking collectives: 23.6 us -> 0 us
  matrix products: 6.91 us -> 0 us
  Pallas kernels: 0 us -> 6.56 us
  local copies, waits for them, and re-layouts: 5.2 us -> 0.65 us
  starting transfers between devices: 6.45 us -> 9.23 us
  waiting for transfers between devices: 4.34 us -> 6.81 us
  other arithmetic: 1.28 us -> 0.01 us
    all_to_all x3 -> x0, blocking collectives: 23.6 us -> none  [the longest x1 8.36 us: body(): lax.all_to_all(spread, 'orig', split_axis=4, concat_axis=0, tiled=True)]
    ppermute x0 -> x7, starting transfers between devices: none -> 9.23 us  [the longest x3 5.62 us: body(): lax.ppermute(tile, 'dest', meet(dest_size, s))]
    dot_general x36 -> x0, matrix products: 6.91 us -> none  [the longest x16 3.58 us: one_block(): jnp.einsum('qd,kd->qk', block_queries, head_keys, preferred_element_type=...]
    ppermute x0 -> x7, waiting for transfers between devices: none -> 6.81 us  [the longest x3 3.38 us: body(): lax.ppermute(turned, 'orig', meet(orig_size, s))]
    pallas_call x0 -> x3, Pallas kernels: none -> 6.56 us  [the longest x2 5.52 us: attend(): pl.pallas_call(functools.partial(attend_kernel, counts, items, pack, grou...]
    all_to_all x1 -> x0, starting transfers between devices: 6.45 us -> none  [body(): lax.all_to_all(pieces, 'dest', split_axis=0, concat_axis=2, tiled=True)[0]]
    all_to_all x1 -> x0, waiting for transfers between devices: 4.34 us -> none  [body(): lax.all_to_all(pieces, 'dest', split_axis=0, concat_axis=2, tiled=True)[0]]
    unnamed x26 -> x4, local copies, waits for them, and re-layouts: 3.34 us -> 0.65 us
  transfers between devices with their start and end apart: 1 -> 7, of which waited for: 1 -> 5; matrix products, arithmetic and copies ran while one was open for 0% -> 0% of each run, Pallas kernels for 0% -> 4%
where the time goes in v1:
time: 24.2 us; the launch traced here: 24 us
  starting transfers between devices  9.23 us (38%)
  waiting for transfers between devices  6.81 us (28%)
  Pallas kernels  6.56 us (27%)
  between operations  0.7 us (3%)
  local copies, waits for them, and re-layouts  0.65 us (3%)
    ppermute x3, starting transfers between devices, body(): lax.ppermute(tile, 'dest', meet(dest_size, s))  5.62 us
    pallas_call x2, Pallas kernels, attend(): pl.pallas_call(functools.partial(attend_kernel, counts, items, pack, grou...  5.52 us
    ppermute x3, starting transfers between devices, body(): lax.ppermute(turned, 'orig', meet(orig_size, s))  3.54 us
    ppermute x3, waiting for transfers between devices, body(): lax.ppermute(turned, 'orig', meet(orig_size, s))  3.38 us
    ppermute x3, waiting for transfers between devices, body(): lax.ppermute(tile, 'dest', meet(dest_size, s))  2.1 us
    ppermute x1, waiting for transfers between devices, body(): other = lax.ppermute(held, 'orig', meet(orig_size, 1))  1.33 us
    pallas_call x1, Pallas kernels, prepare(): pl.pallas_call(functools.partial(prepare_kernel, axes, steps, parts, pack...  1.04 us
    unnamed x4, local copies, waits for them, and re-layouts  0.65 us
  transfers between devices with their start and end apart: 7, of which 5 were waited for; matrix products, arithmetic and copies ran while one was open for 0% of the time, Pallas kernels for 4%

profile of v1, /device:TPU:0, one launch (start us, length us, event | category | flops | bytes accessed | tf_op | source)
XLA Modules:
  0.0 24.0 jit_solution(12024718480988268982)
XLA Ops:
  0.0 5.0 %collective-permute-start.2 = (bf16[128,128]{1,0:T(8,128)(2,1)}, bf16[128,128]{1,0:T(8,128)(2,1)S(1)}, u32[]{:S(2)}, u32[]{:S(2)}) collective-permute-start(bf16[128,128]{1,0:T(8,128)(2,1)} %bitcast.3), channel_id=1, source_target_pairs={{0,3},{1,2},{2,1},{3,0},{4,7},{5,6},{6,5},{7,4},{8,11},{9,10},{10,... | collective-permute-start | bytes 98312 | tf_op jit(solution)/shard_map/ppermute | solution.py:243
  5.0 0.0 collective-permute-start.1
  5.1 0.6 %collective-permute-start = (bf16[128,128]{1,0:T(8,128)(2,1)}, bf16[128,128]{1,0:T(8,128)(2,1)S(1)}, u32[]{:S(2)}, u32[]{:S(2)}) collective-permute-start(bf16[128,128]{1,0:T(8,128)(2,1)} %bitcast.5), channel_id=1, source_target_pairs={{0,1},{1,0},{2,3},{3,2},{4,5},{5,4},{6,7},{7,6},{8,9},{9,8},{10,11... | collective-permute-start | bytes 98312 | tf_op jit(solution)/shard_map/ppermute | solution.py:243
  6.3 0.0 copy-start.1
  6.3 0.6 %copy-done.1 = s32[64]{0:T(128)S(1)} copy-done((s32[64]{0:T(128)S(1)}, s32[64]{0:T(128)}, u32[]{:S(2)}) %copy-start.1) | copy-done | bytes 280
  6.9 0.0 copy-start
  6.9 1.0 %shard_map.145 = (bf16[128,640]{1,0:T(8,128)(2,1)S(1)}, f32[1,128]{1,0:T(1,128)S(1)}, f32[1,128]{1,0:T(1,128)S(1)}, bf16[128,640]{1,0:T(8,128)(2,1)S(1)}, f32[1,128]{1,0:T(1,128)S(1)}, /*index=5*/f32[1,128]{1,0:T(1,128)S(1)}) custom-call(s32[1,64]{1,0:T(1,128)S(1)} %bitcast.7, s32[1]{0:T(128)S(6)} %copy.16.count_ref, bf16[1,128,128]{2,1,0:T(8,128)(2,1)} %refs_0_.1, ...), custom_call_target="tpu_custom_call" | custom-call | flops 1048576 | bytes 1048576 | tf_op jit(solution)/shard_map/pallas_call | solution.py:81
  8.0 0.0 collective-permute-done.2.refs_3_
  8.0 2.1 %collective-permute-done.1.refs_2_ = bf16[128,128]{1,0:T(8,128)(2,1)S(1)} collective-permute-done((bf16[128,128]{1,0:T(8,128)(2,1)}, bf16[128,128]{1,0:T(8,128)(2,1)S(1)}, u32[]{:S(2)}, u32[]{:S(2)}) %collective-permute-start.1) | collective-permute-done | bytes 32800 | tf_op jit(solution)/shard_map/ppermute | solution.py:243
  10.1 0.0 collective-permute-done.refs_1_
  10.1 0.0 copy-done
  10.1 1.7 %shard_map.146 = bf16[128,128]{1,0:T(8,128)(2,1)S(1)} custom-call(bf16[128,128]{1,0:T(8,128)(2,1)S(1)} %bitcast.6, bf16[128,128]{1,0:T(8,128)(2,1)S(1)} %collective-permute-done.refs_1_, bf16[128,128]{1,0:T(8,128)(2,1)S(1)} %collective-permute-done.1.refs_2_, bf16[128,128]{1,0:T(8,128)(2,1)S(1)} %collective-permute-done.2.refs_3_, ...), custom_call_target="tpu_custom_call" | custom-call | tf_op jit(solution)/shard_map/pallas_call | solution.py:190
  11.8 2.5 %collective-permute-start.5 = (bf16[128,128]{1,0:T(8,128)(2,1)S(1)}, bf16[128,128]{1,0:T(8,128)(2,1)S(1)}, u32[]{:S(2)}, u32[]{:S(2)}) collective-permute-start(bf16[128,128]{1,0:T(8,128)(2,1)S(1)} %shard_map.146), channel_id=1, source_target_pairs={{0,24},{4,28},{8,16},{12,20},{16,8},{20,12},{24,0},{28,4},{1,25},{... | collective-permute-start | bytes 98312 | tf_op jit(solution)/shard_map/ppermute | solution.py:247
  14.3 0.5 %collective-permute-start.4 = (bf16[128,128]{1,0:T(8,128)(2,1)S(1)}, bf16[128,128]{1,0:T(8,128)(2,1)S(1)}, u32[]{:S(2)}, u32[]{:S(2)}) collective-permute-start(bf16[128,128]{1,0:T(8,128)(2,1)S(1)} %shard_map.146), channel_id=1, source_target_pairs={{0,16},{4,20},{8,24},{12,28},{16,0},{20,4},{24,8},{28,12},{1,17},{... | collective-permute-start | bytes 98312 | tf_op jit(solution)/shard_map/ppermute | solution.py:247
  14.8 0.5 %collective-permute-start.3 = (bf16[128,128]{1,0:T(8,128)(2,1)S(1)}, bf16[128,128]{1,0:T(8,128)(2,1)S(1)}, u32[]{:S(2)}, u32[]{:S(2)}) collective-permute-start(bf16[128,128]{1,0:T(8,128)(2,1)S(1)} %shard_map.146), channel_id=1, source_target_pairs={{0,8},{4,12},{8,0},{12,4},{16,24},{20,28},{24,16},{28,20},{1,9},{5... | collective-permute-start | bytes 98312 | tf_op jit(solution)/shard_map/ppermute | solution.py:247
  15.3 1.6 %collective-permute-done.5 = bf16[128,128]{1,0:T(8,128)(2,1)S(1)} collective-permute-done((bf16[128,128]{1,0:T(8,128)(2,1)S(1)}, bf16[128,128]{1,0:T(8,128)(2,1)S(1)}, u32[]{:S(2)}, u32[]{:S(2)}) %collective-permute-start.5) | collective-permute-done | bytes 32800 | tf_op jit(solution)/shard_map/ppermute | solution.py:247
  16.9 1.3 %collective-permute-done.4 = bf16[128,128]{1,0:T(8,128)(2,1)S(1)} collective-permute-done((bf16[128,128]{1,0:T(8,128)(2,1)S(1)}, bf16[128,128]{1,0:T(8,128)(2,1)S(1)}, u32[]{:S(2)}, u32[]{:S(2)}) %collective-permute-start.4) | collective-permute-done | bytes 32800 | tf_op jit(solution)/shard_map/ppermute | solution.py:247
  18.2 0.5 %collective-permute-done.3 = bf16[128,128]{1,0:T(8,128)(2,1)S(1)} collective-permute-done((bf16[128,128]{1,0:T(8,128)(2,1)S(1)}, bf16[128,128]{1,0:T(8,128)(2,1)S(1)}, u32[]{:S(2)}, u32[]{:S(2)}) %collective-permute-start.3) | collective-permute-done | bytes 32800 | tf_op jit(solution)/shard_map/ppermute | solution.py:247
  18.7 0.1 collective-permute-start.6
  18.8 1.3 %collective-permute-done.6.refs_1_ = bf16[512,128]{1,0:T(8,128)(2,1)S(1)} collective-permute-done((bf16[512,128]{1,0:T(8,128)(2,1)S(1)}, bf16[512,128]{1,0:T(8,128)(2,1)S(1)}, u32[]{:S(2)}, u32[]{:S(2)}) %collective-permute-start.6) | collective-permute-done | bytes 131104 | tf_op jit(solution)/shard_map/ppermute | solution.py:249
  20.1 3.8 %shard_map.147 = bf16[128,128]{1,0:T(8,128)(2,1)} custom-call(bf16[512,128]{1,0:T(8,128)(2,1)S(1)} %pad_maximum_fusion.refs_0_, bf16[512,128]{1,0:T(8,128)(2,1)S(1)} %collective-permute-done.6.refs_1_, bf16[128,640]{1,0:T(8,128)(2,1)S(1)} %get-tuple-element.14.refs_2_, f32[1,128]{1,0:T(1,128)S(1)} %get-tuple-element.15.refs_3_, ...), custom_call_target="tpu_custom_call" | custom-call | tf_op jit(solution)/shard_map/pallas_call | solution.py:190
  (1 shorter events, 0.0 us)
Async XLA Ops:
  0.0 8.0 %collective-permute-start.2 = (bf16[128,128]{1,0:T(8,128)(2,1)}, bf16[128,128]{1,0:T(8,128)(2,1)S(1)}, u32[]{:S(2)}, u32[]{:S(2)}) collective-permute-start(bf16[128,128]{1,0:T(8,128)(2,1)} %bitcast.3), channel_id=1, source_target_pairs={{0,3},{1,2},{2,1},{3,0},{4,7},{5,6},{6,5},{7,4},{8,11},{9,10},{10,... | collective-permute-start | bytes 98312 | tf_op jit(solution)/shard_map/ppermute | solution.py:243
  5.0 5.0 %collective-permute-start.1 = (bf16[128,128]{1,0:T(8,128)(2,1)}, bf16[128,128]{1,0:T(8,128)(2,1)S(1)}, u32[]{:S(2)}, u32[]{:S(2)}) collective-permute-start(bf16[128,128]{1,0:T(8,128)(2,1)} %bitcast.4), channel_id=1, source_target_pairs={{0,2},{1,3},{2,0},{3,1},{4,6},{5,7},{6,4},{7,5},{8,10},{9,11},{10,... | collective-permute-start | bytes 98312 | tf_op jit(solution)/shard_map/ppermute | solution.py:243
  5.1 5.0 %collective-permute-start = (bf16[128,128]{1,0:T(8,128)(2,1)}, bf16[128,128]{1,0:T(8,128)(2,1)S(1)}, u32[]{:S(2)}, u32[]{:S(2)}) collective-permute-start(bf16[128,128]{1,0:T(8,128)(2,1)} %bitcast.5), channel_id=1, source_target_pairs={{0,1},{1,0},{2,3},{3,2},{4,5},{5,4},{6,7},{7,6},{8,9},{9,8},{10,11... | collective-permute-start | bytes 98312 | tf_op jit(solution)/shard_map/ppermute | solution.py:243
  6.3 0.7 %copy-start.1 = (s32[64]{0:T(128)S(1)}, s32[64]{0:T(128)}, u32[]{:S(2)}) copy-start(s32[64]{0:T(128)} %param.16) | copy-start | bytes 772
  6.9 3.2 %copy-start = (bf16[8,16,128]{2,1,0:T(8,128)(2,1)S(1)}, bf16[8,16,128]{2,1,0:T(8,128)(2,1)}, u32[]{:S(2)}) copy-start(bf16[8,16,128]{2,1,0:T(8,128)(2,1)} %param.15) | copy-start | bytes 98308
  11.8 5.1 %collective-permute-start.5 = (bf16[128,128]{1,0:T(8,128)(2,1)S(1)}, bf16[128,128]{1,0:T(8,128)(2,1)S(1)}, u32[]{:S(2)}, u32[]{:S(2)}) collective-permute-start(bf16[128,128]{1,0:T(8,128)(2,1)S(1)} %shard_map.146), channel_id=1, source_target_pairs={{0,24},{4,28},{8,16},{12,20},{16,8},{20,12},{24,0},{28,4},{1,25},{... | collective-permute-start | bytes 98312 | tf_op jit(solution)/shard_map/ppermute | solution.py:247
  14.3 3.9 %collective-permute-start.4 = (bf16[128,128]{1,0:T(8,128)(2,1)S(1)}, bf16[128,128]{1,0:T(8,128)(2,1)S(1)}, u32[]{:S(2)}, u32[]{:S(2)}) collective-permute-start(bf16[128,128]{1,0:T(8,128)(2,1)S(1)} %shard_map.146), channel_id=1, source_target_pairs={{0,16},{4,20},{8,24},{12,28},{16,0},{20,4},{24,8},{28,12},{1,17},{... | collective-permute-start | bytes 98312 | tf_op jit(solution)/shard_map/ppermute | solution.py:247
  14.8 3.9 %collective-permute-start.3 = (bf16[128,128]{1,0:T(8,128)(2,1)S(1)}, bf16[128,128]{1,0:T(8,128)(2,1)S(1)}, u32[]{:S(2)}, u32[]{:S(2)}) collective-permute-start(bf16[128,128]{1,0:T(8,128)(2,1)S(1)} %shard_map.146), channel_id=1, source_target_pairs={{0,8},{4,12},{8,0},{12,4},{16,24},{20,28},{24,16},{28,20},{1,9},{5... | collective-permute-start | bytes 98312 | tf_op jit(solution)/shard_map/ppermute | solution.py:247
  18.7 1.4 %collective-permute-start.6 = (bf16[512,128]{1,0:T(8,128)(2,1)S(1)}, bf16[512,128]{1,0:T(8,128)(2,1)S(1)}, u32[]{:S(2)}, u32[]{:S(2)}) collective-permute-start(bf16[512,128]{1,0:T(8,128)(2,1)S(1)} %pad_maximum_fusion.refs_0_), channel_id=1, source_target_pairs={{0,4},{4,0},{8,12},{12,8},{16,20},{20,16},{24,28},{28,24},{1,5},{5... | collective-permute-start | bytes 393224 | tf_op jit(solution)/shard_map/ppermute | solution.py:249

commit v2 on v1

--- a/solution.py
+++ b/solution.py
@@ -54,10 +54,9 @@
         shape = (regions, pack * regions)
         lane = lax.broadcasted_iota(jnp.int32, (1, shape[1]), 1)
         block = lane // (part * pack)
-        odd = me % 2 == 1
         step = jnp.zeros_like(lane)
-        for b, (for_even, for_odd) in enumerate(steps[a]):
-            step = jnp.where(block == b, jnp.where(odd, for_odd, for_even), step)
+        for b, value in enumerate(steps[a]):
+            step = jnp.where(block == b, value, step)
         region = (step ^ me) * part + lane % part
         hit = lax.broadcasted_iota(jnp.int32, shape, 0) == region
         found = jnp.dot(
@@ -94,15 +93,15 @@
     )
 
 
-def attend_kernel(counts, items, pack, group, *refs):
-    block_refs = refs[: len(counts)]
-    weight_ref, gate_bias_ref, bias_ref, out_ref, turned_ref = refs[len(counts) :]
+def attend_kernel(items, pack, group, *refs):
+    *block_refs, weight_ref, gate_bias_ref, bias_ref, out_ref, turned_ref = refs
     channels = weight_ref.shape[0]
     head_size = channels // H
     rows = out_ref.shape[0]
     part = rows // items
     step_rows, pack_rows = group * part, pack * part
-    blocks = sum(counts)
+    places = [(ref, b) for ref in block_refs for b in range(ref.shape[0] // rows)]
+    blocks = len(places)
     scale = math.log2(math.e) / math.sqrt(head_size)
     head_of = lax.broadcasted_iota(jnp.int32, (1, channels), 1) // head_size
     shape = (H * pack_rows, blocks * pack_rows)
@@ -112,12 +111,7 @@
 
     def step(start):
         x = jnp.concatenate(
-            [
-                ref[pl.ds(b * rows + start, step_rows), :]
-                for ref, count in zip(block_refs, counts)
-                for b in range(count)
-            ],
-            0,
+            [ref[pl.ds(b * rows + start, step_rows), :] for ref, b in places], 0
         ).astype(jnp.float32)
         centered = x - jnp.mean(x, axis=1, keepdims=True)
         variance = jnp.mean(centered * centered, axis=1, keepdims=True)
@@ -130,28 +124,43 @@
         products = jnp.dot(
             normed, weight_ref[:, 2 * channels : 4 * channels], preferred_element_type=jnp.float32
         ).astype(jnp.bfloat16)
+        packs = range(group // pack)
+        held = [
+            jnp.concatenate(
+                [products[b * step_rows + i * pack_rows :][:pack_rows] for b in range(blocks)], 0
+            )
+            for i in packs
+        ]
+        stacked = [
+            jnp.concatenate(
+                [
+                    jnp.where(head_of == h, queries[i * pack_rows : (i + 1) * pack_rows], 0.0)
+                    for h in range(H)
+                ],
+                0,
+            ).astype(jnp.bfloat16)
+            for i in packs
+        ]
+        scores = [
+            lax.dot_general(
+                stacked[i],
+                held[i][:, :channels],
+                (((1,), (1,)), ((), ())),
+                preferred_element_type=jnp.float32,
+            )
+            * scale
+            + bias
+            for i in packs
+        ]
+        scores = jnp.concatenate(scores, 0)
+        expanded = jnp.exp2(scores - jnp.max(scores, axis=1, keepdims=True))
+        weights = (expanded * (1.0 / jnp.sum(expanded, axis=1, keepdims=True))).astype(jnp.bfloat16)
         attended = []
-        for i in range(group // pack):
-            at = [b * step_rows + i * pack_rows for b in range(blocks)]
-            both = jnp.concatenate([products[a : a + pack_rows] for a in at], 0)
-            q = queries[i * pack_rows : (i + 1) * pack_rows]
-            stacked = jnp.concatenate(
-                [jnp.where(head_of == h, q, 0.0) for h in range(H)], 0
-            ).astype(jnp.bfloat16)
-            scores = (
-                lax.dot_general(
-                    stacked,
-                    both[:, :channels],
-                    (((1,), (1,)), ((), ())),
-                    preferred_element_type=jnp.float32,
-                )
-                * scale
-                + bias
-            )
-            expanded = jnp.exp2(scores - jnp.max(scores, axis=1, keepdims=True))
-            weights = expanded * (1.0 / jnp.sum(expanded, axis=1, keepdims=True))
+        for i in packs:
             heads = jnp.dot(
-                weights.astype(jnp.bfloat16), both[:, channels:], preferred_element_type=jnp.float32
+                weights[i * H * pack_rows : (i + 1) * H * pack_rows],
+                held[i][:, channels:],
+                preferred_element_type=jnp.float32,
             )
             picked = heads[:pack_rows]
             for h in range(1, H):
@@ -184,11 +193,11 @@
     out_ref[...] = turned_ref[...].astype(out_ref.dtype)
 
 
-def attend(blocks, counts, items, pack, group, prepared):
-    rows, channels = blocks[0].shape[0] // counts[0], blocks[0].shape[1]
+def attend(blocks, rows, items, packing, prepared):
+    channels = blocks[0].shape[1]
     held = sum(b.size * b.dtype.itemsize for b in blocks)
     return pl.pallas_call(
-        functools.partial(attend_kernel, counts, items, pack, group),
+        functools.partial(attend_kernel, items, *packing),
         out_shape=jax.ShapeDtypeStruct((rows, channels), jnp.bfloat16),
         in_specs=[vmem] * (len(blocks) + len(prepared)),
         out_specs=vmem,
@@ -197,8 +206,14 @@
     )(*blocks, *prepared)
 
 
-def meet(size, step):
-    return [(i, i ^ step) for i in range(size)]
+def fetch(values, orig_step, dest_step=0):
+    orig_size, dest_size = lax.axis_size("orig"), lax.axis_size("dest")
+    pairs = [
+        (o * dest_size + d, (o ^ orig_step) * dest_size + (d ^ dest_step))
+        for o in range(orig_size)
+        for d in range(dest_size)
+    ]
+    return lax.ppermute(values, ("orig", "dest"), pairs)
 
 
 def body(
@@ -223,13 +238,14 @@
     orig_size = lax.axis_size("orig")
     regions = region_mask.shape[0]
     row_steps = list(range(dest_size))
-    near = list(range(0, orig_size, 2))
-    col_steps = near + [s ^ 1 for s in near]
+    chip_steps = list(range(2, orig_size, 2))
+    col_steps = [0, 1] + chip_steps + [s ^ 1 for s in chip_steps]
     row_packing = packing(tile_rows, regions)
     col_packing = packing(tile_cols, regions)
+    rows = tile_rows * tile_cols
     prepared = prepare(
         ("dest", "orig"),
-        ([(s, s) for s in row_steps], [(s, s) for s in col_steps]),
+        (row_steps, col_steps),
         (tile_cols, tile_rows),
         (row_packing[0], col_packing[0]),
         region_mask,
@@ -239,15 +255,13 @@
         (row_gate_bias, col_gate_bias),
     )
 
-    tile = pair_field.reshape(tile_rows * tile_cols, channels)
-    blocks = [tile] + [lax.ppermute(tile, "dest", meet(dest_size, s)) for s in row_steps[1:]]
-    turned = attend(blocks, [1] * dest_size, tile_rows, *row_packing, prepared[:3])
-
-    held = jnp.concatenate(
-        [turned] + [lax.ppermute(turned, "orig", meet(orig_size, s)) for s in near[1:]], 0
-    )
-    other = lax.ppermute(held, "orig", meet(orig_size, 1))
-    result = attend([held, other], [len(near)] * 2, tile_cols, *col_packing, prepared[3:])
+    tile = pair_field.reshape(rows, channels)
+    blocks = [fetch(tile, 1, s) for s in row_steps]
+    turned = attend(blocks, rows, tile_rows, row_packing, prepared[:3])
+    own = fetch(turned, 1)
+    near = jnp.concatenate([fetch(turned, s ^ 1) for s in chip_steps], 0)
+    blocks = [own, turned, near, fetch(near, 1)]
+    result = attend(blocks, rows, tile_cols, col_packing, prepared[3:])
     return result.reshape(tile_rows, tile_cols, channels)
 
 

time: 24.2 us -> 21 us (0.87)
  Pallas kernels: 6.56 us -> 4.44 us
  waiting for transfers between devices: 6.81 us -> 5.8 us
    pallas_call x2, Pallas kernels: 5.52 us -> 3.41 us  [attend(): pl.pallas_call(functools.partial(attend_kernel, items, *packing), out_sha...]
    ppermute x7 -> x9, waiting for transfers between devices: 6.81 us -> 5.8 us  [fetch(): return lax.ppermute(values, ('orig', 'dest'), pairs)]
    ppermute x7 -> x9, starting transfers between devices: 9.23 us -> 9.17 us  [fetch(): return lax.ppermute(values, ('orig', 'dest'), pairs)]
  transfers between devices with their start and end apart: 7 -> 9, of which waited for: 5 -> 4; matrix products, arithmetic and copies ran while one was open for 0% -> 0% of each run, Pallas kernels for 4% -> 5%
where the time goes in v2:
time: 21 us; the launch traced here: 20.8 us
  starting transfers between devices  9.17 us (44%)
  waiting for transfers between devices  5.8 us (28%)
  Pallas kernels  4.44 us (21%)
  between operations  0.69 us (3%)
  local copies, waits for them, and re-layouts  0.67 us (3%)
    ppermute x9, starting transfers between devices, fetch(): return lax.ppermute(values, ('orig', 'dest'), pairs)  9.17 us
    ppermute x9, waiting for transfers between devices, fetch(): return lax.ppermute(values, ('orig', 'dest'), pairs)  5.8 us
    pallas_call x2, Pallas kernels, attend(): pl.pallas_call(functools.partial(attend_kernel, items, *packing), out_sha...  3.41 us
    pallas_call x1, Pallas kernels, prepare(): pl.pallas_call(functools.partial(prepare_kernel, axes, steps, parts, pack...  1.03 us
    unnamed x4, local copies, waits for them, and re-layouts  0.66 us
  transfers between devices with their start and end apart: 9, of which 4 were waited for; matrix products, arithmetic and copies ran while one was open for 0% of the time, Pallas kernels for 5%

profile of v2, /device:TPU:0, one launch (start us, length us, event | category | flops | bytes accessed | tf_op | source)
XLA Modules:
  0.0 20.8 jit_solution(10983125007993372533)
XLA Ops:
  0.0 4.5 %collective-permute-start.3 = (bf16[128,128]{1,0:T(8,128)(2,1)}, bf16[128,128]{1,0:T(8,128)(2,1)S(1)}, u32[]{:S(2)}, u32[]{:S(2)}) collective-permute-start(bf16[128,128]{1,0:T(8,128)(2,1)} %bitcast.4), channel_id=1, source_target_pairs={{0,7},{1,6},{2,5},{3,4},{4,3},{5,2},{6,1},{7,0},{8,15},{9,14},{10,... | collective-permute-start | bytes 98312 | tf_op jit(solution)/shard_map/ppermute | solution.py:216
  4.5 0.0 collective-permute-start.2
  4.5 0.8 %collective-permute-start.1 = (bf16[128,128]{1,0:T(8,128)(2,1)}, bf16[128,128]{1,0:T(8,128)(2,1)S(1)}, u32[]{:S(2)}, u32[]{:S(2)}) collective-permute-start(bf16[128,128]{1,0:T(8,128)(2,1)} %bitcast.6), channel_id=1, source_target_pairs={{0,5},{1,4},{2,7},{3,6},{4,1},{5,0},{6,3},{7,2},{8,13},{9,12},{10,... | collective-permute-start | bytes 98312 | tf_op jit(solution)/shard_map/ppermute | solution.py:216
  5.3 0.0 collective-permute-start
  6.0 0.0 copy-start
  6.0 0.6 %copy-done = s32[64]{0:T(128)S(1)} copy-done((s32[64]{0:T(128)S(1)}, s32[64]{0:T(128)}, u32[]{:S(2)}) %copy-start) | copy-done | bytes 280
  6.6 1.0 %shard_map.145 = (bf16[128,640]{1,0:T(8,128)(2,1)S(1)}, f32[1,128]{1,0:T(1,128)S(1)}, f32[1,128]{1,0:T(1,128)S(1)}, bf16[128,640]{1,0:T(8,128)(2,1)S(1)}, f32[1,128]{1,0:T(1,128)S(1)}, /*index=5*/f32[1,128]{1,0:T(1,128)S(1)}) custom-call(s32[1,64]{1,0:T(1,128)S(1)} %bitcast.3, s32[1]{0:T(128)S(6)} %copy.18.count_ref, bf16[1,128,128]{2,1,0:T(8,128)(2,1)} %refs_0_.1, ...), custom_call_target="tpu_custom_call" | custom-call | flops 1048576 | bytes 1048576 | tf_op jit(solution)/shard_map/pallas_call | solution.py:80
  7.7 0.0 collective-permute-done.3.refs_3_
  7.7 1.5 %collective-permute-done.2.refs_2_ = bf16[128,128]{1,0:T(8,128)(2,1)S(1)} collective-permute-done((bf16[128,128]{1,0:T(8,128)(2,1)}, bf16[128,128]{1,0:T(8,128)(2,1)S(1)}, u32[]{:S(2)}, u32[]{:S(2)}) %collective-permute-start.2) | collective-permute-done | bytes 32800 | tf_op jit(solution)/shard_map/ppermute | solution.py:216
  9.2 0.0 collective-permute-done.1.refs_1_
  9.2 0.0 collective-permute-done.refs_0_
  9.2 1.2 %shard_map.146.refs_1_ = bf16[128,128]{1,0:T(8,128)(2,1)S(1)} custom-call(bf16[128,128]{1,0:T(8,128)(2,1)S(1)} %collective-permute-done.refs_0_, bf16[128,128]{1,0:T(8,128)(2,1)S(1)} %collective-permute-done.1.refs_1_, bf16[128,128]{1,0:T(8,128)(2,1)S(1)} %collective-permute-done.2.refs_2_, bf16[128,128]{1,0:T(8,128)(2,1)S(1)} %collective-permute-done.3.refs_3_, ...), custom_call_target="tpu_custom_call" | custom-call | tf_op jit(solution)/shard_map/pallas_call | solution.py:199
  10.4 1.5 %collective-permute-start.5 = (bf16[128,128]{1,0:T(8,128)(2,1)S(1)}, bf16[128,128]{1,0:T(8,128)(2,1)S(1)}, u32[]{:S(2)}, u32[]{:S(2)}) collective-permute-start(bf16[128,128]{1,0:T(8,128)(2,1)S(1)} %shard_map.146.refs_1_), channel_id=1, source_target_pairs={{0,12},{1,13},{2,14},{3,15},{4,8},{5,9},{6,10},{7,11},{8,4},{9,5},... | collective-permute-start | bytes 98312 | tf_op jit(solution)/shard_map/ppermute | solution.py:216
  12.0 1.2 %collective-permute-start.7 = (bf16[128,128]{1,0:T(8,128)(2,1)S(1)}, bf16[128,128]{1,0:T(8,128)(2,1)S(1)}, u32[]{:S(2)}, u32[]{:S(2)}) collective-permute-start(bf16[128,128]{1,0:T(8,128)(2,1)S(1)} %shard_map.146.refs_1_), channel_id=1, source_target_pairs={{0,28},{1,29},{2,30},{3,31},{4,24},{5,25},{6,26},{7,27},{8,20},{9,... | collective-permute-start | bytes 98312 | tf_op jit(solution)/shard_map/ppermute | solution.py:216
  13.2 0.5 %collective-permute-start.6 = (bf16[128,128]{1,0:T(8,128)(2,1)S(1)}, bf16[128,128]{1,0:T(8,128)(2,1)S(1)}, u32[]{:S(2)}, u32[]{:S(2)}) collective-permute-start(bf16[128,128]{1,0:T(8,128)(2,1)S(1)} %shard_map.146.refs_1_), channel_id=1, source_target_pairs={{0,20},{1,21},{2,22},{3,23},{4,16},{5,17},{6,18},{7,19},{8,28},{9,... | collective-permute-start | bytes 98312 | tf_op jit(solution)/shard_map/ppermute | solution.py:216
  13.7 0.2 collective-permute-done.5
  13.9 3.2 %collective-permute-done.6 = bf16[128,128]{1,0:T(8,128)(2,1)S(1)} collective-permute-done((bf16[128,128]{1,0:T(8,128)(2,1)S(1)}, bf16[128,128]{1,0:T(8,128)(2,1)S(1)}, u32[]{:S(2)}, u32[]{:S(2)}) %collective-permute-start.6) | collective-permute-done | bytes 32800 | tf_op jit(solution)/shard_map/ppermute | solution.py:216
  17.1 0.0 collective-permute-done.7
  17.1 0.2 collective-permute-start.8
  17.3 0.4 %collective-permute-start.4 = (bf16[128,128]{1,0:T(8,128)(2,1)S(1)}, bf16[128,128]{1,0:T(8,128)(2,1)S(1)}, u32[]{:S(2)}, u32[]{:S(2)}) collective-permute-start(bf16[128,128]{1,0:T(8,128)(2,1)S(1)} %shard_map.146.refs_1_), channel_id=1, source_target_pairs={{0,4},{1,5},{2,6},{3,7},{4,0},{5,1},{6,2},{7,3},{8,12},{9,13},{10,... | collective-permute-start | bytes 98312 | tf_op jit(solution)/shard_map/ppermute | solution.py:216
  17.7 0.9 %collective-permute-done.4.refs_0_ = bf16[128,128]{1,0:T(8,128)(2,1)S(1)} collective-permute-done((bf16[128,128]{1,0:T(8,128)(2,1)S(1)}, bf16[128,128]{1,0:T(8,128)(2,1)S(1)}, u32[]{:S(2)}, u32[]{:S(2)}) %collective-permute-start.4) | collective-permute-done | bytes 32800 | tf_op jit(solution)/shard_map/ppermute | solution.py:216
  18.5 0.0 collective-permute-done.8.refs_3_
  18.6 2.2 %shard_map.147 = bf16[128,128]{1,0:T(8,128)(2,1)} custom-call(bf16[128,128]{1,0:T(8,128)(2,1)S(1)} %collective-permute-done.4.refs_0_, bf16[128,128]{1,0:T(8,128)(2,1)S(1)} %shard_map.146.refs_1_, bf16[384,128]{1,0:T(8,128)(2,1)S(1)} %constant_dynamic-update-slice_fusion.refs_2_, bf16[384,128]{1,0:T(8,128)(2,1)S(1)} %collective-permute-done.8.refs_3_, ...), custom_call_target="tpu_custom_call" | custom-call | tf_op jit(solution)/shard_map/pallas_call | solution.py:199
  (3 shorter events, 0.0 us)
Async XLA Ops:
  0.0 7.7 %collective-permute-start.3 = (bf16[128,128]{1,0:T(8,128)(2,1)}, bf16[128,128]{1,0:T(8,128)(2,1)S(1)}, u32[]{:S(2)}, u32[]{:S(2)}) collective-permute-start(bf16[128,128]{1,0:T(8,128)(2,1)} %bitcast.4), channel_id=1, source_target_pairs={{0,7},{1,6},{2,5},{3,4},{4,3},{5,2},{6,1},{7,0},{8,15},{9,14},{10,... | collective-permute-start | bytes 98312 | tf_op jit(solution)/shard_map/ppermute | solution.py:216
  4.5 4.7 %collective-permute-start.2 = (bf16[128,128]{1,0:T(8,128)(2,1)}, bf16[128,128]{1,0:T(8,128)(2,1)S(1)}, u32[]{:S(2)}, u32[]{:S(2)}) collective-permute-start(bf16[128,128]{1,0:T(8,128)(2,1)} %bitcast.5), channel_id=1, source_target_pairs={{0,6},{1,7},{2,4},{3,5},{4,2},{5,3},{6,0},{7,1},{8,14},{9,15},{10,... | collective-permute-start | bytes 98312 | tf_op jit(solution)/shard_map/ppermute | solution.py:216
  4.5 4.7 %collective-permute-start.1 = (bf16[128,128]{1,0:T(8,128)(2,1)}, bf16[128,128]{1,0:T(8,128)(2,1)S(1)}, u32[]{:S(2)}, u32[]{:S(2)}) collective-permute-start(bf16[128,128]{1,0:T(8,128)(2,1)} %bitcast.6), channel_id=1, source_target_pairs={{0,5},{1,4},{2,7},{3,6},{4,1},{5,0},{6,3},{7,2},{8,13},{9,12},{10,... | collective-permute-start | bytes 98312 | tf_op jit(solution)/shard_map/ppermute | solution.py:216
  5.3 3.9 %collective-permute-start = (bf16[128,128]{1,0:T(8,128)(2,1)}, bf16[128,128]{1,0:T(8,128)(2,1)S(1)}, u32[]{:S(2)}, u32[]{:S(2)}) collective-permute-start(bf16[128,128]{1,0:T(8,128)(2,1)} %bitcast.7), channel_id=1, source_target_pairs={{0,4},{1,5},{2,6},{3,7},{4,0},{5,1},{6,2},{7,3},{8,12},{9,13},{10,... | collective-permute-start | bytes 98312 | tf_op jit(solution)/shard_map/ppermute | solution.py:216
  6.0 0.7 %copy-start = (s32[64]{0:T(128)S(1)}, s32[64]{0:T(128)}, u32[]{:S(2)}) copy-start(s32[64]{0:T(128)} %param.16) | copy-start | bytes 772
  10.4 3.4 %collective-permute-start.5 = (bf16[128,128]{1,0:T(8,128)(2,1)S(1)}, bf16[128,128]{1,0:T(8,128)(2,1)S(1)}, u32[]{:S(2)}, u32[]{:S(2)}) collective-permute-start(bf16[128,128]{1,0:T(8,128)(2,1)S(1)} %shard_map.146.refs_1_), channel_id=1, source_target_pairs={{0,12},{1,13},{2,14},{3,15},{4,8},{5,9},{6,10},{7,11},{8,4},{9,5},... | collective-permute-start | bytes 98312 | tf_op jit(solution)/shard_map/ppermute | solution.py:216
  12.0 5.1 %collective-permute-start.7 = (bf16[128,128]{1,0:T(8,128)(2,1)S(1)}, bf16[128,128]{1,0:T(8,128)(2,1)S(1)}, u32[]{:S(2)}, u32[]{:S(2)}) collective-permute-start(bf16[128,128]{1,0:T(8,128)(2,1)S(1)} %shard_map.146.refs_1_), channel_id=1, source_target_pairs={{0,28},{1,29},{2,30},{3,31},{4,24},{5,25},{6,26},{7,27},{8,20},{9,... | collective-permute-start | bytes 98312 | tf_op jit(solution)/shard_map/ppermute | solution.py:216
  13.2 3.9 %collective-permute-start.6 = (bf16[128,128]{1,0:T(8,128)(2,1)S(1)}, bf16[128,128]{1,0:T(8,128)(2,1)S(1)}, u32[]{:S(2)}, u32[]{:S(2)}) collective-permute-start(bf16[128,128]{1,0:T(8,128)(2,1)S(1)} %shard_map.146.refs_1_), channel_id=1, source_target_pairs={{0,20},{1,21},{2,22},{3,23},{4,16},{5,17},{6,18},{7,19},{8,28},{9,... | collective-permute-start | bytes 98312 | tf_op jit(solution)/shard_map/ppermute | solution.py:216
  17.1 1.4 %collective-permute-start.8 = (bf16[384,128]{1,0:T(8,128)(2,1)S(1)}, bf16[384,128]{1,0:T(8,128)(2,1)S(1)}, u32[]{:S(2)}, u32[]{:S(2)}) collective-permute-start(bf16[384,128]{1,0:T(8,128)(2,1)S(1)} %constant_dynamic-update-slice_fusion.refs_2_), channel_id=1, source_target_pairs={{0,4},{1,5},{2,6},{3,7},{4,0},{5,1},{6,2},{7,3},{8,12},{9,13},{10,... | collective-permute-start | bytes 294920 | tf_op jit(solution)/shard_map/ppermute | solution.py:216
  17.3 1.3 %collective-permute-start.4 = (bf16[128,128]{1,0:T(8,128)(2,1)S(1)}, bf16[128,128]{1,0:T(8,128)(2,1)S(1)}, u32[]{:S(2)}, u32[]{:S(2)}) collective-permute-start(bf16[128,128]{1,0:T(8,128)(2,1)S(1)} %shard_map.146.refs_1_), channel_id=1, source_target_pairs={{0,4},{1,5},{2,6},{3,7},{4,0},{5,1},{6,2},{7,3},{8,12},{9,13},{10,... | collective-permute-start | bytes 98312 | tf_op jit(solution)/shard_map/ppermute | solution.py:216

commit v3 on v2

--- a/solution.py
+++ b/solution.py
@@ -28,7 +28,12 @@
     return pack, group
 
 
-def prepare_kernel(axes, steps, parts, packs, mask_ref, count_ref, *refs):
+def reverse(index, size):
+    bits = size.bit_length() - 1
+    return sum(((index >> b) & 1) << (bits - 1 - b) for b in range(bits))
+
+
+def prepare_kernel(axes, sources, parts, packs, mask_ref, count_ref, *refs):
     weights, gate_biases, outs, sem = refs[:10], refs[10:12], refs[12:18], refs[18]
     channels = weights[0].shape[1]
     copies = []
@@ -54,10 +59,9 @@
         shape = (regions, pack * regions)
         lane = lax.broadcasted_iota(jnp.int32, (1, shape[1]), 1)
         block = lane // (part * pack)
-        step = jnp.zeros_like(lane)
-        for b, value in enumerate(steps[a]):
-            step = jnp.where(block == b, value, step)
-        region = (step ^ me) * part + lane % part
+        region = lane % part
+        for b, source in enumerate(sources[a]):
+            region += jnp.where(block == b, source(me) * part, 0)
         hit = lax.broadcasted_iota(jnp.int32, shape, 0) == region
         found = jnp.dot(
             valid, jnp.where(hit, 1.0, 0.0).astype(jnp.bfloat16), preferred_element_type=jnp.float32
@@ -67,7 +71,7 @@
         copy.wait()
 
 
-def prepare(axes, steps, parts, packs, region_mask, region_count, weights, gate_biases):
+def prepare(axes, sources, parts, packs, region_mask, region_count, weights, gate_biases):
     regions = region_mask.shape[0]
     channels = weights[0].shape[-1]
     outs = []
@@ -78,7 +82,7 @@
             pltpu.VMEM((1, pack * regions), jnp.float32),
         ]
     return pl.pallas_call(
-        functools.partial(prepare_kernel, axes, steps, parts, packs),
+        functools.partial(prepare_kernel, axes, sources, parts, packs),
         out_shape=tuple(outs),
         in_specs=[vmem, pl.BlockSpec(memory_space=pltpu.SMEM)]
         + [pl.BlockSpec(memory_space=pltpu.HBM)] * 12,
@@ -112,8 +116,11 @@
     def step(start):
         x = jnp.concatenate(
             [ref[pl.ds(b * rows + start, step_rows), :] for ref, b in places], 0
-        ).astype(jnp.float32)
-        centered = x - jnp.mean(x, axis=1, keepdims=True)
+        )
+        averaging = jnp.full((channels, channels), 1.0 / channels, jnp.bfloat16)
+        mean = jnp.dot(x, averaging, preferred_element_type=jnp.float32)
+        x = x.astype(jnp.float32)
+        centered = x - mean
         variance = jnp.mean(centered * centered, axis=1, keepdims=True)
         normed = (centered * lax.rsqrt(variance + epsilon)).astype(jnp.bfloat16)
         own_products = jnp.dot(
@@ -206,13 +213,13 @@
     )(*blocks, *prepared)
 
 
-def fetch(values, orig_step, dest_step=0):
+def send(values, to):
     orig_size, dest_size = lax.axis_size("orig"), lax.axis_size("dest")
-    pairs = [
-        (o * dest_size + d, (o ^ orig_step) * dest_size + (d ^ dest_step))
-        for o in range(orig_size)
-        for d in range(dest_size)
-    ]
+    pairs = []
+    for o in range(orig_size):
+        for d in range(dest_size):
+            far_o, far_d = to(o, d)
+            pairs.append((o * dest_size + d, far_o * dest_size + far_d))
     return lax.ppermute(values, ("orig", "dest"), pairs)
 
 
@@ -237,15 +244,22 @@
     dest_size = lax.axis_size("dest")
     orig_size = lax.axis_size("orig")
     regions = region_mask.shape[0]
-    row_steps = list(range(dest_size))
+    row_steps = sorted(range(dest_size), key=lambda s: (s > 0, -min(s, dest_size - s), -s))
     chip_steps = list(range(2, orig_size, 2))
     col_steps = [0, 1] + chip_steps + [s ^ 1 for s in chip_steps]
+
+    def along_dest(d, step):
+        return reverse((reverse(d, dest_size) + step) % dest_size, dest_size)
+
     row_packing = packing(tile_rows, regions)
     col_packing = packing(tile_cols, regions)
     rows = tile_rows * tile_cols
     prepared = prepare(
         ("dest", "orig"),
-        (row_steps, col_steps),
+        (
+            [lambda d, s=s: along_dest(d, dest_size - s) for s in row_steps],
+            [lambda o, s=s: o ^ s for s in col_steps],
+        ),
         (tile_cols, tile_rows),
         (row_packing[0], col_packing[0]),
         region_mask,
@@ -256,11 +270,12 @@
     )
 
     tile = pair_field.reshape(rows, channels)
-    blocks = [fetch(tile, 1, s) for s in row_steps]
+    blocks = [send(tile, lambda o, d: (o ^ 1, along_dest(d, s))) for s in row_steps]
     turned = attend(blocks, rows, tile_rows, row_packing, prepared[:3])
-    own = fetch(turned, 1)
-    near = jnp.concatenate([fetch(turned, s ^ 1) for s in chip_steps], 0)
-    blocks = [own, turned, near, fetch(near, 1)]
+    own = send(turned, lambda o, d: (o ^ 1, d))
+    near = [send(turned, lambda o, d: (o ^ s ^ 1, d)) for s in chip_steps]
+    other = [send(block, lambda o, d: (o ^ 1, d)) for block in near]
+    blocks = [own, turned] + near + other
     result = attend(blocks, rows, tile_cols, col_packing, prepared[3:])
     return result.reshape(tile_rows, tile_cols, channels)
 

time: 21 us -> 19.6 us (0.933)
  waiting for transfers between devices: 5.8 us -> 3.86 us
  starting transfers between devices: 9.17 us -> 9.99 us
  Pallas kernels: 4.44 us -> 4.16 us
    ppermute x9 -> x11, waiting for transfers between devices: 5.8 us -> 3.86 us  [send(): return lax.ppermute(values, ('orig', 'dest'), pairs)]
    ppermute x9 -> x11, starting transfers between devices: 9.17 us -> 9.99 us  [send(): return lax.ppermute(values, ('orig', 'dest'), pairs)]
    pallas_call x2, Pallas kernels: 3.41 us -> 3.12 us  [attend(): pl.pallas_call(functools.partial(attend_kernel, items, *packing), out_sha...]
    unnamed x4 -> x2, local copies, waits for them, and re-layouts: 0.66 us -> 0.65 us
  transfers between devices with their start and end apart: 9 -> 11, of which waited for: 4 -> 6; matrix products, arithmetic and copies ran while one was open for 0% -> 0% of each run, Pallas kernels for 5% -> 5%
where the time goes in v3:
time: 19.6 us; the launch traced here: 19.3 us
  starting transfers between devices  9.99 us (51%)
  Pallas kernels  4.16 us (21%)
  waiting for transfers between devices  3.86 us (20%)
  between operations  0.69 us (4%)
  local copies, waits for them, and re-layouts  0.65 us (3%)
    ppermute x11, starting transfers between devices, send(): return lax.ppermute(values, ('orig', 'dest'), pairs)  9.99 us
    ppermute x11, waiting for transfers between devices, send(): return lax.ppermute(values, ('orig', 'dest'), pairs)  3.86 us
    pallas_call x2, Pallas kernels, attend(): pl.pallas_call(functools.partial(attend_kernel, items, *packing), out_sha...  3.12 us
    pallas_call x1, Pallas kernels, prepare(): pl.pallas_call(functools.partial(prepare_kernel, axes, sources, parts, pa...  1.04 us
    unnamed x2, local copies, waits for them, and re-layouts  0.65 us
  transfers between devices with their start and end apart: 11, of which 6 were waited for; matrix products, arithmetic and copies ran while one was open for 0% of the time, Pallas kernels for 5%

profile of v3, /device:TPU:0, one launch (start us, length us, event | category | flops | bytes accessed | tf_op | source)
XLA Modules:
  0.0 19.3 jit_solution(10843718988515198915)
XLA Ops:
  0.0 3.5 %collective-permute-start.3 = (bf16[128,128]{1,0:T(8,128)(2,1)}, bf16[128,128]{1,0:T(8,128)(2,1)S(1)}, u32[]{:S(2)}, u32[]{:S(2)}) collective-permute-start(bf16[128,128]{1,0:T(8,128)(2,1)} %bitcast.4), channel_id=1, source_target_pairs={{0,6},{1,7},{2,5},{3,4},{4,2},{5,3},{6,1},{7,0},{8,14},{9,15},{10,... | collective-permute-start | bytes 98312 | tf_op jit(solution)/shard_map/ppermute | solution.py:223
  3.5 1.0 %collective-permute-start.2 = (bf16[128,128]{1,0:T(8,128)(2,1)}, bf16[128,128]{1,0:T(8,128)(2,1)S(1)}, u32[]{:S(2)}, u32[]{:S(2)}) collective-permute-start(bf16[128,128]{1,0:T(8,128)(2,1)} %bitcast.5), channel_id=1, source_target_pairs={{0,7},{1,6},{2,4},{3,5},{4,3},{5,2},{6,0},{7,1},{8,15},{9,14},{10,... | collective-permute-start | bytes 98312 | tf_op jit(solution)/shard_map/ppermute | solution.py:223
  4.5 0.8 %collective-permute-start.1 = (bf16[128,128]{1,0:T(8,128)(2,1)}, bf16[128,128]{1,0:T(8,128)(2,1)S(1)}, u32[]{:S(2)}, u32[]{:S(2)}) collective-permute-start(bf16[128,128]{1,0:T(8,128)(2,1)} %bitcast.6), channel_id=1, source_target_pairs={{0,5},{1,4},{2,7},{3,6},{4,1},{5,0},{6,3},{7,2},{8,13},{9,12},{10,... | collective-permute-start | bytes 98312 | tf_op jit(solution)/shard_map/ppermute | solution.py:223
  5.3 0.0 collective-permute-start
  6.0 0.0 copy-start
  6.0 0.6 %copy-done = s32[64]{0:T(128)S(1)} copy-done((s32[64]{0:T(128)S(1)}, s32[64]{0:T(128)}, u32[]{:S(2)}) %copy-start) | copy-done | bytes 280
  6.6 1.0 %shard_map.145 = (bf16[128,640]{1,0:T(8,128)(2,1)S(1)}, f32[1,128]{1,0:T(1,128)S(1)}, f32[1,128]{1,0:T(1,128)S(1)}, bf16[128,640]{1,0:T(8,128)(2,1)S(1)}, f32[1,128]{1,0:T(1,128)S(1)}, /*index=5*/f32[1,128]{1,0:T(1,128)S(1)}) custom-call(s32[1,64]{1,0:T(1,128)S(1)} %bitcast.3, s32[1]{0:T(128)S(6)} %copy.16.count_ref, bf16[1,128,128]{2,1,0:T(8,128)(2,1)} %refs_0_.1, ...), custom_call_target="tpu_custom_call" | custom-call | flops 1048576 | bytes 1048576 | tf_op jit(solution)/shard_map/pallas_call | solution.py:84
  7.7 0.0 collective-permute-done.3.refs_3_
  7.7 0.2 %collective-permute-done.2.refs_2_ = bf16[128,128]{1,0:T(8,128)(2,1)S(1)} collective-permute-done((bf16[128,128]{1,0:T(8,128)(2,1)}, bf16[128,128]{1,0:T(8,128)(2,1)S(1)}, u32[]{:S(2)}, u32[]{:S(2)}) %collective-permute-start.2) | collective-permute-done | bytes 32800 | tf_op jit(solution)/shard_map/ppermute | solution.py:223
  7.9 0.3 %collective-permute-done.1.refs_1_ = bf16[128,128]{1,0:T(8,128)(2,1)S(1)} collective-permute-done((bf16[128,128]{1,0:T(8,128)(2,1)}, bf16[128,128]{1,0:T(8,128)(2,1)S(1)}, u32[]{:S(2)}, u32[]{:S(2)}) %collective-permute-start.1) | collective-permute-done | bytes 32800 | tf_op jit(solution)/shard_map/ppermute | solution.py:223
  8.3 0.0 collective-permute-done.refs_0_
  8.3 1.1 %shard_map.146.refs_1_ = bf16[128,128]{1,0:T(8,128)(2,1)S(1)} custom-call(bf16[128,128]{1,0:T(8,128)(2,1)S(1)} %collective-permute-done.refs_0_, bf16[128,128]{1,0:T(8,128)(2,1)S(1)} %collective-permute-done.1.refs_1_, bf16[128,128]{1,0:T(8,128)(2,1)S(1)} %collective-permute-done.2.refs_2_, bf16[128,128]{1,0:T(8,128)(2,1)S(1)} %collective-permute-done.3.refs_3_, ...), custom_call_target="tpu_custom_call" | custom-call | tf_op jit(solution)/shard_map/pallas_call | solution.py:206
  9.4 2.9 %collective-permute-start.7 = (bf16[128,128]{1,0:T(8,128)(2,1)S(1)}, bf16[128,128]{1,0:T(8,128)(2,1)S(1)}, u32[]{:S(2)}, u32[]{:S(2)}) collective-permute-start(bf16[128,128]{1,0:T(8,128)(2,1)S(1)} %shard_map.146.refs_1_), channel_id=1, source_target_pairs={{0,28},{1,29},{2,30},{3,31},{4,24},{5,25},{6,26},{7,27},{8,20},{9,... | collective-permute-start | bytes 98312 | tf_op jit(solution)/shard_map/ppermute | solution.py:223
  12.3 0.4 %collective-permute-start.6 = (bf16[128,128]{1,0:T(8,128)(2,1)S(1)}, bf16[128,128]{1,0:T(8,128)(2,1)S(1)}, u32[]{:S(2)}, u32[]{:S(2)}) collective-permute-start(bf16[128,128]{1,0:T(8,128)(2,1)S(1)} %shard_map.146.refs_1_), channel_id=1, source_target_pairs={{0,20},{1,21},{2,22},{3,23},{4,16},{5,17},{6,18},{7,19},{8,28},{9,... | collective-permute-start | bytes 98312 | tf_op jit(solution)/shard_map/ppermute | solution.py:223
  12.7 0.3 %collective-permute-start.5 = (bf16[128,128]{1,0:T(8,128)(2,1)S(1)}, bf16[128,128]{1,0:T(8,128)(2,1)S(1)}, u32[]{:S(2)}, u32[]{:S(2)}) collective-permute-start(bf16[128,128]{1,0:T(8,128)(2,1)S(1)} %shard_map.146.refs_1_), channel_id=1, source_target_pairs={{0,12},{1,13},{2,14},{3,15},{4,8},{5,9},{6,10},{7,11},{8,4},{9,5},... | collective-permute-start | bytes 98312 | tf_op jit(solution)/shard_map/ppermute | solution.py:223
  13.0 0.1 collective-permute-start.4
  13.1 1.0 %collective-permute-done.7.refs_4_ = bf16[128,128]{1,0:T(8,128)(2,1)S(1)} collective-permute-done((bf16[128,128]{1,0:T(8,128)(2,1)S(1)}, bf16[128,128]{1,0:T(8,128)(2,1)S(1)}, u32[]{:S(2)}, u32[]{:S(2)}) %collective-permute-start.7) | collective-permute-done | bytes 32800 | tf_op jit(solution)/shard_map/ppermute | solution.py:223
  14.0 0.4 %collective-permute-start.10 = (bf16[128,128]{1,0:T(8,128)(2,1)S(1)}, bf16[128,128]{1,0:T(8,128)(2,1)S(1)}, u32[]{:S(2)}, u32[]{:S(2)}) collective-permute-start(bf16[128,128]{1,0:T(8,128)(2,1)S(1)} %collective-permute-done.7.refs_4_), channel_id=1, source_target_pairs={{0,4},{1,5},{2,6},{3,7},{4,0},{5,1},{6,2},{7,3},{8,12},{9,13},{10,... | collective-permute-start | bytes 98312 | tf_op jit(solution)/shard_map/ppermute | solution.py:223
  14.4 1.3 %collective-permute-done.6.refs_3_ = bf16[128,128]{1,0:T(8,128)(2,1)S(1)} collective-permute-done((bf16[128,128]{1,0:T(8,128)(2,1)S(1)}, bf16[128,128]{1,0:T(8,128)(2,1)S(1)}, u32[]{:S(2)}, u32[]{:S(2)}) %collective-permute-start.6) | collective-permute-done | bytes 32800 | tf_op jit(solution)/shard_map/ppermute | solution.py:223
  15.7 0.5 %collective-permute-start.9 = (bf16[128,128]{1,0:T(8,128)(2,1)S(1)}, bf16[128,128]{1,0:T(8,128)(2,1)S(1)}, u32[]{:S(2)}, u32[]{:S(2)}) collective-permute-start(bf16[128,128]{1,0:T(8,128)(2,1)S(1)} %collective-permute-done.6.refs_3_), channel_id=1, source_target_pairs={{0,4},{1,5},{2,6},{3,7},{4,0},{5,1},{6,2},{7,3},{8,12},{9,13},{10,... | collective-permute-start | bytes 98312 | tf_op jit(solution)/shard_map/ppermute | solution.py:223
  16.1 0.0 collective-permute-done.5.refs_2_
  16.2 0.1 collective-permute-start.8
  16.3 0.0 collective-permute-done.4.refs_0_
  16.3 0.0 collective-permute-done.10.refs_7_
  16.3 0.7 %collective-permute-done.9.refs_6_ = bf16[128,128]{1,0:T(8,128)(2,1)S(1)} collective-permute-done((bf16[128,128]{1,0:T(8,128)(2,1)S(1)}, bf16[128,128]{1,0:T(8,128)(2,1)S(1)}, u32[]{:S(2)}, u32[]{:S(2)}) %collective-permute-start.9) | collective-permute-done | bytes 32800 | tf_op jit(solution)/shard_map/ppermute | solution.py:223
  17.0 0.4 %collective-permute-done.8.refs_5_ = bf16[128,128]{1,0:T(8,128)(2,1)S(1)} collective-permute-done((bf16[128,128]{1,0:T(8,128)(2,1)S(1)}, bf16[128,128]{1,0:T(8,128)(2,1)S(1)}, u32[]{:S(2)}, u32[]{:S(2)}) %collective-permute-start.8) | collective-permute-done | bytes 32800 | tf_op jit(solution)/shard_map/ppermute | solution.py:223
  17.4 2.0 %shard_map.147 = bf16[128,128]{1,0:T(8,128)(2,1)} custom-call(bf16[128,128]{1,0:T(8,128)(2,1)S(1)} %collective-permute-done.4.refs_0_, bf16[128,128]{1,0:T(8,128)(2,1)S(1)} %shard_map.146.refs_1_, bf16[128,128]{1,0:T(8,128)(2,1)S(1)} %collective-permute-done.5.refs_2_, bf16[128,128]{1,0:T(8,128)(2,1)S(1)} %collective-permute-done.6.refs_3_, ...), custom_call_target="tpu_custom_call" | custom-call | tf_op jit(solution)/shard_map/pallas_call | solution.py:206
Async XLA Ops:
  0.0 7.7 %collective-permute-start.3 = (bf16[128,128]{1,0:T(8,128)(2,1)}, bf16[128,128]{1,0:T(8,128)(2,1)S(1)}, u32[]{:S(2)}, u32[]{:S(2)}) collective-permute-start(bf16[128,128]{1,0:T(8,128)(2,1)} %bitcast.4), channel_id=1, source_target_pairs={{0,6},{1,7},{2,5},{3,4},{4,2},{5,3},{6,1},{7,0},{8,14},{9,15},{10,... | collective-permute-start | bytes 98312 | tf_op jit(solution)/shard_map/ppermute | solution.py:223
  3.5 4.5 %collective-permute-start.2 = (bf16[128,128]{1,0:T(8,128)(2,1)}, bf16[128,128]{1,0:T(8,128)(2,1)S(1)}, u32[]{:S(2)}, u32[]{:S(2)}) collective-permute-start(bf16[128,128]{1,0:T(8,128)(2,1)} %bitcast.5), channel_id=1, source_target_pairs={{0,7},{1,6},{2,4},{3,5},{4,3},{5,2},{6,0},{7,1},{8,15},{9,14},{10,... | collective-permute-start | bytes 98312 | tf_op jit(solution)/shard_map/ppermute | solution.py:223
  4.5 3.8 %collective-permute-start.1 = (bf16[128,128]{1,0:T(8,128)(2,1)}, bf16[128,128]{1,0:T(8,128)(2,1)S(1)}, u32[]{:S(2)}, u32[]{:S(2)}) collective-permute-start(bf16[128,128]{1,0:T(8,128)(2,1)} %bitcast.6), channel_id=1, source_target_pairs={{0,5},{1,4},{2,7},{3,6},{4,1},{5,0},{6,3},{7,2},{8,13},{9,12},{10,... | collective-permute-start | bytes 98312 | tf_op jit(solution)/shard_map/ppermute | solution.py:223
  5.3 2.9 %collective-permute-start = (bf16[128,128]{1,0:T(8,128)(2,1)}, bf16[128,128]{1,0:T(8,128)(2,1)S(1)}, u32[]{:S(2)}, u32[]{:S(2)}) collective-permute-start(bf16[128,128]{1,0:T(8,128)(2,1)} %bitcast.7), channel_id=1, source_target_pairs={{0,4},{1,5},{2,6},{3,7},{4,0},{5,1},{6,2},{7,3},{8,12},{9,13},{10,... | collective-permute-start | bytes 98312 | tf_op jit(solution)/shard_map/ppermute | solution.py:223
  6.0 0.7 %copy-start = (s32[64]{0:T(128)S(1)}, s32[64]{0:T(128)}, u32[]{:S(2)}) copy-start(s32[64]{0:T(128)} %param.16) | copy-start | bytes 772
  9.4 4.6 %collective-permute-start.7 = (bf16[128,128]{1,0:T(8,128)(2,1)S(1)}, bf16[128,128]{1,0:T(8,128)(2,1)S(1)}, u32[]{:S(2)}, u32[]{:S(2)}) collective-permute-start(bf16[128,128]{1,0:T(8,128)(2,1)S(1)} %shard_map.146.refs_1_), channel_id=1, source_target_pairs={{0,28},{1,29},{2,30},{3,31},{4,24},{5,25},{6,26},{7,27},{8,20},{9,... | collective-permute-start | bytes 98312 | tf_op jit(solution)/shard_map/ppermute | solution.py:223
  12.3 3.3 %collective-permute-start.6 = (bf16[128,128]{1,0:T(8,128)(2,1)S(1)}, bf16[128,128]{1,0:T(8,128)(2,1)S(1)}, u32[]{:S(2)}, u32[]{:S(2)}) collective-permute-start(bf16[128,128]{1,0:T(8,128)(2,1)S(1)} %shard_map.146.refs_1_), channel_id=1, source_target_pairs={{0,20},{1,21},{2,22},{3,23},{4,16},{5,17},{6,18},{7,19},{8,28},{9,... | collective-permute-start | bytes 98312 | tf_op jit(solution)/shard_map/ppermute | solution.py:223
  12.7 3.5 %collective-permute-start.5 = (bf16[128,128]{1,0:T(8,128)(2,1)S(1)}, bf16[128,128]{1,0:T(8,128)(2,1)S(1)}, u32[]{:S(2)}, u32[]{:S(2)}) collective-permute-start(bf16[128,128]{1,0:T(8,128)(2,1)S(1)} %shard_map.146.refs_1_), channel_id=1, source_target_pairs={{0,12},{1,13},{2,14},{3,15},{4,8},{5,9},{6,10},{7,11},{8,4},{9,5},... | collective-permute-start | bytes 98312 | tf_op jit(solution)/shard_map/ppermute | solution.py:223
  13.0 3.3 %collective-permute-start.4 = (bf16[128,128]{1,0:T(8,128)(2,1)S(1)}, bf16[128,128]{1,0:T(8,128)(2,1)S(1)}, u32[]{:S(2)}, u32[]{:S(2)}) collective-permute-start(bf16[128,128]{1,0:T(8,128)(2,1)S(1)} %shard_map.146.refs_1_), channel_id=1, source_target_pairs={{0,4},{1,5},{2,6},{3,7},{4,0},{5,1},{6,2},{7,3},{8,12},{9,13},{10,... | collective-permute-start | bytes 98312 | tf_op jit(solution)/shard_map/ppermute | solution.py:223
  14.0 2.3 %collective-permute-start.10 = (bf16[128,128]{1,0:T(8,128)(2,1)S(1)}, bf16[128,128]{1,0:T(8,128)(2,1)S(1)}, u32[]{:S(2)}, u32[]{:S(2)}) collective-permute-start(bf16[128,128]{1,0:T(8,128)(2,1)S(1)} %collective-permute-done.7.refs_4_), channel_id=1, source_target_pairs={{0,4},{1,5},{2,6},{3,7},{4,0},{5,1},{6,2},{7,3},{8,12},{9,13},{10,... | collective-permute-start | bytes 98312 | tf_op jit(solution)/shard_map/ppermute | solution.py:223
  15.7 1.3 %collective-permute-start.9 = (bf16[128,128]{1,0:T(8,128)(2,1)S(1)}, bf16[128,128]{1,0:T(8,128)(2,1)S(1)}, u32[]{:S(2)}, u32[]{:S(2)}) collective-permute-start(bf16[128,128]{1,0:T(8,128)(2,1)S(1)} %collective-permute-done.6.refs_3_), channel_id=1, source_target_pairs={{0,4},{1,5},{2,6},{3,7},{4,0},{5,1},{6,2},{7,3},{8,12},{9,13},{10,... | collective-permute-start | bytes 98312 | tf_op jit(solution)/shard_map/ppermute | solution.py:223
  16.2 1.2 %collective-permute-start.8 = (bf16[128,128]{1,0:T(8,128)(2,1)S(1)}, bf16[128,128]{1,0:T(8,128)(2,1)S(1)}, u32[]{:S(2)}, u32[]{:S(2)}) collective-permute-start(bf16[128,128]{1,0:T(8,128)(2,1)S(1)} %collective-permute-done.5.refs_2_), channel_id=1, source_target_pairs={{0,4},{1,5},{2,6},{3,7},{4,0},{5,1},{6,2},{7,3},{8,12},{9,13},{10,... | collective-permute-start | bytes 98312 | tf_op jit(solution)/shard_map/ppermute | solution.py:223

commit v4 on v3

--- a/solution.py
+++ b/solution.py
@@ -97,15 +97,69 @@
     )
 
 
-def attend_kernel(items, pack, group, *refs):
-    *block_refs, weight_ref, gate_bias_ref, bias_ref, out_ref, turned_ref = refs
+def normalize(x):
+    channels = x.shape[1]
+    averaging = jnp.full((channels, channels), 1.0 / channels, jnp.bfloat16)
+    mean = jnp.dot(x, averaging, preferred_element_type=jnp.float32)
+    centered = x.astype(jnp.float32) - mean
+    variance = jnp.mean(centered * centered, axis=1, keepdims=True)
+    return (centered * lax.rsqrt(variance + epsilon)).astype(jnp.bfloat16)
+
+
+def keys_and_values(normed, weight_ref):
     channels = weight_ref.shape[0]
+    return jnp.dot(
+        normed, weight_ref[:, 2 * channels : 4 * channels], preferred_element_type=jnp.float32
+    ).astype(jnp.bfloat16)
+
+
+def queries_and_gate(normed, weight_ref, gate_bias_ref):
+    channels = weight_ref.shape[0]
+    products = jnp.dot(normed, weight_ref[:, : 2 * channels], preferred_element_type=jnp.float32)
+    return products[:, :channels], jax.nn.sigmoid(products[:, channels:] + gate_bias_ref[...])
+
+
+def project_kernel(own, *refs):
+    *block_refs, weight_ref, gate_bias_ref, query_ref, gate_ref, product_ref = refs
+    rows, channels = block_refs[0].shape
+
+    def keep(at, normed):
+        queries, gate_ref[at] = queries_and_gate(normed, weight_ref, gate_bias_ref)
+        query_ref[at] = queries.astype(jnp.bfloat16)
+
+    if rows * len(block_refs) <= group_rows:
+        normed = normalize(jnp.concatenate([ref[...] for ref in block_refs], 0))
+        keep(slice(None), normed[own * rows : (own + 1) * rows])
+        product_ref[...] = keys_and_values(normed, weight_ref)
+        return
+    chunk = math.gcd(rows, group_rows)
+    for b, ref in enumerate(block_refs):
+
+        def body(c, carry):
+            at = pl.ds(pl.multiple_of(c * chunk, chunk), chunk)
+            normed = normalize(ref[at])
+            if b == own:
+                keep(at, normed)
+            to = pl.ds(pl.multiple_of(b * rows + c * chunk, chunk), chunk)
+            product_ref[to] = keys_and_values(normed, weight_ref)
+            return carry
+
+        lax.fori_loop(0, rows // chunk, body, 0)
+
+
+def attend_kernel(split, own, items, pack, group, *refs):
+    weight_ref, gate_bias_ref, bias_ref, out_ref, turned_ref = refs[-5:]
+    rows, channels = out_ref.shape
+    if split:
+        own_ref, query_ref, gate_ref, product_ref, *late_refs = refs[:-5]
+    else:
+        late_refs = refs[:-5]
+        own_ref = late_refs[own]
+    early = product_ref.shape[0] // rows if split else 0
     head_size = channels // H
-    rows = out_ref.shape[0]
     part = rows // items
     step_rows, pack_rows = group * part, pack * part
-    places = [(ref, b) for ref in block_refs for b in range(ref.shape[0] // rows)]
-    blocks = len(places)
+    blocks = early + len(late_refs)
     scale = math.log2(math.e) / math.sqrt(head_size)
     head_of = lax.broadcasted_iota(jnp.int32, (1, channels), 1) // head_size
     shape = (H * pack_rows, blocks * pack_rows)
@@ -114,51 +168,36 @@
     bias = jnp.where(row_item == key_item, bias_ref[...], masked_score)
 
     def step(start):
-        x = jnp.concatenate(
-            [ref[pl.ds(b * rows + start, step_rows), :] for ref, b in places], 0
-        )
-        averaging = jnp.full((channels, channels), 1.0 / channels, jnp.bfloat16)
-        mean = jnp.dot(x, averaging, preferred_element_type=jnp.float32)
-        x = x.astype(jnp.float32)
-        centered = x - mean
-        variance = jnp.mean(centered * centered, axis=1, keepdims=True)
-        normed = (centered * lax.rsqrt(variance + epsilon)).astype(jnp.bfloat16)
-        own_products = jnp.dot(
-            normed[:step_rows], weight_ref[:, : 2 * channels], preferred_element_type=jnp.float32
-        )
-        queries = own_products[:, :channels]
-        gate = jax.nn.sigmoid(own_products[:, channels:] + gate_bias_ref[...])
-        products = jnp.dot(
-            normed, weight_ref[:, 2 * channels : 4 * channels], preferred_element_type=jnp.float32
-        ).astype(jnp.bfloat16)
+        here = pl.ds(start, step_rows)
+        normed = normalize(jnp.concatenate([ref[here] for ref in late_refs], 0))
+        if split:
+            queries, gate = query_ref[here].astype(jnp.float32), gate_ref[here]
+        else:
+            queries, gate = queries_and_gate(
+                normed[own * step_rows : (own + 1) * step_rows], weight_ref, gate_bias_ref
+            )
+        late = keys_and_values(normed, weight_ref)
+        products = [product_ref[pl.ds(b * rows + start, step_rows)] for b in range(early)]
+        products += [late[b * step_rows : (b + 1) * step_rows] for b in range(len(late_refs))]
         packs = range(group // pack)
         held = [
-            jnp.concatenate(
-                [products[b * step_rows + i * pack_rows :][:pack_rows] for b in range(blocks)], 0
-            )
+            jnp.concatenate([p[i * pack_rows : (i + 1) * pack_rows] for p in products], 0)
             for i in packs
         ]
-        stacked = [
-            jnp.concatenate(
-                [
-                    jnp.where(head_of == h, queries[i * pack_rows : (i + 1) * pack_rows], 0.0)
-                    for h in range(H)
-                ],
-                0,
-            ).astype(jnp.bfloat16)
-            for i in packs
-        ]
-        scores = [
-            lax.dot_general(
-                stacked[i],
-                held[i][:, :channels],
-                (((1,), (1,)), ((), ())),
-                preferred_element_type=jnp.float32,
+        scores = []
+        for i in packs:
+            query = queries[i * pack_rows : (i + 1) * pack_rows]
+            stacked = jnp.concatenate([jnp.where(head_of == h, query, 0.0) for h in range(H)], 0)
+            scores.append(
+                lax.dot_general(
+                    stacked.astype(jnp.bfloat16),
+                    held[i][:, :channels],
+                    (((1,), (1,)), ((), ())),
+                    preferred_element_type=jnp.float32,
+                )
+                * scale
+                + bias
             )
-            * scale
-            + bias
-            for i in packs
-        ]
         scores = jnp.concatenate(scores, 0)
         expanded = jnp.exp2(scores - jnp.max(scores, axis=1, keepdims=True))
         weights = (expanded * (1.0 / jnp.sum(expanded, axis=1, keepdims=True))).astype(jnp.bfloat16)
@@ -177,7 +216,7 @@
             attended.append(picked)
         attended = jnp.concatenate(attended, 0).astype(jnp.bfloat16).astype(jnp.float32)
         gated = (gate * attended).astype(jnp.bfloat16)
-        return x[:step_rows] + jnp.dot(
+        return own_ref[here].astype(jnp.float32) + jnp.dot(
             gated, weight_ref[:, 4 * channels :], preferred_element_type=jnp.float32
         )
 
@@ -200,17 +239,42 @@
     out_ref[...] = turned_ref[...].astype(out_ref.dtype)
 
 
-def attend(blocks, rows, items, packing, prepared):
-    channels = blocks[0].shape[1]
-    held = sum(b.size * b.dtype.itemsize for b in blocks)
+def project(blocks, own, weights, gate_bias):
+    rows, channels = blocks[0].shape
     return pl.pallas_call(
-        functools.partial(attend_kernel, items, *packing),
-        out_shape=jax.ShapeDtypeStruct((rows, channels), jnp.bfloat16),
-        in_specs=[vmem] * (len(blocks) + len(prepared)),
+        functools.partial(project_kernel, own),
+        out_shape=(
+            jax.ShapeDtypeStruct((rows, channels), jnp.bfloat16),
+            jax.ShapeDtypeStruct((rows, channels), jnp.float32),
+            jax.ShapeDtypeStruct((len(blocks) * rows, 2 * channels), jnp.bfloat16),
+        ),
+        in_specs=[vmem] * (len(blocks) + 2),
+        out_specs=(vmem,) * 3,
+        compiler_params=pltpu.CompilerParams(
+            vmem_limit_bytes=8 * len(blocks) * rows * channels + 16 * 2**20
+        ),
+    )(*blocks, weights, gate_bias)
+
+
+def attend(early, late, own, items, packing, prepared):
+    weights, gate_bias, bias = prepared
+    operands = [*late, *prepared]
+    if early:
+        operands = [early[own], *project(early, own, weights, gate_bias), *operands]
+    return pl.pallas_call(
+        functools.partial(attend_kernel, bool(early), own, items, *packing),
+        out_shape=jax.ShapeDtypeStruct(late[0].shape, jnp.bfloat16),
+        in_specs=[vmem] * len(operands),
         out_specs=vmem,
-        scratch_shapes=[pltpu.VMEM((rows, channels), jnp.float32)],
-        compiler_params=pltpu.CompilerParams(vmem_limit_bytes=held + 16 * 2**20),
-    )(*blocks, *prepared)
+        scratch_shapes=[pltpu.VMEM(late[0].shape, jnp.float32)],
+        compiler_params=pltpu.CompilerParams(
+            vmem_limit_bytes=sum(v.size * v.dtype.itemsize for v in operands) + 16 * 2**20
+        ),
+    )(*operands)
+
+
+def shifts(size):
+    return sorted(range(1, size), key=lambda s: (min(s, size - s), s))
 
 
 def send(values, to):
@@ -244,22 +308,27 @@
     dest_size = lax.axis_size("dest")
     orig_size = lax.axis_size("orig")
     regions = region_mask.shape[0]
-    row_steps = sorted(range(dest_size), key=lambda s: (s > 0, -min(s, dest_size - s), -s))
-    chip_steps = list(range(2, orig_size, 2))
-    col_steps = [0, 1] + chip_steps + [s ^ 1 for s in chip_steps]
+    row_steps = shifts(dest_size) + [0]
+    chip_steps = shifts(orig_size // 2)
 
     def along_dest(d, step):
         return reverse((reverse(d, dest_size) + step) % dest_size, dest_size)
 
+    def along_orig(o, step, flip):
+        return (o // 2 + step) % (orig_size // 2) * 2 + (o % 2 ^ flip)
+
+    row_sources = [lambda d, s=s: along_dest(d, dest_size - s) for s in row_steps]
+    col_sources = [lambda o: o, lambda o: o ^ 1]
+    for flip in (0, 1):
+        col_sources += [
+            lambda o, s=s, flip=flip: along_orig(o, orig_size // 2 - s, flip) for s in chip_steps
+        ]
     row_packing = packing(tile_rows, regions)
     col_packing = packing(tile_cols, regions)
     rows = tile_rows * tile_cols
     prepared = prepare(
         ("dest", "orig"),
-        (
-            [lambda d, s=s: along_dest(d, dest_size - s) for s in row_steps],
-            [lambda o, s=s: o ^ s for s in col_steps],
-        ),
+        (row_sources, col_sources),
         (tile_cols, tile_rows),
         (row_packing[0], col_packing[0]),
         region_mask,
@@ -271,12 +340,12 @@
 
     tile = pair_field.reshape(rows, channels)
     blocks = [send(tile, lambda o, d: (o ^ 1, along_dest(d, s))) for s in row_steps]
-    turned = attend(blocks, rows, tile_rows, row_packing, prepared[:3])
+    turned = attend([], blocks, row_steps.index(0), tile_rows, row_packing, prepared[:3])
     own = send(turned, lambda o, d: (o ^ 1, d))
-    near = [send(turned, lambda o, d: (o ^ s ^ 1, d)) for s in chip_steps]
+    near = [send(turned, lambda o, d: (along_orig(o, s, 1), d)) for s in chip_steps]
     other = [send(block, lambda o, d: (o ^ 1, d)) for block in near]
-    blocks = [own, turned] + near + other
-    result = attend(blocks, rows, tile_cols, col_packing, prepared[3:])
+    early = [own, turned, *near, *other[:-1]]
+    result = attend(early, other[-1:], 0, tile_cols, col_packing, prepared[3:])
     return result.reshape(tile_rows, tile_cols, channels)
 
 

time: 19.6 us -> 18.9 us (0.964)
  waiting for transfers between devices: 3.86 us -> 1.54 us
  starting transfers between devices: 9.99 us -> 11.4 us
  Pallas kernels: 4.16 us -> 4.41 us
    ppermute x11, waiting for transfers between devices: 3.86 us -> 1.54 us  [send(): return lax.ppermute(values, ('orig', 'dest'), pairs)]
    ppermute x11, starting transfers between devices: 9.99 us -> 11.4 us  [send(): return lax.ppermute(values, ('orig', 'dest'), pairs)]
    pallas_call x2 -> x3, Pallas kernels: 3.12 us -> 3.38 us  [the longest x2 2.82 us: attend(): pl.pallas_call(functools.partial(attend_kernel, bool(early), own, items,...]
  transfers between devices with their start and end apart: 11 -> 11, of which waited for: 6 -> 6; matrix products, arithmetic and copies ran while one was open for 0% -> 0% of each run, Pallas kernels for 5% -> 8%
where the time goes in v4:
time: 18.9 us; the launch traced here: 18.7 us
  starting transfers between devices  11.4 us (60%)
  Pallas kernels  4.41 us (23%)
  waiting for transfers between devices  1.54 us (8%)
  between operations  0.69 us (4%)
  local copies, waits for them, and re-layouts  0.65 us (3%)
    ppermute x11, starting transfers between devices, send(): return lax.ppermute(values, ('orig', 'dest'), pairs)  11.4 us
    pallas_call x2, Pallas kernels, attend(): pl.pallas_call(functools.partial(attend_kernel, bool(early), own, items,...  2.82 us
    ppermute x11, waiting for transfers between devices, send(): return lax.ppermute(values, ('orig', 'dest'), pairs)  1.54 us
    pallas_call x1, Pallas kernels, prepare(): pl.pallas_call(functools.partial(prepare_kernel, axes, sources, parts, pa...  1.04 us
    unnamed x2, local copies, waits for them, and re-layouts  0.65 us
    pallas_call x1, Pallas kernels, project(): pl.pallas_call(functools.partial(project_kernel, own), out_shape=(jax.Sha...  0.55 us
  transfers between devices with their start and end apart: 11, of which 6 were waited for; matrix products, arithmetic and copies ran while one was open for 0% of the time, Pallas kernels for 8%

profile of v4, /device:TPU:0, one launch (start us, length us, event | category | flops | bytes accessed | tf_op | source)
XLA Modules:
  0.0 18.7 jit_solution(11791049197621452747)
XLA Ops:
  0.0 3.5 %collective-permute-start = (bf16[128,128]{1,0:T(8,128)(2,1)}, bf16[128,128]{1,0:T(8,128)(2,1)S(1)}, u32[]{:S(2)}, u32[]{:S(2)}) collective-permute-start(bf16[128,128]{1,0:T(8,128)(2,1)} %bitcast.4), channel_id=1, source_target_pairs={{0,6},{1,7},{2,5},{3,4},{4,2},{5,3},{6,1},{7,0},{8,14},{9,15},{10,... | collective-permute-start | bytes 98312 | tf_op jit(solution)/shard_map/ppermute | solution.py:287
  3.5 1.0 %collective-permute-start.1 = (bf16[128,128]{1,0:T(8,128)(2,1)}, bf16[128,128]{1,0:T(8,128)(2,1)S(1)}, u32[]{:S(2)}, u32[]{:S(2)}) collective-permute-start(bf16[128,128]{1,0:T(8,128)(2,1)} %bitcast.5), channel_id=1, source_target_pairs={{0,7},{1,6},{2,4},{3,5},{4,3},{5,2},{6,0},{7,1},{8,15},{9,14},{10,... | collective-permute-start | bytes 98312 | tf_op jit(solution)/shard_map/ppermute | solution.py:287
  4.5 0.8 %collective-permute-start.2 = (bf16[128,128]{1,0:T(8,128)(2,1)}, bf16[128,128]{1,0:T(8,128)(2,1)S(1)}, u32[]{:S(2)}, u32[]{:S(2)}) collective-permute-start(bf16[128,128]{1,0:T(8,128)(2,1)} %bitcast.6), channel_id=1, source_target_pairs={{0,5},{1,4},{2,7},{3,6},{4,1},{5,0},{6,3},{7,2},{8,13},{9,12},{10,... | collective-permute-start | bytes 98312 | tf_op jit(solution)/shard_map/ppermute | solution.py:287
  5.3 0.0 collective-permute-start.3
  6.0 0.0 copy-start
  6.0 0.6 %copy-done = s32[64]{0:T(128)S(1)} copy-done((s32[64]{0:T(128)S(1)}, s32[64]{0:T(128)}, u32[]{:S(2)}) %copy-start) | copy-done | bytes 280
  6.6 1.0 %shard_map.145 = (bf16[128,640]{1,0:T(8,128)(2,1)S(1)}, f32[1,128]{1,0:T(1,128)S(1)}, f32[1,128]{1,0:T(1,128)S(1)}, bf16[128,640]{1,0:T(8,128)(2,1)S(1)}, f32[1,128]{1,0:T(1,128)S(1)}, /*index=5*/f32[1,128]{1,0:T(1,128)S(1)}) custom-call(s32[1,64]{1,0:T(1,128)S(1)} %bitcast.3, s32[1]{0:T(128)S(6)} %copy.16.count_ref, bf16[1,128,128]{2,1,0:T(8,128)(2,1)} %refs_0_.1, ...), custom_call_target="tpu_custom_call" | custom-call | flops 1048576 | bytes 1048576 | tf_op jit(solution)/shard_map/pallas_call | solution.py:84
  7.7 0.0 collective-permute-done.refs_0_
  7.7 0.2 %collective-permute-done.1.refs_1_ = bf16[128,128]{1,0:T(8,128)(2,1)S(1)} collective-permute-done((bf16[128,128]{1,0:T(8,128)(2,1)}, bf16[128,128]{1,0:T(8,128)(2,1)S(1)}, u32[]{:S(2)}, u32[]{:S(2)}) %collective-permute-start.1) | collective-permute-done | bytes 32800 | tf_op jit(solution)/shard_map/ppermute | solution.py:287
  7.9 0.3 %collective-permute-done.2.refs_2_ = bf16[128,128]{1,0:T(8,128)(2,1)S(1)} collective-permute-done((bf16[128,128]{1,0:T(8,128)(2,1)}, bf16[128,128]{1,0:T(8,128)(2,1)S(1)}, u32[]{:S(2)}, u32[]{:S(2)}) %collective-permute-start.2) | collective-permute-done | bytes 32800 | tf_op jit(solution)/shard_map/ppermute | solution.py:287
  8.3 0.0 collective-permute-done.3.refs_3_
  8.3 1.2 %shard_map.146.refs_1_ = bf16[128,128]{1,0:T(8,128)(2,1)S(1)} custom-call(bf16[128,128]{1,0:T(8,128)(2,1)S(1)} %collective-permute-done.refs_0_, bf16[128,128]{1,0:T(8,128)(2,1)S(1)} %collective-permute-done.1.refs_1_, bf16[128,128]{1,0:T(8,128)(2,1)S(1)} %collective-permute-done.2.refs_2_, bf16[128,128]{1,0:T(8,128)(2,1)S(1)} %collective-permute-done.3.refs_3_, ...), custom_call_target="tpu_custom_call" | custom-call | tf_op jit(solution)/shard_map/pallas_call | solution.py:264
  9.5 1.9 %collective-permute-start.5 = (bf16[128,128]{1,0:T(8,128)(2,1)S(1)}, bf16[128,128]{1,0:T(8,128)(2,1)S(1)}, u32[]{:S(2)}, u32[]{:S(2)}) collective-permute-start(bf16[128,128]{1,0:T(8,128)(2,1)S(1)} %shard_map.146.refs_1_), channel_id=1, source_target_pairs={{0,12},{1,13},{2,14},{3,15},{4,8},{5,9},{6,10},{7,11},{8,20},{9,21... | collective-permute-start | bytes 98312 | tf_op jit(solution)/shard_map/ppermute | solution.py:287
  11.4 1.0 %collective-permute-start.6 = (bf16[128,128]{1,0:T(8,128)(2,1)S(1)}, bf16[128,128]{1,0:T(8,128)(2,1)S(1)}, u32[]{:S(2)}, u32[]{:S(2)}) collective-permute-start(bf16[128,128]{1,0:T(8,128)(2,1)S(1)} %shard_map.146.refs_1_), channel_id=1, source_target_pairs={{0,28},{1,29},{2,30},{3,31},{4,24},{5,25},{6,26},{7,27},{8,4},{9,5... | collective-permute-start | bytes 98312 | tf_op jit(solution)/shard_map/ppermute | solution.py:287
  12.4 1.7 %collective-permute-start.7 = (bf16[128,128]{1,0:T(8,128)(2,1)S(1)}, bf16[128,128]{1,0:T(8,128)(2,1)S(1)}, u32[]{:S(2)}, u32[]{:S(2)}) collective-permute-start(bf16[128,128]{1,0:T(8,128)(2,1)S(1)} %shard_map.146.refs_1_), channel_id=1, source_target_pairs={{0,20},{1,21},{2,22},{3,23},{4,16},{5,17},{6,18},{7,19},{8,28},{9,... | collective-permute-start | bytes 98312 | tf_op jit(solution)/shard_map/ppermute | solution.py:287
  14.1 0.3 %collective-permute-start.4 = (bf16[128,128]{1,0:T(8,128)(2,1)S(1)}, bf16[128,128]{1,0:T(8,128)(2,1)S(1)}, u32[]{:S(2)}, u32[]{:S(2)}) collective-permute-start(bf16[128,128]{1,0:T(8,128)(2,1)S(1)} %shard_map.146.refs_1_), channel_id=1, source_target_pairs={{0,4},{1,5},{2,6},{3,7},{4,0},{5,1},{6,2},{7,3},{8,12},{9,13},{10,... | collective-permute-start | bytes 98312 | tf_op jit(solution)/shard_map/ppermute | solution.py:287
  14.3 0.0 collective-permute-done.5.refs_2_
  14.3 0.3 %collective-permute-start.8 = (bf16[128,128]{1,0:T(8,128)(2,1)S(1)}, bf16[128,128]{1,0:T(8,128)(2,1)S(1)}, u32[]{:S(2)}, u32[]{:S(2)}) collective-permute-start(bf16[128,128]{1,0:T(8,128)(2,1)S(1)} %collective-permute-done.5.refs_2_), channel_id=1, source_target_pairs={{0,4},{1,5},{2,6},{3,7},{4,0},{5,1},{6,2},{7,3},{8,12},{9,13},{10,... | collective-permute-start | bytes 98312 | tf_op jit(solution)/shard_map/ppermute | solution.py:287
  14.6 0.5 %collective-permute-done.6.refs_3_ = bf16[128,128]{1,0:T(8,128)(2,1)S(1)} collective-permute-done((bf16[128,128]{1,0:T(8,128)(2,1)S(1)}, bf16[128,128]{1,0:T(8,128)(2,1)S(1)}, u32[]{:S(2)}, u32[]{:S(2)}) %collective-permute-start.6) | collective-permute-done | bytes 32800 | tf_op jit(solution)/shard_map/ppermute | solution.py:287
  15.1 0.5 %collective-permute-start.9 = (bf16[128,128]{1,0:T(8,128)(2,1)S(1)}, bf16[128,128]{1,0:T(8,128)(2,1)S(1)}, u32[]{:S(2)}, u32[]{:S(2)}) collective-permute-start(bf16[128,128]{1,0:T(8,128)(2,1)S(1)} %collective-permute-done.6.refs_3_), channel_id=1, source_target_pairs={{0,4},{1,5},{2,6},{3,7},{4,0},{5,1},{6,2},{7,3},{8,12},{9,13},{10,... | collective-permute-start | bytes 98312 | tf_op jit(solution)/shard_map/ppermute | solution.py:287
  15.6 0.2 %collective-permute-done.7.refs_4_ = bf16[128,128]{1,0:T(8,128)(2,1)S(1)} collective-permute-done((bf16[128,128]{1,0:T(8,128)(2,1)S(1)}, bf16[128,128]{1,0:T(8,128)(2,1)S(1)}, u32[]{:S(2)}, u32[]{:S(2)}) %collective-permute-start.7) | collective-permute-done | bytes 32800 | tf_op jit(solution)/shard_map/ppermute | solution.py:287
  15.8 0.4 %collective-permute-start.10 = (bf16[128,128]{1,0:T(8,128)(2,1)S(1)}, bf16[128,128]{1,0:T(8,128)(2,1)S(1)}, u32[]{:S(2)}, u32[]{:S(2)}) collective-permute-start(bf16[128,128]{1,0:T(8,128)(2,1)S(1)} %collective-permute-done.7.refs_4_), channel_id=1, source_target_pairs={{0,4},{1,5},{2,6},{3,7},{4,0},{5,1},{6,2},{7,3},{8,12},{9,13},{10,... | collective-permute-start | bytes 98312 | tf_op jit(solution)/shard_map/ppermute | solution.py:287
  16.2 0.0 collective-permute-done.4.refs_0_
  16.2 0.0 collective-permute-done.8.refs_5_
  16.2 0.2 %collective-permute-done.9.refs_6_ = bf16[128,128]{1,0:T(8,128)(2,1)S(1)} collective-permute-done((bf16[128,128]{1,0:T(8,128)(2,1)S(1)}, bf16[128,128]{1,0:T(8,128)(2,1)S(1)}, u32[]{:S(2)}, u32[]{:S(2)}) %collective-permute-start.9) | collective-permute-done | bytes 32800 | tf_op jit(solution)/shard_map/ppermute | solution.py:287
  16.4 0.6 %shard_map.147 = (bf16[128,128]{1,0:T(8,128)(2,1)S(1)}, f32[128,128]{1,0:T(8,128)S(1)}, bf16[896,256]{1,0:T(8,128)(2,1)S(1)}) custom-call(bf16[128,128]{1,0:T(8,128)(2,1)S(1)} %collective-permute-done.4.refs_0_, bf16[128,128]{1,0:T(8,128)(2,1)S(1)} %shard_map.146.refs_1_, bf16[128,128]{1,0:T(8,128)(2,1)S(1)} %collective-permute-done.5.refs_2_, ...), custom_call_target="tpu_custom_call" | custom-call | tf_op jit(solution)/shard_map/pallas_call | solution.py:244
  17.0 0.1 collective-permute-done.10.refs_4_
  17.1 1.6 %shard_map.148 = bf16[128,128]{1,0:T(8,128)(2,1)} custom-call(bf16[128,128]{1,0:T(8,128)(2,1)S(1)} %collective-permute-done.4.refs_0_, bf16[128,128]{1,0:T(8,128)(2,1)S(1)} %get-tuple-element.19.refs_1_, f32[128,128]{1,0:T(8,128)S(1)} %get-tuple-element.20.refs_2_, bf16[896,256]{1,0:T(8,128)(2,1)S(1)} %get-tuple-element.21.refs_3_, ...), custom_call_target="tpu_custom_call" | custom-call | tf_op jit(solution)/shard_map/pallas_call | solution.py:264
Async XLA Ops:
  0.0 7.7 %collective-permute-start = (bf16[128,128]{1,0:T(8,128)(2,1)}, bf16[128,128]{1,0:T(8,128)(2,1)S(1)}, u32[]{:S(2)}, u32[]{:S(2)}) collective-permute-start(bf16[128,128]{1,0:T(8,128)(2,1)} %bitcast.4), channel_id=1, source_target_pairs={{0,6},{1,7},{2,5},{3,4},{4,2},{5,3},{6,1},{7,0},{8,14},{9,15},{10,... | collective-permute-start | bytes 98312 | tf_op jit(solution)/shard_map/ppermute | solution.py:287
  3.5 4.5 %collective-permute-start.1 = (bf16[128,128]{1,0:T(8,128)(2,1)}, bf16[128,128]{1,0:T(8,128)(2,1)S(1)}, u32[]{:S(2)}, u32[]{:S(2)}) collective-permute-start(bf16[128,128]{1,0:T(8,128)(2,1)} %bitcast.5), channel_id=1, source_target_pairs={{0,7},{1,6},{2,4},{3,5},{4,3},{5,2},{6,0},{7,1},{8,15},{9,14},{10,... | collective-permute-start | bytes 98312 | tf_op jit(solution)/shard_map/ppermute | solution.py:287
  4.5 3.8 %collective-permute-start.2 = (bf16[128,128]{1,0:T(8,128)(2,1)}, bf16[128,128]{1,0:T(8,128)(2,1)S(1)}, u32[]{:S(2)}, u32[]{:S(2)}) collective-permute-start(bf16[128,128]{1,0:T(8,128)(2,1)} %bitcast.6), channel_id=1, source_target_pairs={{0,5},{1,4},{2,7},{3,6},{4,1},{5,0},{6,3},{7,2},{8,13},{9,12},{10,... | collective-permute-start | bytes 98312 | tf_op jit(solution)/shard_map/ppermute | solution.py:287
  5.3 2.9 %collective-permute-start.3 = (bf16[128,128]{1,0:T(8,128)(2,1)}, bf16[128,128]{1,0:T(8,128)(2,1)S(1)}, u32[]{:S(2)}, u32[]{:S(2)}) collective-permute-start(bf16[128,128]{1,0:T(8,128)(2,1)} %bitcast.7), channel_id=1, source_target_pairs={{0,4},{1,5},{2,6},{3,7},{4,0},{5,1},{6,2},{7,3},{8,12},{9,13},{10,... | collective-permute-start | bytes 98312 | tf_op jit(solution)/shard_map/ppermute | solution.py:287
  6.0 0.7 %copy-start = (s32[64]{0:T(128)S(1)}, s32[64]{0:T(128)}, u32[]{:S(2)}) copy-start(s32[64]{0:T(128)} %param.16) | copy-start | bytes 772
  9.5 4.9 %collective-permute-start.5 = (bf16[128,128]{1,0:T(8,128)(2,1)S(1)}, bf16[128,128]{1,0:T(8,128)(2,1)S(1)}, u32[]{:S(2)}, u32[]{:S(2)}) collective-permute-start(bf16[128,128]{1,0:T(8,128)(2,1)S(1)} %shard_map.146.refs_1_), channel_id=1, source_target_pairs={{0,12},{1,13},{2,14},{3,15},{4,8},{5,9},{6,10},{7,11},{8,20},{9,21... | collective-permute-start | bytes 98312 | tf_op jit(solution)/shard_map/ppermute | solution.py:287
  11.4 3.6 %collective-permute-start.6 = (bf16[128,128]{1,0:T(8,128)(2,1)S(1)}, bf16[128,128]{1,0:T(8,128)(2,1)S(1)}, u32[]{:S(2)}, u32[]{:S(2)}) collective-permute-start(bf16[128,128]{1,0:T(8,128)(2,1)S(1)} %shard_map.146.refs_1_), channel_id=1, source_target_pairs={{0,28},{1,29},{2,30},{3,31},{4,24},{5,25},{6,26},{7,27},{8,4},{9,5... | collective-permute-start | bytes 98312 | tf_op jit(solution)/shard_map/ppermute | solution.py:287
  12.4 3.3 %collective-permute-start.7 = (bf16[128,128]{1,0:T(8,128)(2,1)S(1)}, bf16[128,128]{1,0:T(8,128)(2,1)S(1)}, u32[]{:S(2)}, u32[]{:S(2)}) collective-permute-start(bf16[128,128]{1,0:T(8,128)(2,1)S(1)} %shard_map.146.refs_1_), channel_id=1, source_target_pairs={{0,20},{1,21},{2,22},{3,23},{4,16},{5,17},{6,18},{7,19},{8,28},{9,... | collective-permute-start | bytes 98312 | tf_op jit(solution)/shard_map/ppermute | solution.py:287
  14.1 2.1 %collective-permute-start.4 = (bf16[128,128]{1,0:T(8,128)(2,1)S(1)}, bf16[128,128]{1,0:T(8,128)(2,1)S(1)}, u32[]{:S(2)}, u32[]{:S(2)}) collective-permute-start(bf16[128,128]{1,0:T(8,128)(2,1)S(1)} %shard_map.146.refs_1_), channel_id=1, source_target_pairs={{0,4},{1,5},{2,6},{3,7},{4,0},{5,1},{6,2},{7,3},{8,12},{9,13},{10,... | collective-permute-start | bytes 98312 | tf_op jit(solution)/shard_map/ppermute | solution.py:287
  14.3 1.9 %collective-permute-start.8 = (bf16[128,128]{1,0:T(8,128)(2,1)S(1)}, bf16[128,128]{1,0:T(8,128)(2,1)S(1)}, u32[]{:S(2)}, u32[]{:S(2)}) collective-permute-start(bf16[128,128]{1,0:T(8,128)(2,1)S(1)} %collective-permute-done.5.refs_2_), channel_id=1, source_target_pairs={{0,4},{1,5},{2,6},{3,7},{4,0},{5,1},{6,2},{7,3},{8,12},{9,13},{10,... | collective-permute-start | bytes 98312 | tf_op jit(solution)/shard_map/ppermute | solution.py:287
  15.1 1.4 %collective-permute-start.9 = (bf16[128,128]{1,0:T(8,128)(2,1)S(1)}, bf16[128,128]{1,0:T(8,128)(2,1)S(1)}, u32[]{:S(2)}, u32[]{:S(2)}) collective-permute-start(bf16[128,128]{1,0:T(8,128)(2,1)S(1)} %collective-permute-done.6.refs_3_), channel_id=1, source_target_pairs={{0,4},{1,5},{2,6},{3,7},{4,0},{5,1},{6,2},{7,3},{8,12},{9,13},{10,... | collective-permute-start | bytes 98312 | tf_op jit(solution)/shard_map/ppermute | solution.py:287
  15.8 1.3 %collective-permute-start.10 = (bf16[128,128]{1,0:T(8,128)(2,1)S(1)}, bf16[128,128]{1,0:T(8,128)(2,1)S(1)}, u32[]{:S(2)}, u32[]{:S(2)}) collective-permute-start(bf16[128,128]{1,0:T(8,128)(2,1)S(1)} %collective-permute-done.7.refs_4_), channel_id=1, source_target_pairs={{0,4},{1,5},{2,6},{3,7},{4,0},{5,1},{6,2},{7,3},{8,12},{9,13},{10,... | collective-permute-start | bytes 98312 | tf_op jit(solution)/shard_map/ppermute | solution.py:287

commit v5 on v4

--- a/solution.py
+++ b/solution.py
@@ -121,30 +121,13 @@
 
 def project_kernel(own, *refs):
     *block_refs, weight_ref, gate_bias_ref, query_ref, gate_ref, product_ref = refs
-    rows, channels = block_refs[0].shape
-
-    def keep(at, normed):
-        queries, gate_ref[at] = queries_and_gate(normed, weight_ref, gate_bias_ref)
-        query_ref[at] = queries.astype(jnp.bfloat16)
-
-    if rows * len(block_refs) <= group_rows:
-        normed = normalize(jnp.concatenate([ref[...] for ref in block_refs], 0))
-        keep(slice(None), normed[own * rows : (own + 1) * rows])
-        product_ref[...] = keys_and_values(normed, weight_ref)
-        return
-    chunk = math.gcd(rows, group_rows)
-    for b, ref in enumerate(block_refs):
-
-        def body(c, carry):
-            at = pl.ds(pl.multiple_of(c * chunk, chunk), chunk)
-            normed = normalize(ref[at])
-            if b == own:
-                keep(at, normed)
-            to = pl.ds(pl.multiple_of(b * rows + c * chunk, chunk), chunk)
-            product_ref[to] = keys_and_values(normed, weight_ref)
-            return carry
-
-        lax.fori_loop(0, rows // chunk, body, 0)
+    rows = query_ref.shape[0]
+    normed = normalize(jnp.concatenate([ref[...] for ref in block_refs], 0))
+    queries, gate_ref[...] = queries_and_gate(
+        normed[own * rows : (own + 1) * rows], weight_ref, gate_bias_ref
+    )
+    query_ref[...] = queries.astype(jnp.bfloat16)
+    product_ref[...] = keys_and_values(normed, weight_ref)
 
 
 def attend_kernel(split, own, items, pack, group, *refs):
@@ -344,8 +327,9 @@
     own = send(turned, lambda o, d: (o ^ 1, d))
     near = [send(turned, lambda o, d: (along_orig(o, s, 1), d)) for s in chip_steps]
     other = [send(block, lambda o, d: (o ^ 1, d)) for block in near]
-    early = [own, turned, *near, *other[:-1]]
-    result = attend(early, other[-1:], 0, tile_cols, col_packing, prepared[3:])
+    blocks = [own, turned, *near, *other]
+    early = len(blocks) - 1 if (len(blocks) - 1) * rows <= group_rows else 0
+    result = attend(blocks[:early], blocks[early:], 0, tile_cols, col_packing, prepared[3:])
     return result.reshape(tile_rows, tile_cols, channels)
 
 

time: 18.9 us -> 18.9 us (level)
  no operation moved by 1% of the time
where the time goes in v5:
time: 18.9 us; the launch traced here: 18.7 us
  starting transfers between devices  11.4 us (60%)
  Pallas kernels  4.41 us (23%)
  waiting for transfers between devices  1.54 us (8%)
  between operations  0.69 us (4%)
  local copies, waits for them, and re-layouts  0.65 us (3%)
    ppermute x11, starting transfers between devices, send(): return lax.ppermute(values, ('orig', 'dest'), pairs)  11.4 us
    pallas_call x2, Pallas kernels, attend(): pl.pallas_call(functools.partial(attend_kernel, bool(early), own, items,...  2.82 us
    ppermute x11, waiting for transfers between devices, send(): return lax.ppermute(values, ('orig', 'dest'), pairs)  1.54 us
    pallas_call x1, Pallas kernels, prepare(): pl.pallas_call(functools.partial(prepare_kernel, axes, sources, parts, pa...  1.04 us
    unnamed x2, local copies, waits for them, and re-layouts  0.65 us
    pallas_call x1, Pallas kernels, project(): pl.pallas_call(functools.partial(project_kernel, own), out_shape=(jax.Sha...  0.55 us
  transfers between devices with their start and end apart: 11, of which 6 were waited for; matrix products, arithmetic and copies ran while one was open for 0% of the time, Pallas kernels for 8%

profile of v5, /device:TPU:0, one launch (start us, length us, event | category | flops | bytes accessed | tf_op | source)
XLA Modules:
  0.0 18.7 jit_solution(11791049197621452747)
XLA Ops:
  0.0 3.5 %collective-permute-start = (bf16[128,128]{1,0:T(8,128)(2,1)}, bf16[128,128]{1,0:T(8,128)(2,1)S(1)}, u32[]{:S(2)}, u32[]{:S(2)}) collective-permute-start(bf16[128,128]{1,0:T(8,128)(2,1)} %bitcast.4), channel_id=1, source_target_pairs={{0,6},{1,7},{2,5},{3,4},{4,2},{5,3},{6,1},{7,0},{8,14},{9,15},{10,... | collective-permute-start | bytes 98312 | tf_op jit(solution)/shard_map/ppermute | solution.py:270
  3.5 1.0 %collective-permute-start.1 = (bf16[128,128]{1,0:T(8,128)(2,1)}, bf16[128,128]{1,0:T(8,128)(2,1)S(1)}, u32[]{:S(2)}, u32[]{:S(2)}) collective-permute-start(bf16[128,128]{1,0:T(8,128)(2,1)} %bitcast.5), channel_id=1, source_target_pairs={{0,7},{1,6},{2,4},{3,5},{4,3},{5,2},{6,0},{7,1},{8,15},{9,14},{10,... | collective-permute-start | bytes 98312 | tf_op jit(solution)/shard_map/ppermute | solution.py:270
  4.5 0.8 %collective-permute-start.2 = (bf16[128,128]{1,0:T(8,128)(2,1)}, bf16[128,128]{1,0:T(8,128)(2,1)S(1)}, u32[]{:S(2)}, u32[]{:S(2)}) collective-permute-start(bf16[128,128]{1,0:T(8,128)(2,1)} %bitcast.6), channel_id=1, source_target_pairs={{0,5},{1,4},{2,7},{3,6},{4,1},{5,0},{6,3},{7,2},{8,13},{9,12},{10,... | collective-permute-start | bytes 98312 | tf_op jit(solution)/shard_map/ppermute | solution.py:270
  5.3 0.0 collective-permute-start.3
  6.0 0.0 copy-start
  6.0 0.6 %copy-done = s32[64]{0:T(128)S(1)} copy-done((s32[64]{0:T(128)S(1)}, s32[64]{0:T(128)}, u32[]{:S(2)}) %copy-start) | copy-done | bytes 280
  6.6 1.0 %shard_map.145 = (bf16[128,640]{1,0:T(8,128)(2,1)S(1)}, f32[1,128]{1,0:T(1,128)S(1)}, f32[1,128]{1,0:T(1,128)S(1)}, bf16[128,640]{1,0:T(8,128)(2,1)S(1)}, f32[1,128]{1,0:T(1,128)S(1)}, /*index=5*/f32[1,128]{1,0:T(1,128)S(1)}) custom-call(s32[1,64]{1,0:T(1,128)S(1)} %bitcast.3, s32[1]{0:T(128)S(6)} %copy.16.count_ref, bf16[1,128,128]{2,1,0:T(8,128)(2,1)} %refs_0_.1, ...), custom_call_target="tpu_custom_call" | custom-call | flops 1048576 | bytes 1048576 | tf_op jit(solution)/shard_map/pallas_call | solution.py:84
  7.7 0.0 collective-permute-done.refs_0_
  7.7 0.2 %collective-permute-done.1.refs_1_ = bf16[128,128]{1,0:T(8,128)(2,1)S(1)} collective-permute-done((bf16[128,128]{1,0:T(8,128)(2,1)}, bf16[128,128]{1,0:T(8,128)(2,1)S(1)}, u32[]{:S(2)}, u32[]{:S(2)}) %collective-permute-start.1) | collective-permute-done | bytes 32800 | tf_op jit(solution)/shard_map/ppermute | solution.py:270
  7.9 0.3 %collective-permute-done.2.refs_2_ = bf16[128,128]{1,0:T(8,128)(2,1)S(1)} collective-permute-done((bf16[128,128]{1,0:T(8,128)(2,1)}, bf16[128,128]{1,0:T(8,128)(2,1)S(1)}, u32[]{:S(2)}, u32[]{:S(2)}) %collective-permute-start.2) | collective-permute-done | bytes 32800 | tf_op jit(solution)/shard_map/ppermute | solution.py:270
  8.3 0.0 collective-permute-done.3.refs_3_
  8.3 1.2 %shard_map.146.refs_1_ = bf16[128,128]{1,0:T(8,128)(2,1)S(1)} custom-call(bf16[128,128]{1,0:T(8,128)(2,1)S(1)} %collective-permute-done.refs_0_, bf16[128,128]{1,0:T(8,128)(2,1)S(1)} %collective-permute-done.1.refs_1_, bf16[128,128]{1,0:T(8,128)(2,1)S(1)} %collective-permute-done.2.refs_2_, bf16[128,128]{1,0:T(8,128)(2,1)S(1)} %collective-permute-done.3.refs_3_, ...), custom_call_target="tpu_custom_call" | custom-call | tf_op jit(solution)/shard_map/pallas_call | solution.py:247
  9.5 1.9 %collective-permute-start.5 = (bf16[128,128]{1,0:T(8,128)(2,1)S(1)}, bf16[128,128]{1,0:T(8,128)(2,1)S(1)}, u32[]{:S(2)}, u32[]{:S(2)}) collective-permute-start(bf16[128,128]{1,0:T(8,128)(2,1)S(1)} %shard_map.146.refs_1_), channel_id=1, source_target_pairs={{0,12},{1,13},{2,14},{3,15},{4,8},{5,9},{6,10},{7,11},{8,20},{9,21... | collective-permute-start | bytes 98312 | tf_op jit(solution)/shard_map/ppermute | solution.py:270
  11.4 1.0 %collective-permute-start.6 = (bf16[128,128]{1,0:T(8,128)(2,1)S(1)}, bf16[128,128]{1,0:T(8,128)(2,1)S(1)}, u32[]{:S(2)}, u32[]{:S(2)}) collective-permute-start(bf16[128,128]{1,0:T(8,128)(2,1)S(1)} %shard_map.146.refs_1_), channel_id=1, source_target_pairs={{0,28},{1,29},{2,30},{3,31},{4,24},{5,25},{6,26},{7,27},{8,4},{9,5... | collective-permute-start | bytes 98312 | tf_op jit(solution)/shard_map/ppermute | solution.py:270
  12.4 1.7 %collective-permute-start.7 = (bf16[128,128]{1,0:T(8,128)(2,1)S(1)}, bf16[128,128]{1,0:T(8,128)(2,1)S(1)}, u32[]{:S(2)}, u32[]{:S(2)}) collective-permute-start(bf16[128,128]{1,0:T(8,128)(2,1)S(1)} %shard_map.146.refs_1_), channel_id=1, source_target_pairs={{0,20},{1,21},{2,22},{3,23},{4,16},{5,17},{6,18},{7,19},{8,28},{9,... | collective-permute-start | bytes 98312 | tf_op jit(solution)/shard_map/ppermute | solution.py:270
  14.1 0.3 %collective-permute-start.4 = (bf16[128,128]{1,0:T(8,128)(2,1)S(1)}, bf16[128,128]{1,0:T(8,128)(2,1)S(1)}, u32[]{:S(2)}, u32[]{:S(2)}) collective-permute-start(bf16[128,128]{1,0:T(8,128)(2,1)S(1)} %shard_map.146.refs_1_), channel_id=1, source_target_pairs={{0,4},{1,5},{2,6},{3,7},{4,0},{5,1},{6,2},{7,3},{8,12},{9,13},{10,... | collective-permute-start | bytes 98312 | tf_op jit(solution)/shard_map/ppermute | solution.py:270
  14.3 0.0 collective-permute-done.5.refs_2_
  14.3 0.3 %collective-permute-start.8 = (bf16[128,128]{1,0:T(8,128)(2,1)S(1)}, bf16[128,128]{1,0:T(8,128)(2,1)S(1)}, u32[]{:S(2)}, u32[]{:S(2)}) collective-permute-start(bf16[128,128]{1,0:T(8,128)(2,1)S(1)} %collective-permute-done.5.refs_2_), channel_id=1, source_target_pairs={{0,4},{1,5},{2,6},{3,7},{4,0},{5,1},{6,2},{7,3},{8,12},{9,13},{10,... | collective-permute-start | bytes 98312 | tf_op jit(solution)/shard_map/ppermute | solution.py:270
  14.6 0.5 %collective-permute-done.6.refs_3_ = bf16[128,128]{1,0:T(8,128)(2,1)S(1)} collective-permute-done((bf16[128,128]{1,0:T(8,128)(2,1)S(1)}, bf16[128,128]{1,0:T(8,128)(2,1)S(1)}, u32[]{:S(2)}, u32[]{:S(2)}) %collective-permute-start.6) | collective-permute-done | bytes 32800 | tf_op jit(solution)/shard_map/ppermute | solution.py:270
  15.1 0.5 %collective-permute-start.9 = (bf16[128,128]{1,0:T(8,128)(2,1)S(1)}, bf16[128,128]{1,0:T(8,128)(2,1)S(1)}, u32[]{:S(2)}, u32[]{:S(2)}) collective-permute-start(bf16[128,128]{1,0:T(8,128)(2,1)S(1)} %collective-permute-done.6.refs_3_), channel_id=1, source_target_pairs={{0,4},{1,5},{2,6},{3,7},{4,0},{5,1},{6,2},{7,3},{8,12},{9,13},{10,... | collective-permute-start | bytes 98312 | tf_op jit(solution)/shard_map/ppermute | solution.py:270
  15.6 0.2 %collective-permute-done.7.refs_4_ = bf16[128,128]{1,0:T(8,128)(2,1)S(1)} collective-permute-done((bf16[128,128]{1,0:T(8,128)(2,1)S(1)}, bf16[128,128]{1,0:T(8,128)(2,1)S(1)}, u32[]{:S(2)}, u32[]{:S(2)}) %collective-permute-start.7) | collective-permute-done | bytes 32800 | tf_op jit(solution)/shard_map/ppermute | solution.py:270
  15.8 0.4 %collective-permute-start.10 = (bf16[128,128]{1,0:T(8,128)(2,1)S(1)}, bf16[128,128]{1,0:T(8,128)(2,1)S(1)}, u32[]{:S(2)}, u32[]{:S(2)}) collective-permute-start(bf16[128,128]{1,0:T(8,128)(2,1)S(1)} %collective-permute-done.7.refs_4_), channel_id=1, source_target_pairs={{0,4},{1,5},{2,6},{3,7},{4,0},{5,1},{6,2},{7,3},{8,12},{9,13},{10,... | collective-permute-start | bytes 98312 | tf_op jit(solution)/shard_map/ppermute | solution.py:270
  16.2 0.0 collective-permute-done.4.refs_0_
  16.2 0.0 collective-permute-done.8.refs_5_
  16.2 0.2 %collective-permute-done.9.refs_6_ = bf16[128,128]{1,0:T(8,128)(2,1)S(1)} collective-permute-done((bf16[128,128]{1,0:T(8,128)(2,1)S(1)}, bf16[128,128]{1,0:T(8,128)(2,1)S(1)}, u32[]{:S(2)}, u32[]{:S(2)}) %collective-permute-start.9) | collective-permute-done | bytes 32800 | tf_op jit(solution)/shard_map/ppermute | solution.py:270
  16.4 0.6 %shard_map.147 = (bf16[128,128]{1,0:T(8,128)(2,1)S(1)}, f32[128,128]{1,0:T(8,128)S(1)}, bf16[896,256]{1,0:T(8,128)(2,1)S(1)}) custom-call(bf16[128,128]{1,0:T(8,128)(2,1)S(1)} %collective-permute-done.4.refs_0_, bf16[128,128]{1,0:T(8,128)(2,1)S(1)} %shard_map.146.refs_1_, bf16[128,128]{1,0:T(8,128)(2,1)S(1)} %collective-permute-done.5.refs_2_, ...), custom_call_target="tpu_custom_call" | custom-call | tf_op jit(solution)/shard_map/pallas_call | solution.py:227
  17.0 0.1 collective-permute-done.10.refs_4_
  17.1 1.6 %shard_map.148 = bf16[128,128]{1,0:T(8,128)(2,1)} custom-call(bf16[128,128]{1,0:T(8,128)(2,1)S(1)} %collective-permute-done.4.refs_0_, bf16[128,128]{1,0:T(8,128)(2,1)S(1)} %get-tuple-element.19.refs_1_, f32[128,128]{1,0:T(8,128)S(1)} %get-tuple-element.20.refs_2_, bf16[896,256]{1,0:T(8,128)(2,1)S(1)} %get-tuple-element.21.refs_3_, ...), custom_call_target="tpu_custom_call" | custom-call | tf_op jit(solution)/shard_map/pallas_call | solution.py:247
Async XLA Ops:
  0.0 7.7 %collective-permute-start = (bf16[128,128]{1,0:T(8,128)(2,1)}, bf16[128,128]{1,0:T(8,128)(2,1)S(1)}, u32[]{:S(2)}, u32[]{:S(2)}) collective-permute-start(bf16[128,128]{1,0:T(8,128)(2,1)} %bitcast.4), channel_id=1, source_target_pairs={{0,6},{1,7},{2,5},{3,4},{4,2},{5,3},{6,1},{7,0},{8,14},{9,15},{10,... | collective-permute-start | bytes 98312 | tf_op jit(solution)/shard_map/ppermute | solution.py:270
  3.5 4.5 %collective-permute-start.1 = (bf16[128,128]{1,0:T(8,128)(2,1)}, bf16[128,128]{1,0:T(8,128)(2,1)S(1)}, u32[]{:S(2)}, u32[]{:S(2)}) collective-permute-start(bf16[128,128]{1,0:T(8,128)(2,1)} %bitcast.5), channel_id=1, source_target_pairs={{0,7},{1,6},{2,4},{3,5},{4,3},{5,2},{6,0},{7,1},{8,15},{9,14},{10,... | collective-permute-start | bytes 98312 | tf_op jit(solution)/shard_map/ppermute | solution.py:270
  4.5 3.8 %collective-permute-start.2 = (bf16[128,128]{1,0:T(8,128)(2,1)}, bf16[128,128]{1,0:T(8,128)(2,1)S(1)}, u32[]{:S(2)}, u32[]{:S(2)}) collective-permute-start(bf16[128,128]{1,0:T(8,128)(2,1)} %bitcast.6), channel_id=1, source_target_pairs={{0,5},{1,4},{2,7},{3,6},{4,1},{5,0},{6,3},{7,2},{8,13},{9,12},{10,... | collective-permute-start | bytes 98312 | tf_op jit(solution)/shard_map/ppermute | solution.py:270
  5.3 2.9 %collective-permute-start.3 = (bf16[128,128]{1,0:T(8,128)(2,1)}, bf16[128,128]{1,0:T(8,128)(2,1)S(1)}, u32[]{:S(2)}, u32[]{:S(2)}) collective-permute-start(bf16[128,128]{1,0:T(8,128)(2,1)} %bitcast.7), channel_id=1, source_target_pairs={{0,4},{1,5},{2,6},{3,7},{4,0},{5,1},{6,2},{7,3},{8,12},{9,13},{10,... | collective-permute-start | bytes 98312 | tf_op jit(solution)/shard_map/ppermute | solution.py:270
  6.0 0.7 %copy-start = (s32[64]{0:T(128)S(1)}, s32[64]{0:T(128)}, u32[]{:S(2)}) copy-start(s32[64]{0:T(128)} %param.16) | copy-start | bytes 772
  9.5 4.9 %collective-permute-start.5 = (bf16[128,128]{1,0:T(8,128)(2,1)S(1)}, bf16[128,128]{1,0:T(8,128)(2,1)S(1)}, u32[]{:S(2)}, u32[]{:S(2)}) collective-permute-start(bf16[128,128]{1,0:T(8,128)(2,1)S(1)} %shard_map.146.refs_1_), channel_id=1, source_target_pairs={{0,12},{1,13},{2,14},{3,15},{4,8},{5,9},{6,10},{7,11},{8,20},{9,21... | collective-permute-start | bytes 98312 | tf_op jit(solution)/shard_map/ppermute | solution.py:270
  11.4 3.6 %collective-permute-start.6 = (bf16[128,128]{1,0:T(8,128)(2,1)S(1)}, bf16[128,128]{1,0:T(8,128)(2,1)S(1)}, u32[]{:S(2)}, u32[]{:S(2)}) collective-permute-start(bf16[128,128]{1,0:T(8,128)(2,1)S(1)} %shard_map.146.refs_1_), channel_id=1, source_target_pairs={{0,28},{1,29},{2,30},{3,31},{4,24},{5,25},{6,26},{7,27},{8,4},{9,5... | collective-permute-start | bytes 98312 | tf_op jit(solution)/shard_map/ppermute | solution.py:270
  12.4 3.3 %collective-permute-start.7 = (bf16[128,128]{1,0:T(8,128)(2,1)S(1)}, bf16[128,128]{1,0:T(8,128)(2,1)S(1)}, u32[]{:S(2)}, u32[]{:S(2)}) collective-permute-start(bf16[128,128]{1,0:T(8,128)(2,1)S(1)} %shard_map.146.refs_1_), channel_id=1, source_target_pairs={{0,20},{1,21},{2,22},{3,23},{4,16},{5,17},{6,18},{7,19},{8,28},{9,... | collective-permute-start | bytes 98312 | tf_op jit(solution)/shard_map/ppermute | solution.py:270
  14.1 2.1 %collective-permute-start.4 = (bf16[128,128]{1,0:T(8,128)(2,1)S(1)}, bf16[128,128]{1,0:T(8,128)(2,1)S(1)}, u32[]{:S(2)}, u32[]{:S(2)}) collective-permute-start(bf16[128,128]{1,0:T(8,128)(2,1)S(1)} %shard_map.146.refs_1_), channel_id=1, source_target_pairs={{0,4},{1,5},{2,6},{3,7},{4,0},{5,1},{6,2},{7,3},{8,12},{9,13},{10,... | collective-permute-start | bytes 98312 | tf_op jit(solution)/shard_map/ppermute | solution.py:270
  14.3 1.9 %collective-permute-start.8 = (bf16[128,128]{1,0:T(8,128)(2,1)S(1)}, bf16[128,128]{1,0:T(8,128)(2,1)S(1)}, u32[]{:S(2)}, u32[]{:S(2)}) collective-permute-start(bf16[128,128]{1,0:T(8,128)(2,1)S(1)} %collective-permute-done.5.refs_2_), channel_id=1, source_target_pairs={{0,4},{1,5},{2,6},{3,7},{4,0},{5,1},{6,2},{7,3},{8,12},{9,13},{10,... | collective-permute-start | bytes 98312 | tf_op jit(solution)/shard_map/ppermute | solution.py:270
  15.1 1.4 %collective-permute-start.9 = (bf16[128,128]{1,0:T(8,128)(2,1)S(1)}, bf16[128,128]{1,0:T(8,128)(2,1)S(1)}, u32[]{:S(2)}, u32[]{:S(2)}) collective-permute-start(bf16[128,128]{1,0:T(8,128)(2,1)S(1)} %collective-permute-done.6.refs_3_), channel_id=1, source_target_pairs={{0,4},{1,5},{2,6},{3,7},{4,0},{5,1},{6,2},{7,3},{8,12},{9,13},{10,... | collective-permute-start | bytes 98312 | tf_op jit(solution)/shard_map/ppermute | solution.py:270
  15.8 1.3 %collective-permute-start.10 = (bf16[128,128]{1,0:T(8,128)(2,1)S(1)}, bf16[128,128]{1,0:T(8,128)(2,1)S(1)}, u32[]{:S(2)}, u32[]{:S(2)}) collective-permute-start(bf16[128,128]{1,0:T(8,128)(2,1)S(1)} %collective-permute-done.7.refs_4_), channel_id=1, source_target_pairs={{0,4},{1,5},{2,6},{3,7},{4,0},{5,1},{6,2},{7,3},{8,12},{9,13},{10,... | collective-permute-start | bytes 98312 | tf_op jit(solution)/shard_map/ppermute | solution.py:270

commit v6 on v5

--- a/solution.py
+++ b/solution.py
@@ -108,9 +108,12 @@
 
 def keys_and_values(normed, weight_ref):
     channels = weight_ref.shape[0]
-    return jnp.dot(
-        normed, weight_ref[:, 2 * channels : 4 * channels], preferred_element_type=jnp.float32
-    ).astype(jnp.bfloat16)
+    return tuple(
+        jnp.dot(
+            normed, weight_ref[:, w * channels : (w + 1) * channels], preferred_element_type=jnp.float32
+        ).astype(jnp.bfloat16)
+        for w in (2, 3)
+    )
 
 
 def queries_and_gate(normed, weight_ref, gate_bias_ref):
@@ -120,25 +123,25 @@
 
 
 def project_kernel(own, *refs):
-    *block_refs, weight_ref, gate_bias_ref, query_ref, gate_ref, product_ref = refs
+    *block_refs, weight_ref, gate_bias_ref, query_ref, gate_ref, key_ref, value_ref = refs
     rows = query_ref.shape[0]
     normed = normalize(jnp.concatenate([ref[...] for ref in block_refs], 0))
     queries, gate_ref[...] = queries_and_gate(
         normed[own * rows : (own + 1) * rows], weight_ref, gate_bias_ref
     )
     query_ref[...] = queries.astype(jnp.bfloat16)
-    product_ref[...] = keys_and_values(normed, weight_ref)
+    key_ref[...], value_ref[...] = keys_and_values(normed, weight_ref)
 
 
 def attend_kernel(split, own, items, pack, group, *refs):
     weight_ref, gate_bias_ref, bias_ref, out_ref, turned_ref = refs[-5:]
     rows, channels = out_ref.shape
     if split:
-        own_ref, query_ref, gate_ref, product_ref, *late_refs = refs[:-5]
+        own_ref, query_ref, gate_ref, key_ref, value_ref, *late_refs = refs[:-5]
     else:
         late_refs = refs[:-5]
         own_ref = late_refs[own]
-    early = product_ref.shape[0] // rows if split else 0
+    early = key_ref.shape[0] // rows if split else 0
     head_size = channels // H
     part = rows // items
     step_rows, pack_rows = group * part, pack * part
@@ -159,14 +162,21 @@
             queries, gate = queries_and_gate(
                 normed[own * step_rows : (own + 1) * step_rows], weight_ref, gate_bias_ref
             )
-        late = keys_and_values(normed, weight_ref)
-        products = [product_ref[pl.ds(b * rows + start, step_rows)] for b in range(early)]
-        products += [late[b * step_rows : (b + 1) * step_rows] for b in range(len(late_refs))]
+        late_keys, late_values = keys_and_values(normed, weight_ref)
         packs = range(group // pack)
-        held = [
-            jnp.concatenate([p[i * pack_rows : (i + 1) * pack_rows] for p in products], 0)
-            for i in packs
-        ]
+
+        def by_pack(early_ref, late):
+            products = [early_ref[pl.ds(b * rows + start, step_rows)] for b in range(early)]
+            products += [
+                late[b * step_rows : (b + 1) * step_rows] for b in range(len(late_refs))
+            ]
+            return [
+                jnp.concatenate([p[i * pack_rows : (i + 1) * pack_rows] for p in products], 0)
+                for i in packs
+            ]
+
+        keys = by_pack(key_ref if split else None, late_keys)
+        values = by_pack(value_ref if split else None, late_values)
         scores = []
         for i in packs:
             query = queries[i * pack_rows : (i + 1) * pack_rows]
@@ -174,7 +184,7 @@
             scores.append(
                 lax.dot_general(
                     stacked.astype(jnp.bfloat16),
-                    held[i][:, :channels],
+                    keys[i],
                     (((1,), (1,)), ((), ())),
                     preferred_element_type=jnp.float32,
                 )
@@ -183,14 +193,12 @@
             )
         scores = jnp.concatenate(scores, 0)
         expanded = jnp.exp2(scores - jnp.max(scores, axis=1, keepdims=True))
-        weights = (expanded * (1.0 / jnp.sum(expanded, axis=1, keepdims=True))).astype(jnp.bfloat16)
+        share = 1.0 / jnp.sum(expanded, axis=1, keepdims=True)
+        weights = expanded.astype(jnp.bfloat16)
         attended = []
         for i in packs:
-            heads = jnp.dot(
-                weights[i * H * pack_rows : (i + 1) * H * pack_rows],
-                held[i][:, channels:],
-                preferred_element_type=jnp.float32,
-            )
+            at = slice(i * H * pack_rows, (i + 1) * H * pack_rows)
+            heads = jnp.dot(weights[at], values[i], preferred_element_type=jnp.float32) * share[at]
             picked = heads[:pack_rows]
             for h in range(1, H):
                 picked = jnp.where(
@@ -229,10 +237,11 @@
         out_shape=(
             jax.ShapeDtypeStruct((rows, channels), jnp.bfloat16),
             jax.ShapeDtypeStruct((rows, channels), jnp.float32),
-            jax.ShapeDtypeStruct((len(blocks) * rows, 2 * channels), jnp.bfloat16),
+            jax.ShapeDtypeStruct((len(blocks) * rows, channels), jnp.bfloat16),
+            jax.ShapeDtypeStruct((len(blocks) * rows, channels), jnp.bfloat16),
         ),
         in_specs=[vmem] * (len(blocks) + 2),
-        out_specs=(vmem,) * 3,
+        out_specs=(vmem,) * 4,
         compiler_params=pltpu.CompilerParams(
             vmem_limit_bytes=8 * len(blocks) * rows * channels + 16 * 2**20
         ),

time: 18.9 us -> 18.7 us (0.989)
  Pallas kernels: 4.41 us -> 4.16 us
    pallas_call x2, Pallas kernels: 2.82 us -> 2.6 us  [attend(): pl.pallas_call(functools.partial(attend_kernel, bool(early), own, items,...]
where the time goes in v6:
time: 18.7 us; the launch traced here: 18.5 us
  starting transfers between devices  11.4 us (61%)
  Pallas kernels  4.16 us (22%)
  waiting for transfers between devices  1.58 us (8%)
  between operations  0.7 us (4%)
  local copies, waits for them, and re-layouts  0.65 us (3%)
    ppermute x11, starting transfers between devices, send(): return lax.ppermute(values, ('orig', 'dest'), pairs)  11.4 us
    pallas_call x2, Pallas kernels, attend(): pl.pallas_call(functools.partial(attend_kernel, bool(early), own, items,...  2.6 us
    ppermute x11, waiting for transfers between devices, send(): return lax.ppermute(values, ('orig', 'dest'), pairs)  1.58 us
    pallas_call x1, Pallas kernels, prepare(): pl.pallas_call(functools.partial(prepare_kernel, axes, sources, parts, pa...  1.04 us
    unnamed x2, local copies, waits for them, and re-layouts  0.65 us
    pallas_call x1, Pallas kernels, project(): pl.pallas_call(functools.partial(project_kernel, own), out_shape=(jax.Sha...  0.52 us
  transfers between devices with their start and end apart: 11, of which 6 were waited for; matrix products, arithmetic and copies ran while one was open for 0% of the time, Pallas kernels for 8%

profile of v6, /device:TPU:0, one launch (start us, length us, event | category | flops | bytes accessed | tf_op | source)
XLA Modules:
  0.0 18.5 jit_solution(1036622901935690619)
XLA Ops:
  0.0 3.5 %collective-permute-start = (bf16[128,128]{1,0:T(8,128)(2,1)}, bf16[128,128]{1,0:T(8,128)(2,1)S(1)}, u32[]{:S(2)}, u32[]{:S(2)}) collective-permute-start(bf16[128,128]{1,0:T(8,128)(2,1)} %bitcast.4), channel_id=1, source_target_pairs={{0,6},{1,7},{2,5},{3,4},{4,2},{5,3},{6,1},{7,0},{8,14},{9,15},{10,... | collective-permute-start | bytes 98312 | tf_op jit(solution)/shard_map/ppermute | solution.py:279
  3.5 1.0 %collective-permute-start.1 = (bf16[128,128]{1,0:T(8,128)(2,1)}, bf16[128,128]{1,0:T(8,128)(2,1)S(1)}, u32[]{:S(2)}, u32[]{:S(2)}) collective-permute-start(bf16[128,128]{1,0:T(8,128)(2,1)} %bitcast.5), channel_id=1, source_target_pairs={{0,7},{1,6},{2,4},{3,5},{4,3},{5,2},{6,0},{7,1},{8,15},{9,14},{10,... | collective-permute-start | bytes 98312 | tf_op jit(solution)/shard_map/ppermute | solution.py:279
  4.5 0.8 %collective-permute-start.2 = (bf16[128,128]{1,0:T(8,128)(2,1)}, bf16[128,128]{1,0:T(8,128)(2,1)S(1)}, u32[]{:S(2)}, u32[]{:S(2)}) collective-permute-start(bf16[128,128]{1,0:T(8,128)(2,1)} %bitcast.6), channel_id=1, source_target_pairs={{0,5},{1,4},{2,7},{3,6},{4,1},{5,0},{6,3},{7,2},{8,13},{9,12},{10,... | collective-permute-start | bytes 98312 | tf_op jit(solution)/shard_map/ppermute | solution.py:279
  5.3 0.0 collective-permute-start.3
  6.0 0.0 copy-start
  6.0 0.6 %copy-done = s32[64]{0:T(128)S(1)} copy-done((s32[64]{0:T(128)S(1)}, s32[64]{0:T(128)}, u32[]{:S(2)}) %copy-start) | copy-done | bytes 280
  6.6 1.0 %shard_map.145 = (bf16[128,640]{1,0:T(8,128)(2,1)S(1)}, f32[1,128]{1,0:T(1,128)S(1)}, f32[1,128]{1,0:T(1,128)S(1)}, bf16[128,640]{1,0:T(8,128)(2,1)S(1)}, f32[1,128]{1,0:T(1,128)S(1)}, /*index=5*/f32[1,128]{1,0:T(1,128)S(1)}) custom-call(s32[1,64]{1,0:T(1,128)S(1)} %bitcast.3, s32[1]{0:T(128)S(6)} %copy.16.count_ref, bf16[1,128,128]{2,1,0:T(8,128)(2,1)} %refs_0_.1, ...), custom_call_target="tpu_custom_call" | custom-call | flops 1048576 | bytes 1048576 | tf_op jit(solution)/shard_map/pallas_call | solution.py:84
  7.7 0.0 collective-permute-done.refs_0_
  7.7 0.2 %collective-permute-done.1.refs_1_ = bf16[128,128]{1,0:T(8,128)(2,1)S(1)} collective-permute-done((bf16[128,128]{1,0:T(8,128)(2,1)}, bf16[128,128]{1,0:T(8,128)(2,1)S(1)}, u32[]{:S(2)}, u32[]{:S(2)}) %collective-permute-start.1) | collective-permute-done | bytes 32800 | tf_op jit(solution)/shard_map/ppermute | solution.py:279
  7.9 0.3 %collective-permute-done.2.refs_2_ = bf16[128,128]{1,0:T(8,128)(2,1)S(1)} collective-permute-done((bf16[128,128]{1,0:T(8,128)(2,1)}, bf16[128,128]{1,0:T(8,128)(2,1)S(1)}, u32[]{:S(2)}, u32[]{:S(2)}) %collective-permute-start.2) | collective-permute-done | bytes 32800 | tf_op jit(solution)/shard_map/ppermute | solution.py:279
  8.3 0.0 collective-permute-done.3.refs_3_
  8.3 1.0 %shard_map.146.refs_1_ = bf16[128,128]{1,0:T(8,128)(2,1)S(1)} custom-call(bf16[128,128]{1,0:T(8,128)(2,1)S(1)} %collective-permute-done.refs_0_, bf16[128,128]{1,0:T(8,128)(2,1)S(1)} %collective-permute-done.1.refs_1_, bf16[128,128]{1,0:T(8,128)(2,1)S(1)} %collective-permute-done.2.refs_2_, bf16[128,128]{1,0:T(8,128)(2,1)S(1)} %collective-permute-done.3.refs_3_, ...), custom_call_target="tpu_custom_call" | custom-call | tf_op jit(solution)/shard_map/pallas_call | solution.py:256
  9.3 1.9 %collective-permute-start.5 = (bf16[128,128]{1,0:T(8,128)(2,1)S(1)}, bf16[128,128]{1,0:T(8,128)(2,1)S(1)}, u32[]{:S(2)}, u32[]{:S(2)}) collective-permute-start(bf16[128,128]{1,0:T(8,128)(2,1)S(1)} %shard_map.146.refs_1_), channel_id=1, source_target_pairs={{0,12},{1,13},{2,14},{3,15},{4,8},{5,9},{6,10},{7,11},{8,20},{9,21... | collective-permute-start | bytes 98312 | tf_op jit(solution)/shard_map/ppermute | solution.py:279
  11.2 1.0 %collective-permute-start.6 = (bf16[128,128]{1,0:T(8,128)(2,1)S(1)}, bf16[128,128]{1,0:T(8,128)(2,1)S(1)}, u32[]{:S(2)}, u32[]{:S(2)}) collective-permute-start(bf16[128,128]{1,0:T(8,128)(2,1)S(1)} %shard_map.146.refs_1_), channel_id=1, source_target_pairs={{0,28},{1,29},{2,30},{3,31},{4,24},{5,25},{6,26},{7,27},{8,4},{9,5... | collective-permute-start | bytes 98312 | tf_op jit(solution)/shard_map/ppermute | solution.py:279
  12.3 1.7 %collective-permute-start.7 = (bf16[128,128]{1,0:T(8,128)(2,1)S(1)}, bf16[128,128]{1,0:T(8,128)(2,1)S(1)}, u32[]{:S(2)}, u32[]{:S(2)}) collective-permute-start(bf16[128,128]{1,0:T(8,128)(2,1)S(1)} %shard_map.146.refs_1_), channel_id=1, source_target_pairs={{0,20},{1,21},{2,22},{3,23},{4,16},{5,17},{6,18},{7,19},{8,28},{9,... | collective-permute-start | bytes 98312 | tf_op jit(solution)/shard_map/ppermute | solution.py:279
  13.9 0.3 %collective-permute-start.4 = (bf16[128,128]{1,0:T(8,128)(2,1)S(1)}, bf16[128,128]{1,0:T(8,128)(2,1)S(1)}, u32[]{:S(2)}, u32[]{:S(2)}) collective-permute-start(bf16[128,128]{1,0:T(8,128)(2,1)S(1)} %shard_map.146.refs_1_), channel_id=1, source_target_pairs={{0,4},{1,5},{2,6},{3,7},{4,0},{5,1},{6,2},{7,3},{8,12},{9,13},{10,... | collective-permute-start | bytes 98312 | tf_op jit(solution)/shard_map/ppermute | solution.py:279
  14.2 0.0 collective-permute-done.5.refs_2_
  14.2 0.3 %collective-permute-start.8 = (bf16[128,128]{1,0:T(8,128)(2,1)S(1)}, bf16[128,128]{1,0:T(8,128)(2,1)S(1)}, u32[]{:S(2)}, u32[]{:S(2)}) collective-permute-start(bf16[128,128]{1,0:T(8,128)(2,1)S(1)} %collective-permute-done.5.refs_2_), channel_id=1, source_target_pairs={{0,4},{1,5},{2,6},{3,7},{4,0},{5,1},{6,2},{7,3},{8,12},{9,13},{10,... | collective-permute-start | bytes 98312 | tf_op jit(solution)/shard_map/ppermute | solution.py:279
  14.4 0.5 %collective-permute-done.6.refs_3_ = bf16[128,128]{1,0:T(8,128)(2,1)S(1)} collective-permute-done((bf16[128,128]{1,0:T(8,128)(2,1)S(1)}, bf16[128,128]{1,0:T(8,128)(2,1)S(1)}, u32[]{:S(2)}, u32[]{:S(2)}) %collective-permute-start.6) | collective-permute-done | bytes 32800 | tf_op jit(solution)/shard_map/ppermute | solution.py:279
  14.9 0.5 %collective-permute-start.9 = (bf16[128,128]{1,0:T(8,128)(2,1)S(1)}, bf16[128,128]{1,0:T(8,128)(2,1)S(1)}, u32[]{:S(2)}, u32[]{:S(2)}) collective-permute-start(bf16[128,128]{1,0:T(8,128)(2,1)S(1)} %collective-permute-done.6.refs_3_), channel_id=1, source_target_pairs={{0,4},{1,5},{2,6},{3,7},{4,0},{5,1},{6,2},{7,3},{8,12},{9,13},{10,... | collective-permute-start | bytes 98312 | tf_op jit(solution)/shard_map/ppermute | solution.py:279
  15.4 0.2 %collective-permute-done.7.refs_4_ = bf16[128,128]{1,0:T(8,128)(2,1)S(1)} collective-permute-done((bf16[128,128]{1,0:T(8,128)(2,1)S(1)}, bf16[128,128]{1,0:T(8,128)(2,1)S(1)}, u32[]{:S(2)}, u32[]{:S(2)}) %collective-permute-start.7) | collective-permute-done | bytes 32800 | tf_op jit(solution)/shard_map/ppermute | solution.py:279
  15.6 0.4 %collective-permute-start.10 = (bf16[128,128]{1,0:T(8,128)(2,1)S(1)}, bf16[128,128]{1,0:T(8,128)(2,1)S(1)}, u32[]{:S(2)}, u32[]{:S(2)}) collective-permute-start(bf16[128,128]{1,0:T(8,128)(2,1)S(1)} %collective-permute-done.7.refs_4_), channel_id=1, source_target_pairs={{0,4},{1,5},{2,6},{3,7},{4,0},{5,1},{6,2},{7,3},{8,12},{9,13},{10,... | collective-permute-start | bytes 98312 | tf_op jit(solution)/shard_map/ppermute | solution.py:279
  16.0 0.0 collective-permute-done.4.refs_0_
  16.0 0.0 collective-permute-done.8.refs_5_
  16.0 0.2 %collective-permute-done.9.refs_6_ = bf16[128,128]{1,0:T(8,128)(2,1)S(1)} collective-permute-done((bf16[128,128]{1,0:T(8,128)(2,1)S(1)}, bf16[128,128]{1,0:T(8,128)(2,1)S(1)}, u32[]{:S(2)}, u32[]{:S(2)}) %collective-permute-start.9) | collective-permute-done | bytes 32800 | tf_op jit(solution)/shard_map/ppermute | solution.py:279
  16.3 0.5 %shard_map.147 = (bf16[128,128]{1,0:T(8,128)(2,1)S(1)}, f32[128,128]{1,0:T(8,128)S(1)}, bf16[896,128]{1,0:T(8,128)(2,1)S(1)}, bf16[896,128]{1,0:T(8,128)(2,1)S(1)}) custom-call(bf16[128,128]{1,0:T(8,128)(2,1)S(1)} %collective-permute-done.4.refs_0_, bf16[128,128]{1,0:T(8,128)(2,1)S(1)} %shard_map.146.refs_1_, ...), custom_call_target="tpu_custom_call" | custom-call | tf_op jit(solution)/shard_map/pallas_call | solution.py:235
  16.8 0.1 collective-permute-done.10.refs_5_
  16.9 1.6 %shard_map.148 = bf16[128,128]{1,0:T(8,128)(2,1)} custom-call(bf16[128,128]{1,0:T(8,128)(2,1)S(1)} %collective-permute-done.4.refs_0_, bf16[128,128]{1,0:T(8,128)(2,1)S(1)} %get-tuple-element.20.refs_1_, f32[128,128]{1,0:T(8,128)S(1)} %get-tuple-element.21.refs_2_, bf16[896,128]{1,0:T(8,128)(2,1)S(1)} %get-tuple-element.22.refs_3_, ...), custom_call_target="tpu_custom_call" | custom-call | tf_op jit(solution)/shard_map/pallas_call | solution.py:256
Async XLA Ops:
  0.0 7.7 %collective-permute-start = (bf16[128,128]{1,0:T(8,128)(2,1)}, bf16[128,128]{1,0:T(8,128)(2,1)S(1)}, u32[]{:S(2)}, u32[]{:S(2)}) collective-permute-start(bf16[128,128]{1,0:T(8,128)(2,1)} %bitcast.4), channel_id=1, source_target_pairs={{0,6},{1,7},{2,5},{3,4},{4,2},{5,3},{6,1},{7,0},{8,14},{9,15},{10,... | collective-permute-start | bytes 98312 | tf_op jit(solution)/shard_map/ppermute | solution.py:279
  3.5 4.5 %collective-permute-start.1 = (bf16[128,128]{1,0:T(8,128)(2,1)}, bf16[128,128]{1,0:T(8,128)(2,1)S(1)}, u32[]{:S(2)}, u32[]{:S(2)}) collective-permute-start(bf16[128,128]{1,0:T(8,128)(2,1)} %bitcast.5), channel_id=1, source_target_pairs={{0,7},{1,6},{2,4},{3,5},{4,3},{5,2},{6,0},{7,1},{8,15},{9,14},{10,... | collective-permute-start | bytes 98312 | tf_op jit(solution)/shard_map/ppermute | solution.py:279
  4.5 3.8 %collective-permute-start.2 = (bf16[128,128]{1,0:T(8,128)(2,1)}, bf16[128,128]{1,0:T(8,128)(2,1)S(1)}, u32[]{:S(2)}, u32[]{:S(2)}) collective-permute-start(bf16[128,128]{1,0:T(8,128)(2,1)} %bitcast.6), channel_id=1, source_target_pairs={{0,5},{1,4},{2,7},{3,6},{4,1},{5,0},{6,3},{7,2},{8,13},{9,12},{10,... | collective-permute-start | bytes 98312 | tf_op jit(solution)/shard_map/ppermute | solution.py:279
  5.3 2.9 %collective-permute-start.3 = (bf16[128,128]{1,0:T(8,128)(2,1)}, bf16[128,128]{1,0:T(8,128)(2,1)S(1)}, u32[]{:S(2)}, u32[]{:S(2)}) collective-permute-start(bf16[128,128]{1,0:T(8,128)(2,1)} %bitcast.7), channel_id=1, source_target_pairs={{0,4},{1,5},{2,6},{3,7},{4,0},{5,1},{6,2},{7,3},{8,12},{9,13},{10,... | collective-permute-start | bytes 98312 | tf_op jit(solution)/shard_map/ppermute | solution.py:279
  6.0 0.7 %copy-start = (s32[64]{0:T(128)S(1)}, s32[64]{0:T(128)}, u32[]{:S(2)}) copy-start(s32[64]{0:T(128)} %param.16) | copy-start | bytes 772
  9.3 4.9 %collective-permute-start.5 = (bf16[128,128]{1,0:T(8,128)(2,1)S(1)}, bf16[128,128]{1,0:T(8,128)(2,1)S(1)}, u32[]{:S(2)}, u32[]{:S(2)}) collective-permute-start(bf16[128,128]{1,0:T(8,128)(2,1)S(1)} %shard_map.146.refs_1_), channel_id=1, source_target_pairs={{0,12},{1,13},{2,14},{3,15},{4,8},{5,9},{6,10},{7,11},{8,20},{9,21... | collective-permute-start | bytes 98312 | tf_op jit(solution)/shard_map/ppermute | solution.py:279
  11.2 3.7 %collective-permute-start.6 = (bf16[128,128]{1,0:T(8,128)(2,1)S(1)}, bf16[128,128]{1,0:T(8,128)(2,1)S(1)}, u32[]{:S(2)}, u32[]{:S(2)}) collective-permute-start(bf16[128,128]{1,0:T(8,128)(2,1)S(1)} %shard_map.146.refs_1_), channel_id=1, source_target_pairs={{0,28},{1,29},{2,30},{3,31},{4,24},{5,25},{6,26},{7,27},{8,4},{9,5... | collective-permute-start | bytes 98312 | tf_op jit(solution)/shard_map/ppermute | solution.py:279
  12.3 3.3 %collective-permute-start.7 = (bf16[128,128]{1,0:T(8,128)(2,1)S(1)}, bf16[128,128]{1,0:T(8,128)(2,1)S(1)}, u32[]{:S(2)}, u32[]{:S(2)}) collective-permute-start(bf16[128,128]{1,0:T(8,128)(2,1)S(1)} %shard_map.146.refs_1_), channel_id=1, source_target_pairs={{0,20},{1,21},{2,22},{3,23},{4,16},{5,17},{6,18},{7,19},{8,28},{9,... | collective-permute-start | bytes 98312 | tf_op jit(solution)/shard_map/ppermute | solution.py:279
  13.9 2.1 %collective-permute-start.4 = (bf16[128,128]{1,0:T(8,128)(2,1)S(1)}, bf16[128,128]{1,0:T(8,128)(2,1)S(1)}, u32[]{:S(2)}, u32[]{:S(2)}) collective-permute-start(bf16[128,128]{1,0:T(8,128)(2,1)S(1)} %shard_map.146.refs_1_), channel_id=1, source_target_pairs={{0,4},{1,5},{2,6},{3,7},{4,0},{5,1},{6,2},{7,3},{8,12},{9,13},{10,... | collective-permute-start | bytes 98312 | tf_op jit(solution)/shard_map/ppermute | solution.py:279
  14.2 1.9 %collective-permute-start.8 = (bf16[128,128]{1,0:T(8,128)(2,1)S(1)}, bf16[128,128]{1,0:T(8,128)(2,1)S(1)}, u32[]{:S(2)}, u32[]{:S(2)}) collective-permute-start(bf16[128,128]{1,0:T(8,128)(2,1)S(1)} %collective-permute-done.5.refs_2_), channel_id=1, source_target_pairs={{0,4},{1,5},{2,6},{3,7},{4,0},{5,1},{6,2},{7,3},{8,12},{9,13},{10,... | collective-permute-start | bytes 98312 | tf_op jit(solution)/shard_map/ppermute | solution.py:279
  14.9 1.4 %collective-permute-start.9 = (bf16[128,128]{1,0:T(8,128)(2,1)S(1)}, bf16[128,128]{1,0:T(8,128)(2,1)S(1)}, u32[]{:S(2)}, u32[]{:S(2)}) collective-permute-start(bf16[128,128]{1,0:T(8,128)(2,1)S(1)} %collective-permute-done.6.refs_3_), channel_id=1, source_target_pairs={{0,4},{1,5},{2,6},{3,7},{4,0},{5,1},{6,2},{7,3},{8,12},{9,13},{10,... | collective-permute-start | bytes 98312 | tf_op jit(solution)/shard_map/ppermute | solution.py:279
  15.6 1.3 %collective-permute-start.10 = (bf16[128,128]{1,0:T(8,128)(2,1)S(1)}, bf16[128,128]{1,0:T(8,128)(2,1)S(1)}, u32[]{:S(2)}, u32[]{:S(2)}) collective-permute-start(bf16[128,128]{1,0:T(8,128)(2,1)S(1)} %collective-permute-done.7.refs_4_), channel_id=1, source_target_pairs={{0,4},{1,5},{2,6},{3,7},{4,0},{5,1},{6,2},{7,3},{8,12},{9,13},{10,... | collective-permute-start | bytes 98312 | tf_op jit(solution)/shard_map/ppermute | solution.py:279

commit v7 on v6

--- a/solution.py
+++ b/solution.py
@@ -193,12 +193,11 @@
             )
         scores = jnp.concatenate(scores, 0)
         expanded = jnp.exp2(scores - jnp.max(scores, axis=1, keepdims=True))
-        share = 1.0 / jnp.sum(expanded, axis=1, keepdims=True)
-        weights = expanded.astype(jnp.bfloat16)
+        weights = (expanded * (1.0 / jnp.sum(expanded, axis=1, keepdims=True))).astype(jnp.bfloat16)
         attended = []
         for i in packs:
             at = slice(i * H * pack_rows, (i + 1) * H * pack_rows)
-            heads = jnp.dot(weights[at], values[i], preferred_element_type=jnp.float32) * share[at]
+            heads = jnp.dot(weights[at], values[i], preferred_element_type=jnp.float32)
             picked = heads[:pack_rows]
             for h in range(1, H):
                 picked = jnp.where(

time: 18.7 us -> 18.9 us (1.011)
  no operation moved by 1% of the time
where the time goes in v7:
time: 18.9 us; the launch traced here: 18.6 us
  starting transfers between devices  11.4 us (60%)
  Pallas kernels  4.33 us (23%)
  waiting for transfers between devices  1.58 us (8%)
  between operations  0.7 us (4%)
  local copies, waits for them, and re-layouts  0.65 us (3%)
    ppermute x11, starting transfers between devices, send(): return lax.ppermute(values, ('orig', 'dest'), pairs)  11.4 us
    pallas_call x2, Pallas kernels, attend(): pl.pallas_call(functools.partial(attend_kernel, bool(early), own, items,...  2.77 us
    ppermute x11, waiting for transfers between devices, send(): return lax.ppermute(values, ('orig', 'dest'), pairs)  1.58 us
    pallas_call x1, Pallas kernels, prepare(): pl.pallas_call(functools.partial(prepare_kernel, axes, sources, parts, pa...  1.04 us
    unnamed x2, local copies, waits for them, and re-layouts  0.65 us
    pallas_call x1, Pallas kernels, project(): pl.pallas_call(functools.partial(project_kernel, own), out_shape=(jax.Sha...  0.52 us
  transfers between devices with their start and end apart: 11, of which 6 were waited for; matrix products, arithmetic and copies ran while one was open for 0% of the time, Pallas kernels for 8%

profile of v7, /device:TPU:0, one launch (start us, length us, event | category | flops | bytes accessed | tf_op | source)
XLA Modules:
  0.0 18.6 jit_solution(8839348992356747836)
XLA Ops:
  0.0 3.5 %collective-permute-start = (bf16[128,128]{1,0:T(8,128)(2,1)}, bf16[128,128]{1,0:T(8,128)(2,1)S(1)}, u32[]{:S(2)}, u32[]{:S(2)}) collective-permute-start(bf16[128,128]{1,0:T(8,128)(2,1)} %bitcast.4), channel_id=1, source_target_pairs={{0,6},{1,7},{2,5},{3,4},{4,2},{5,3},{6,1},{7,0},{8,14},{9,15},{10,... | collective-permute-start | bytes 98312 | tf_op jit(solution)/shard_map/ppermute | solution.py:278
  3.5 1.0 %collective-permute-start.1 = (bf16[128,128]{1,0:T(8,128)(2,1)}, bf16[128,128]{1,0:T(8,128)(2,1)S(1)}, u32[]{:S(2)}, u32[]{:S(2)}) collective-permute-start(bf16[128,128]{1,0:T(8,128)(2,1)} %bitcast.5), channel_id=1, source_target_pairs={{0,7},{1,6},{2,4},{3,5},{4,3},{5,2},{6,0},{7,1},{8,15},{9,14},{10,... | collective-permute-start | bytes 98312 | tf_op jit(solution)/shard_map/ppermute | solution.py:278
  4.5 0.8 %collective-permute-start.2 = (bf16[128,128]{1,0:T(8,128)(2,1)}, bf16[128,128]{1,0:T(8,128)(2,1)S(1)}, u32[]{:S(2)}, u32[]{:S(2)}) collective-permute-start(bf16[128,128]{1,0:T(8,128)(2,1)} %bitcast.6), channel_id=1, source_target_pairs={{0,5},{1,4},{2,7},{3,6},{4,1},{5,0},{6,3},{7,2},{8,13},{9,12},{10,... | collective-permute-start | bytes 98312 | tf_op jit(solution)/shard_map/ppermute | solution.py:278
  5.3 0.0 collective-permute-start.3
  6.0 0.0 copy-start
  6.0 0.6 %copy-done = s32[64]{0:T(128)S(1)} copy-done((s32[64]{0:T(128)S(1)}, s32[64]{0:T(128)}, u32[]{:S(2)}) %copy-start) | copy-done | bytes 280
  6.6 1.0 %shard_map.145 = (bf16[128,640]{1,0:T(8,128)(2,1)S(1)}, f32[1,128]{1,0:T(1,128)S(1)}, f32[1,128]{1,0:T(1,128)S(1)}, bf16[128,640]{1,0:T(8,128)(2,1)S(1)}, f32[1,128]{1,0:T(1,128)S(1)}, /*index=5*/f32[1,128]{1,0:T(1,128)S(1)}) custom-call(s32[1,64]{1,0:T(1,128)S(1)} %bitcast.3, s32[1]{0:T(128)S(6)} %copy.16.count_ref, bf16[1,128,128]{2,1,0:T(8,128)(2,1)} %refs_0_.1, ...), custom_call_target="tpu_custom_call" | custom-call | flops 1048576 | bytes 1048576 | tf_op jit(solution)/shard_map/pallas_call | solution.py:84
  7.7 0.0 collective-permute-done.refs_0_
  7.7 0.2 %collective-permute-done.1.refs_1_ = bf16[128,128]{1,0:T(8,128)(2,1)S(1)} collective-permute-done((bf16[128,128]{1,0:T(8,128)(2,1)}, bf16[128,128]{1,0:T(8,128)(2,1)S(1)}, u32[]{:S(2)}, u32[]{:S(2)}) %collective-permute-start.1) | collective-permute-done | bytes 32800 | tf_op jit(solution)/shard_map/ppermute | solution.py:278
  7.9 0.3 %collective-permute-done.2.refs_2_ = bf16[128,128]{1,0:T(8,128)(2,1)S(1)} collective-permute-done((bf16[128,128]{1,0:T(8,128)(2,1)}, bf16[128,128]{1,0:T(8,128)(2,1)S(1)}, u32[]{:S(2)}, u32[]{:S(2)}) %collective-permute-start.2) | collective-permute-done | bytes 32800 | tf_op jit(solution)/shard_map/ppermute | solution.py:278
  8.3 0.0 collective-permute-done.3.refs_3_
  8.3 1.1 %shard_map.146.refs_1_ = bf16[128,128]{1,0:T(8,128)(2,1)S(1)} custom-call(bf16[128,128]{1,0:T(8,128)(2,1)S(1)} %collective-permute-done.refs_0_, bf16[128,128]{1,0:T(8,128)(2,1)S(1)} %collective-permute-done.1.refs_1_, bf16[128,128]{1,0:T(8,128)(2,1)S(1)} %collective-permute-done.2.refs_2_, bf16[128,128]{1,0:T(8,128)(2,1)S(1)} %collective-permute-done.3.refs_3_, ...), custom_call_target="tpu_custom_call" | custom-call | tf_op jit(solution)/shard_map/pallas_call | solution.py:255
  9.4 1.9 %collective-permute-start.5 = (bf16[128,128]{1,0:T(8,128)(2,1)S(1)}, bf16[128,128]{1,0:T(8,128)(2,1)S(1)}, u32[]{:S(2)}, u32[]{:S(2)}) collective-permute-start(bf16[128,128]{1,0:T(8,128)(2,1)S(1)} %shard_map.146.refs_1_), channel_id=1, source_target_pairs={{0,12},{1,13},{2,14},{3,15},{4,8},{5,9},{6,10},{7,11},{8,20},{9,21... | collective-permute-start | bytes 98312 | tf_op jit(solution)/shard_map/ppermute | solution.py:278
  11.3 1.0 %collective-permute-start.6 = (bf16[128,128]{1,0:T(8,128)(2,1)S(1)}, bf16[128,128]{1,0:T(8,128)(2,1)S(1)}, u32[]{:S(2)}, u32[]{:S(2)}) collective-permute-start(bf16[128,128]{1,0:T(8,128)(2,1)S(1)} %shard_map.146.refs_1_), channel_id=1, source_target_pairs={{0,28},{1,29},{2,30},{3,31},{4,24},{5,25},{6,26},{7,27},{8,4},{9,5... | collective-permute-start | bytes 98312 | tf_op jit(solution)/shard_map/ppermute | solution.py:278
  12.4 1.7 %collective-permute-start.7 = (bf16[128,128]{1,0:T(8,128)(2,1)S(1)}, bf16[128,128]{1,0:T(8,128)(2,1)S(1)}, u32[]{:S(2)}, u32[]{:S(2)}) collective-permute-start(bf16[128,128]{1,0:T(8,128)(2,1)S(1)} %shard_map.146.refs_1_), channel_id=1, source_target_pairs={{0,20},{1,21},{2,22},{3,23},{4,16},{5,17},{6,18},{7,19},{8,28},{9,... | collective-permute-start | bytes 98312 | tf_op jit(solution)/shard_map/ppermute | solution.py:278
  14.0 0.3 %collective-permute-start.4 = (bf16[128,128]{1,0:T(8,128)(2,1)S(1)}, bf16[128,128]{1,0:T(8,128)(2,1)S(1)}, u32[]{:S(2)}, u32[]{:S(2)}) collective-permute-start(bf16[128,128]{1,0:T(8,128)(2,1)S(1)} %shard_map.146.refs_1_), channel_id=1, source_target_pairs={{0,4},{1,5},{2,6},{3,7},{4,0},{5,1},{6,2},{7,3},{8,12},{9,13},{10,... | collective-permute-start | bytes 98312 | tf_op jit(solution)/shard_map/ppermute | solution.py:278
  14.3 0.0 collective-permute-done.5.refs_2_
  14.3 0.3 %collective-permute-start.8 = (bf16[128,128]{1,0:T(8,128)(2,1)S(1)}, bf16[128,128]{1,0:T(8,128)(2,1)S(1)}, u32[]{:S(2)}, u32[]{:S(2)}) collective-permute-start(bf16[128,128]{1,0:T(8,128)(2,1)S(1)} %collective-permute-done.5.refs_2_), channel_id=1, source_target_pairs={{0,4},{1,5},{2,6},{3,7},{4,0},{5,1},{6,2},{7,3},{8,12},{9,13},{10,... | collective-permute-start | bytes 98312 | tf_op jit(solution)/shard_map/ppermute | solution.py:278
  14.5 0.5 %collective-permute-done.6.refs_3_ = bf16[128,128]{1,0:T(8,128)(2,1)S(1)} collective-permute-done((bf16[128,128]{1,0:T(8,128)(2,1)S(1)}, bf16[128,128]{1,0:T(8,128)(2,1)S(1)}, u32[]{:S(2)}, u32[]{:S(2)}) %collective-permute-start.6) | collective-permute-done | bytes 32800 | tf_op jit(solution)/shard_map/ppermute | solution.py:278
  15.0 0.5 %collective-permute-start.9 = (bf16[128,128]{1,0:T(8,128)(2,1)S(1)}, bf16[128,128]{1,0:T(8,128)(2,1)S(1)}, u32[]{:S(2)}, u32[]{:S(2)}) collective-permute-start(bf16[128,128]{1,0:T(8,128)(2,1)S(1)} %collective-permute-done.6.refs_3_), channel_id=1, source_target_pairs={{0,4},{1,5},{2,6},{3,7},{4,0},{5,1},{6,2},{7,3},{8,12},{9,13},{10,... | collective-permute-start | bytes 98312 | tf_op jit(solution)/shard_map/ppermute | solution.py:278
  15.5 0.2 %collective-permute-done.7.refs_4_ = bf16[128,128]{1,0:T(8,128)(2,1)S(1)} collective-permute-done((bf16[128,128]{1,0:T(8,128)(2,1)S(1)}, bf16[128,128]{1,0:T(8,128)(2,1)S(1)}, u32[]{:S(2)}, u32[]{:S(2)}) %collective-permute-start.7) | collective-permute-done | bytes 32800 | tf_op jit(solution)/shard_map/ppermute | solution.py:278
  15.7 0.4 %collective-permute-start.10 = (bf16[128,128]{1,0:T(8,128)(2,1)S(1)}, bf16[128,128]{1,0:T(8,128)(2,1)S(1)}, u32[]{:S(2)}, u32[]{:S(2)}) collective-permute-start(bf16[128,128]{1,0:T(8,128)(2,1)S(1)} %collective-permute-done.7.refs_4_), channel_id=1, source_target_pairs={{0,4},{1,5},{2,6},{3,7},{4,0},{5,1},{6,2},{7,3},{8,12},{9,13},{10,... | collective-permute-start | bytes 98312 | tf_op jit(solution)/shard_map/ppermute | solution.py:278
  16.1 0.0 collective-permute-done.4.refs_0_
  16.1 0.0 collective-permute-done.8.refs_5_
  16.1 0.2 %collective-permute-done.9.refs_6_ = bf16[128,128]{1,0:T(8,128)(2,1)S(1)} collective-permute-done((bf16[128,128]{1,0:T(8,128)(2,1)S(1)}, bf16[128,128]{1,0:T(8,128)(2,1)S(1)}, u32[]{:S(2)}, u32[]{:S(2)}) %collective-permute-start.9) | collective-permute-done | bytes 32800 | tf_op jit(solution)/shard_map/ppermute | solution.py:278
  16.4 0.5 %shard_map.147 = (bf16[128,128]{1,0:T(8,128)(2,1)S(1)}, f32[128,128]{1,0:T(8,128)S(1)}, bf16[896,128]{1,0:T(8,128)(2,1)S(1)}, bf16[896,128]{1,0:T(8,128)(2,1)S(1)}) custom-call(bf16[128,128]{1,0:T(8,128)(2,1)S(1)} %collective-permute-done.4.refs_0_, bf16[128,128]{1,0:T(8,128)(2,1)S(1)} %shard_map.146.refs_1_, ...), custom_call_target="tpu_custom_call" | custom-call | tf_op jit(solution)/shard_map/pallas_call | solution.py:234
  16.9 0.1 collective-permute-done.10.refs_5_
  17.0 1.7 %shard_map.148 = bf16[128,128]{1,0:T(8,128)(2,1)} custom-call(bf16[128,128]{1,0:T(8,128)(2,1)S(1)} %collective-permute-done.4.refs_0_, bf16[128,128]{1,0:T(8,128)(2,1)S(1)} %get-tuple-element.20.refs_1_, f32[128,128]{1,0:T(8,128)S(1)} %get-tuple-element.21.refs_2_, bf16[896,128]{1,0:T(8,128)(2,1)S(1)} %get-tuple-element.22.refs_3_, ...), custom_call_target="tpu_custom_call" | custom-call | tf_op jit(solution)/shard_map/pallas_call | solution.py:255
Async XLA Ops:
  0.0 7.7 %collective-permute-start = (bf16[128,128]{1,0:T(8,128)(2,1)}, bf16[128,128]{1,0:T(8,128)(2,1)S(1)}, u32[]{:S(2)}, u32[]{:S(2)}) collective-permute-start(bf16[128,128]{1,0:T(8,128)(2,1)} %bitcast.4), channel_id=1, source_target_pairs={{0,6},{1,7},{2,5},{3,4},{4,2},{5,3},{6,1},{7,0},{8,14},{9,15},{10,... | collective-permute-start | bytes 98312 | tf_op jit(solution)/shard_map/ppermute | solution.py:278
  3.5 4.5 %collective-permute-start.1 = (bf16[128,128]{1,0:T(8,128)(2,1)}, bf16[128,128]{1,0:T(8,128)(2,1)S(1)}, u32[]{:S(2)}, u32[]{:S(2)}) collective-permute-start(bf16[128,128]{1,0:T(8,128)(2,1)} %bitcast.5), channel_id=1, source_target_pairs={{0,7},{1,6},{2,4},{3,5},{4,3},{5,2},{6,0},{7,1},{8,15},{9,14},{10,... | collective-permute-start | bytes 98312 | tf_op jit(solution)/shard_map/ppermute | solution.py:278
  4.5 3.8 %collective-permute-start.2 = (bf16[128,128]{1,0:T(8,128)(2,1)}, bf16[128,128]{1,0:T(8,128)(2,1)S(1)}, u32[]{:S(2)}, u32[]{:S(2)}) collective-permute-start(bf16[128,128]{1,0:T(8,128)(2,1)} %bitcast.6), channel_id=1, source_target_pairs={{0,5},{1,4},{2,7},{3,6},{4,1},{5,0},{6,3},{7,2},{8,13},{9,12},{10,... | collective-permute-start | bytes 98312 | tf_op jit(solution)/shard_map/ppermute | solution.py:278
  5.3 2.9 %collective-permute-start.3 = (bf16[128,128]{1,0:T(8,128)(2,1)}, bf16[128,128]{1,0:T(8,128)(2,1)S(1)}, u32[]{:S(2)}, u32[]{:S(2)}) collective-permute-start(bf16[128,128]{1,0:T(8,128)(2,1)} %bitcast.7), channel_id=1, source_target_pairs={{0,4},{1,5},{2,6},{3,7},{4,0},{5,1},{6,2},{7,3},{8,12},{9,13},{10,... | collective-permute-start | bytes 98312 | tf_op jit(solution)/shard_map/ppermute | solution.py:278
  6.0 0.7 %copy-start = (s32[64]{0:T(128)S(1)}, s32[64]{0:T(128)}, u32[]{:S(2)}) copy-start(s32[64]{0:T(128)} %param.16) | copy-start | bytes 772
  9.4 4.9 %collective-permute-start.5 = (bf16[128,128]{1,0:T(8,128)(2,1)S(1)}, bf16[128,128]{1,0:T(8,128)(2,1)S(1)}, u32[]{:S(2)}, u32[]{:S(2)}) collective-permute-start(bf16[128,128]{1,0:T(8,128)(2,1)S(1)} %shard_map.146.refs_1_), channel_id=1, source_target_pairs={{0,12},{1,13},{2,14},{3,15},{4,8},{5,9},{6,10},{7,11},{8,20},{9,21... | collective-permute-start | bytes 98312 | tf_op jit(solution)/shard_map/ppermute | solution.py:278
  11.3 3.7 %collective-permute-start.6 = (bf16[128,128]{1,0:T(8,128)(2,1)S(1)}, bf16[128,128]{1,0:T(8,128)(2,1)S(1)}, u32[]{:S(2)}, u32[]{:S(2)}) collective-permute-start(bf16[128,128]{1,0:T(8,128)(2,1)S(1)} %shard_map.146.refs_1_), channel_id=1, source_target_pairs={{0,28},{1,29},{2,30},{3,31},{4,24},{5,25},{6,26},{7,27},{8,4},{9,5... | collective-permute-start | bytes 98312 | tf_op jit(solution)/shard_map/ppermute | solution.py:278
  12.4 3.3 %collective-permute-start.7 = (bf16[128,128]{1,0:T(8,128)(2,1)S(1)}, bf16[128,128]{1,0:T(8,128)(2,1)S(1)}, u32[]{:S(2)}, u32[]{:S(2)}) collective-permute-start(bf16[128,128]{1,0:T(8,128)(2,1)S(1)} %shard_map.146.refs_1_), channel_id=1, source_target_pairs={{0,20},{1,21},{2,22},{3,23},{4,16},{5,17},{6,18},{7,19},{8,28},{9,... | collective-permute-start | bytes 98312 | tf_op jit(solution)/shard_map/ppermute | solution.py:278
  14.0 2.1 %collective-permute-start.4 = (bf16[128,128]{1,0:T(8,128)(2,1)S(1)}, bf16[128,128]{1,0:T(8,128)(2,1)S(1)}, u32[]{:S(2)}, u32[]{:S(2)}) collective-permute-start(bf16[128,128]{1,0:T(8,128)(2,1)S(1)} %shard_map.146.refs_1_), channel_id=1, source_target_pairs={{0,4},{1,5},{2,6},{3,7},{4,0},{5,1},{6,2},{7,3},{8,12},{9,13},{10,... | collective-permute-start | bytes 98312 | tf_op jit(solution)/shard_map/ppermute | solution.py:278
  14.3 1.9 %collective-permute-start.8 = (bf16[128,128]{1,0:T(8,128)(2,1)S(1)}, bf16[128,128]{1,0:T(8,128)(2,1)S(1)}, u32[]{:S(2)}, u32[]{:S(2)}) collective-permute-start(bf16[128,128]{1,0:T(8,128)(2,1)S(1)} %collective-permute-done.5.refs_2_), channel_id=1, source_target_pairs={{0,4},{1,5},{2,6},{3,7},{4,0},{5,1},{6,2},{7,3},{8,12},{9,13},{10,... | collective-permute-start | bytes 98312 | tf_op jit(solution)/shard_map/ppermute | solution.py:278
  15.0 1.4 %collective-permute-start.9 = (bf16[128,128]{1,0:T(8,128)(2,1)S(1)}, bf16[128,128]{1,0:T(8,128)(2,1)S(1)}, u32[]{:S(2)}, u32[]{:S(2)}) collective-permute-start(bf16[128,128]{1,0:T(8,128)(2,1)S(1)} %collective-permute-done.6.refs_3_), channel_id=1, source_target_pairs={{0,4},{1,5},{2,6},{3,7},{4,0},{5,1},{6,2},{7,3},{8,12},{9,13},{10,... | collective-permute-start | bytes 98312 | tf_op jit(solution)/shard_map/ppermute | solution.py:278
  15.7 1.3 %collective-permute-start.10 = (bf16[128,128]{1,0:T(8,128)(2,1)S(1)}, bf16[128,128]{1,0:T(8,128)(2,1)S(1)}, u32[]{:S(2)}, u32[]{:S(2)}) collective-permute-start(bf16[128,128]{1,0:T(8,128)(2,1)S(1)} %collective-permute-done.7.refs_4_), channel_id=1, source_target_pairs={{0,4},{1,5},{2,6},{3,7},{4,0},{5,1},{6,2},{7,3},{8,12},{9,13},{10,... | collective-permute-start | bytes 98312 | tf_op jit(solution)/shard_map/ppermute | solution.py:278

commit v8 on v7

--- a/solution.py
+++ b/solution.py
@@ -28,15 +28,22 @@
     return pack, group
 
 
-def reverse(index, size):
-    bits = size.bit_length() - 1
-    return sum(((index >> b) & 1) << (bits - 1 - b) for b in range(bits))
-
-
-def prepare_kernel(axes, sources, parts, packs, mask_ref, count_ref, *refs):
-    weights, gate_biases, outs, sem = refs[:10], refs[10:12], refs[12:18], refs[18]
+def gray(index):
+    return index ^ (index >> 1)
+
+
+def gray_place(index, size):
+    place = index
+    for shift in range(1, size.bit_length() - 1):
+        place = place ^ (index >> shift)
+    return place
+
+
+def prepare_kernel(sources, parts, packs, mask_ref, count_ref, *refs):
+    weights, gate_biases, outs = refs[:10], refs[10:12], refs[12:18]
+    held_mask_ref, sem = refs[18:]
     channels = weights[0].shape[1]
-    copies = []
+    copies = [pltpu.make_async_copy(mask_ref, held_mask_ref, sem.at[0])]
     for a in range(2):
         for w in range(5):
             copies.append(
@@ -49,19 +56,20 @@
         copies.append(pltpu.make_async_copy(gate_biases[a], outs[3 * a + 1], sem.at[len(copies)]))
     for copy in copies:
         copy.start()
+    copies.pop(0).wait()
     regions = mask_ref.shape[1]
     place = lax.broadcasted_iota(jnp.int32, (8, regions), 1)
-    valid = ((mask_ref[...] == 1) | (place == 0)) & (place < count_ref[0])
+    valid = ((held_mask_ref[...] == 1) | (place == 0)) & (place < count_ref[0])
     valid = jnp.where(valid, 1.0, 0.0).astype(jnp.bfloat16)
+    me = lax.axis_index("orig"), lax.axis_index("dest")
     for a in range(2):
-        me = lax.axis_index(axes[a])
         part, pack = parts[a], packs[a]
         shape = (regions, pack * regions)
         lane = lax.broadcasted_iota(jnp.int32, (1, shape[1]), 1)
         block = lane // (part * pack)
         region = lane % part
         for b, source in enumerate(sources[a]):
-            region += jnp.where(block == b, source(me) * part, 0)
+            region += jnp.where(block == b, source(*me) * part, 0)
         hit = lax.broadcasted_iota(jnp.int32, shape, 0) == region
         found = jnp.dot(
             valid, jnp.where(hit, 1.0, 0.0).astype(jnp.bfloat16), preferred_element_type=jnp.float32
@@ -71,7 +79,7 @@
         copy.wait()
 
 
-def prepare(axes, sources, parts, packs, region_mask, region_count, weights, gate_biases):
+def prepare(sources, parts, packs, region_mask, region_count, weights, gate_biases):
     regions = region_mask.shape[0]
     channels = weights[0].shape[-1]
     outs = []
@@ -82,16 +90,16 @@
             pltpu.VMEM((1, pack * regions), jnp.float32),
         ]
     return pl.pallas_call(
-        functools.partial(prepare_kernel, axes, sources, parts, packs),
+        functools.partial(prepare_kernel, sources, parts, packs),
         out_shape=tuple(outs),
-        in_specs=[vmem, pl.BlockSpec(memory_space=pltpu.SMEM)]
+        in_specs=[pl.BlockSpec(memory_space=pltpu.HBM), pl.BlockSpec(memory_space=pltpu.SMEM)]
         + [pl.BlockSpec(memory_space=pltpu.HBM)] * 12,
         out_specs=(vmem,) * 6,
-        scratch_shapes=[pltpu.SemaphoreType.DMA((12,))],
+        scratch_shapes=[pltpu.VMEM((1, regions), jnp.int32), pltpu.SemaphoreType.DMA((13,))],
         compiler_params=pltpu.CompilerParams(vmem_limit_bytes=16 * 2**20),
         cost_estimate=pl.CostEstimate(flops=2**20, bytes_accessed=2**20, transcendentals=0),
     )(
-        region_mask.reshape(1, regions),
+        pltpu.with_memory_space_constraint(region_mask.reshape(1, regions), pltpu.HBM),
         region_count,
         *(pltpu.with_memory_space_constraint(w, pltpu.HBM) for w in (*weights, *gate_biases)),
     )
@@ -299,26 +307,28 @@
     dest_size = lax.axis_size("dest")
     orig_size = lax.axis_size("orig")
     regions = region_mask.shape[0]
-    row_steps = shifts(dest_size) + [0]
+    row_steps = [*range(1, dest_size), 0]
     chip_steps = shifts(orig_size // 2)
 
-    def along_dest(d, step):
-        return reverse((reverse(d, dest_size) + step) % dest_size, dest_size)
+    def along_dest(d, step, odd):
+        plain = (d + step) % dest_size
+        return plain + odd * (gray((gray_place(d, dest_size) + step) % dest_size) - plain)
 
     def along_orig(o, step, flip):
         return (o // 2 + step) % (orig_size // 2) * 2 + (o % 2 ^ flip)
 
-    row_sources = [lambda d, s=s: along_dest(d, dest_size - s) for s in row_steps]
-    col_sources = [lambda o: o, lambda o: o ^ 1]
+    row_sources = [
+        lambda o, d, s=s: along_dest(d, dest_size - s, 1 - o % 2) for s in row_steps
+    ]
+    col_sources = [lambda o, d: o, lambda o, d: o ^ 1]
     for flip in (0, 1):
         col_sources += [
-            lambda o, s=s, flip=flip: along_orig(o, orig_size // 2 - s, flip) for s in chip_steps
+            lambda o, d, s=s, flip=flip: along_orig(o, orig_size // 2 - s, flip) for s in chip_steps
         ]
     row_packing = packing(tile_rows, regions)
     col_packing = packing(tile_cols, regions)
     rows = tile_rows * tile_cols
     prepared = prepare(
-        ("dest", "orig"),
         (row_sources, col_sources),
         (tile_cols, tile_rows),
         (row_packing[0], col_packing[0]),
@@ -330,7 +340,7 @@
     )
 
     tile = pair_field.reshape(rows, channels)
-    blocks = [send(tile, lambda o, d: (o ^ 1, along_dest(d, s))) for s in row_steps]
+    blocks = [send(tile, lambda o, d: (o ^ 1, along_dest(d, s, o % 2))) for s in row_steps]
     turned = attend([], blocks, row_steps.index(0), tile_rows, row_packing, prepared[:3])
     own = send(turned, lambda o, d: (o ^ 1, d))
     near = [send(turned, lambda o, d: (along_orig(o, s, 1), d)) for s in chip_steps]

time: 18.9 us -> 18.6 us (0.984)
  local copies, waits for them, and re-layouts: 0.65 us -> 0 us
  waiting for transfers between devices: 1.58 us -> 1.82 us
    unnamed x2 -> x0, local copies, waits for them, and re-layouts: 0.65 us -> none
    ppermute x11, waiting for transfers between devices: 1.58 us -> 1.82 us  [send(): return lax.ppermute(values, ('orig', 'dest'), pairs)]
  transfers between devices with their start and end apart: 11 -> 11, of which waited for: 6 -> 5; matrix products, arithmetic and copies ran while one was open for 0% -> 0% of each run, Pallas kernels for 8% -> 9%
where the time goes in v8:
time: 18.6 us; the launch traced here: 18.4 us
  starting transfers between devices  11.5 us (62%)
  Pallas kernels  4.36 us (23%)
  waiting for transfers between devices  1.82 us (10%)
  between operations  0.69 us (4%)
    ppermute x11, starting transfers between devices, send(): return lax.ppermute(values, ('orig', 'dest'), pairs)  11.5 us
    pallas_call x2, Pallas kernels, attend(): pl.pallas_call(functools.partial(attend_kernel, bool(early), own, items,...  2.77 us
    ppermute x11, waiting for transfers between devices, send(): return lax.ppermute(values, ('orig', 'dest'), pairs)  1.82 us
    pallas_call x1, Pallas kernels, prepare(): pl.pallas_call(functools.partial(prepare_kernel, sources, parts, packs),...  1.06 us
    pallas_call x1, Pallas kernels, project(): pl.pallas_call(functools.partial(project_kernel, own), out_shape=(jax.Sha...  0.53 us
  transfers between devices with their start and end apart: 11, of which 5 were waited for; matrix products, arithmetic and copies ran while one was open for 0% of the time, Pallas kernels for 9%

profile of v8, /device:TPU:0, one launch (start us, length us, event | category | flops | bytes accessed | tf_op | source)
XLA Modules:
  0.0 18.4 jit_solution(16499704017480654834)
XLA Ops:
  0.0 2.5 %collective-permute-start = (bf16[128,128]{1,0:T(8,128)(2,1)}, bf16[128,128]{1,0:T(8,128)(2,1)S(1)}, u32[]{:S(2)}, u32[]{:S(2)}) collective-permute-start(bf16[128,128]{1,0:T(8,128)(2,1)} %bitcast.4), channel_id=1, source_target_pairs={{0,5},{1,6},{2,7},{3,4},{4,1},{5,3},{6,0},{7,2},{8,13},{9,14},{10,... | collective-permute-start | bytes 98312 | tf_op jit(solution)/shard_map/ppermute | solution.py:286
  2.5 1.0 %collective-permute-start.1 = (bf16[128,128]{1,0:T(8,128)(2,1)}, bf16[128,128]{1,0:T(8,128)(2,1)S(1)}, u32[]{:S(2)}, u32[]{:S(2)}) collective-permute-start(bf16[128,128]{1,0:T(8,128)(2,1)} %bitcast.5), channel_id=1, source_target_pairs={{0,6},{1,7},{2,4},{3,5},{4,3},{5,2},{6,1},{7,0},{8,14},{9,15},{10,... | collective-permute-start | bytes 98312 | tf_op jit(solution)/shard_map/ppermute | solution.py:286
  3.5 2.5 %collective-permute-start.2 = (bf16[128,128]{1,0:T(8,128)(2,1)}, bf16[128,128]{1,0:T(8,128)(2,1)S(1)}, u32[]{:S(2)}, u32[]{:S(2)}) collective-permute-start(bf16[128,128]{1,0:T(8,128)(2,1)} %bitcast.6), channel_id=1, source_target_pairs={{0,7},{1,4},{2,5},{3,6},{4,2},{5,0},{6,3},{7,1},{8,15},{9,12},{10,... | collective-permute-start | bytes 98312 | tf_op jit(solution)/shard_map/ppermute | solution.py:286
  6.0 0.0 collective-permute-start.3
  6.7 1.1 %shard_map.145 = (bf16[128,640]{1,0:T(8,128)(2,1)S(1)}, f32[1,128]{1,0:T(1,128)S(1)}, f32[1,128]{1,0:T(1,128)S(1)}, bf16[128,640]{1,0:T(8,128)(2,1)S(1)}, f32[1,128]{1,0:T(1,128)S(1)}, /*index=5*/f32[1,128]{1,0:T(1,128)S(1)}) custom-call(s32[1,64]{1,0:T(1,128)} %bitcast.3, s32[1]{0:T(128)S(6)} %copy.16.count_ref, bf16[1,128,128]{2,1,0:T(8,128)(2,1)} %refs_0_.1, ...), custom_call_target="tpu_custom_call" | custom-call | flops 1048576 | bytes 1048576 | tf_op jit(solution)/shard_map/pallas_call | solution.py:92
  7.7 0.0 collective-permute-done.refs_0_
  7.7 0.2 %collective-permute-done.1.refs_1_ = bf16[128,128]{1,0:T(8,128)(2,1)S(1)} collective-permute-done((bf16[128,128]{1,0:T(8,128)(2,1)}, bf16[128,128]{1,0:T(8,128)(2,1)S(1)}, u32[]{:S(2)}, u32[]{:S(2)}) %collective-permute-start.1) | collective-permute-done | bytes 32800 | tf_op jit(solution)/shard_map/ppermute | solution.py:286
  8.0 0.3 %collective-permute-done.2.refs_2_ = bf16[128,128]{1,0:T(8,128)(2,1)S(1)} collective-permute-done((bf16[128,128]{1,0:T(8,128)(2,1)}, bf16[128,128]{1,0:T(8,128)(2,1)S(1)}, u32[]{:S(2)}, u32[]{:S(2)}) %collective-permute-start.2) | collective-permute-done | bytes 32800 | tf_op jit(solution)/shard_map/ppermute | solution.py:286
  8.2 0.0 collective-permute-done.3.refs_3_
  8.2 1.1 %shard_map.146.refs_1_ = bf16[128,128]{1,0:T(8,128)(2,1)S(1)} custom-call(bf16[128,128]{1,0:T(8,128)(2,1)S(1)} %collective-permute-done.refs_0_, bf16[128,128]{1,0:T(8,128)(2,1)S(1)} %collective-permute-done.1.refs_1_, bf16[128,128]{1,0:T(8,128)(2,1)S(1)} %collective-permute-done.2.refs_2_, bf16[128,128]{1,0:T(8,128)(2,1)S(1)} %collective-permute-done.3.refs_3_, ...), custom_call_target="tpu_custom_call" | custom-call | tf_op jit(solution)/shard_map/pallas_call | solution.py:263
  9.4 1.6 %collective-permute-start.5 = (bf16[128,128]{1,0:T(8,128)(2,1)S(1)}, bf16[128,128]{1,0:T(8,128)(2,1)S(1)}, u32[]{:S(2)}, u32[]{:S(2)}) collective-permute-start(bf16[128,128]{1,0:T(8,128)(2,1)S(1)} %shard_map.146.refs_1_), channel_id=1, source_target_pairs={{0,12},{1,13},{2,14},{3,15},{4,8},{5,9},{6,10},{7,11},{8,20},{9,21... | collective-permute-start | bytes 98312 | tf_op jit(solution)/shard_map/ppermute | solution.py:286
  11.0 1.1 %collective-permute-start.6 = (bf16[128,128]{1,0:T(8,128)(2,1)S(1)}, bf16[128,128]{1,0:T(8,128)(2,1)S(1)}, u32[]{:S(2)}, u32[]{:S(2)}) collective-permute-start(bf16[128,128]{1,0:T(8,128)(2,1)S(1)} %shard_map.146.refs_1_), channel_id=1, source_target_pairs={{0,28},{1,29},{2,30},{3,31},{4,24},{5,25},{6,26},{7,27},{8,4},{9,5... | collective-permute-start | bytes 98312 | tf_op jit(solution)/shard_map/ppermute | solution.py:286
  12.0 1.6 %collective-permute-start.7 = (bf16[128,128]{1,0:T(8,128)(2,1)S(1)}, bf16[128,128]{1,0:T(8,128)(2,1)S(1)}, u32[]{:S(2)}, u32[]{:S(2)}) collective-permute-start(bf16[128,128]{1,0:T(8,128)(2,1)S(1)} %shard_map.146.refs_1_), channel_id=1, source_target_pairs={{0,20},{1,21},{2,22},{3,23},{4,16},{5,17},{6,18},{7,19},{8,28},{9,... | collective-permute-start | bytes 98312 | tf_op jit(solution)/shard_map/ppermute | solution.py:286
  13.7 0.2 %collective-permute-start.4 = (bf16[128,128]{1,0:T(8,128)(2,1)S(1)}, bf16[128,128]{1,0:T(8,128)(2,1)S(1)}, u32[]{:S(2)}, u32[]{:S(2)}) collective-permute-start(bf16[128,128]{1,0:T(8,128)(2,1)S(1)} %shard_map.146.refs_1_), channel_id=1, source_target_pairs={{0,4},{1,5},{2,6},{3,7},{4,0},{5,1},{6,2},{7,3},{8,12},{9,13},{10,... | collective-permute-start | bytes 98312 | tf_op jit(solution)/shard_map/ppermute | solution.py:286
  13.9 0.0 collective-permute-done.5.refs_2_
  13.9 0.3 %collective-permute-start.8 = (bf16[128,128]{1,0:T(8,128)(2,1)S(1)}, bf16[128,128]{1,0:T(8,128)(2,1)S(1)}, u32[]{:S(2)}, u32[]{:S(2)}) collective-permute-start(bf16[128,128]{1,0:T(8,128)(2,1)S(1)} %collective-permute-done.5.refs_2_), channel_id=1, source_target_pairs={{0,4},{1,5},{2,6},{3,7},{4,0},{5,1},{6,2},{7,3},{8,12},{9,13},{10,... | collective-permute-start | bytes 98312 | tf_op jit(solution)/shard_map/ppermute | solution.py:286
  14.2 0.5 %collective-permute-done.6.refs_3_ = bf16[128,128]{1,0:T(8,128)(2,1)S(1)} collective-permute-done((bf16[128,128]{1,0:T(8,128)(2,1)S(1)}, bf16[128,128]{1,0:T(8,128)(2,1)S(1)}, u32[]{:S(2)}, u32[]{:S(2)}) %collective-permute-start.6) | collective-permute-done | bytes 32800 | tf_op jit(solution)/shard_map/ppermute | solution.py:286
  14.6 0.2 %collective-permute-start.9 = (bf16[128,128]{1,0:T(8,128)(2,1)S(1)}, bf16[128,128]{1,0:T(8,128)(2,1)S(1)}, u32[]{:S(2)}, u32[]{:S(2)}) collective-permute-start(bf16[128,128]{1,0:T(8,128)(2,1)S(1)} %collective-permute-done.6.refs_3_), channel_id=1, source_target_pairs={{0,4},{1,5},{2,6},{3,7},{4,0},{5,1},{6,2},{7,3},{8,12},{9,13},{10,... | collective-permute-start | bytes 98312 | tf_op jit(solution)/shard_map/ppermute | solution.py:286
  14.8 0.5 %collective-permute-done.7.refs_4_ = bf16[128,128]{1,0:T(8,128)(2,1)S(1)} collective-permute-done((bf16[128,128]{1,0:T(8,128)(2,1)S(1)}, bf16[128,128]{1,0:T(8,128)(2,1)S(1)}, u32[]{:S(2)}, u32[]{:S(2)}) %collective-permute-start.7) | collective-permute-done | bytes 32800 | tf_op jit(solution)/shard_map/ppermute | solution.py:286
  15.4 0.5 %collective-permute-start.10 = (bf16[128,128]{1,0:T(8,128)(2,1)S(1)}, bf16[128,128]{1,0:T(8,128)(2,1)S(1)}, u32[]{:S(2)}, u32[]{:S(2)}) collective-permute-start(bf16[128,128]{1,0:T(8,128)(2,1)S(1)} %collective-permute-done.7.refs_4_), channel_id=1, source_target_pairs={{0,4},{1,5},{2,6},{3,7},{4,0},{5,1},{6,2},{7,3},{8,12},{9,13},{10,... | collective-permute-start | bytes 98312 | tf_op jit(solution)/shard_map/ppermute | solution.py:286
  15.9 0.0 collective-permute-done.4.refs_0_
  15.9 0.0 collective-permute-done.8.refs_5_
  15.9 0.0 collective-permute-done.9.refs_6_
  15.9 0.5 %shard_map.147 = (bf16[128,128]{1,0:T(8,128)(2,1)S(1)}, f32[128,128]{1,0:T(8,128)S(1)}, bf16[896,128]{1,0:T(8,128)(2,1)S(1)}, bf16[896,128]{1,0:T(8,128)(2,1)S(1)}) custom-call(bf16[128,128]{1,0:T(8,128)(2,1)S(1)} %collective-permute-done.4.refs_0_, bf16[128,128]{1,0:T(8,128)(2,1)S(1)} %shard_map.146.refs_1_, ...), custom_call_target="tpu_custom_call" | custom-call | tf_op jit(solution)/shard_map/pallas_call | solution.py:242
  16.4 0.3 %collective-permute-done.10.refs_5_ = bf16[128,128]{1,0:T(8,128)(2,1)S(1)} collective-permute-done((bf16[128,128]{1,0:T(8,128)(2,1)S(1)}, bf16[128,128]{1,0:T(8,128)(2,1)S(1)}, u32[]{:S(2)}, u32[]{:S(2)}) %collective-permute-start.10) | collective-permute-done | bytes 32800 | tf_op jit(solution)/shard_map/ppermute | solution.py:286
  16.7 1.7 %shard_map.148 = bf16[128,128]{1,0:T(8,128)(2,1)} custom-call(bf16[128,128]{1,0:T(8,128)(2,1)S(1)} %collective-permute-done.4.refs_0_, bf16[128,128]{1,0:T(8,128)(2,1)S(1)} %get-tuple-element.20.refs_1_, f32[128,128]{1,0:T(8,128)S(1)} %get-tuple-element.21.refs_2_, bf16[896,128]{1,0:T(8,128)(2,1)S(1)} %get-tuple-element.22.refs_3_, ...), custom_call_target="tpu_custom_call" | custom-call | tf_op jit(solution)/shard_map/pallas_call | solution.py:263
Async XLA Ops:
  0.0 7.7 %collective-permute-start = (bf16[128,128]{1,0:T(8,128)(2,1)}, bf16[128,128]{1,0:T(8,128)(2,1)S(1)}, u32[]{:S(2)}, u32[]{:S(2)}) collective-permute-start(bf16[128,128]{1,0:T(8,128)(2,1)} %bitcast.4), channel_id=1, source_target_pairs={{0,5},{1,6},{2,7},{3,4},{4,1},{5,3},{6,0},{7,2},{8,13},{9,14},{10,... | collective-permute-start | bytes 98312 | tf_op jit(solution)/shard_map/ppermute | solution.py:286
  2.5 5.5 %collective-permute-start.1 = (bf16[128,128]{1,0:T(8,128)(2,1)}, bf16[128,128]{1,0:T(8,128)(2,1)S(1)}, u32[]{:S(2)}, u32[]{:S(2)}) collective-permute-start(bf16[128,128]{1,0:T(8,128)(2,1)} %bitcast.5), channel_id=1, source_target_pairs={{0,6},{1,7},{2,4},{3,5},{4,3},{5,2},{6,1},{7,0},{8,14},{9,15},{10,... | collective-permute-start | bytes 98312 | tf_op jit(solution)/shard_map/ppermute | solution.py:286
  3.5 4.8 %collective-permute-start.2 = (bf16[128,128]{1,0:T(8,128)(2,1)}, bf16[128,128]{1,0:T(8,128)(2,1)S(1)}, u32[]{:S(2)}, u32[]{:S(2)}) collective-permute-start(bf16[128,128]{1,0:T(8,128)(2,1)} %bitcast.6), channel_id=1, source_target_pairs={{0,7},{1,4},{2,5},{3,6},{4,2},{5,0},{6,3},{7,1},{8,15},{9,12},{10,... | collective-permute-start | bytes 98312 | tf_op jit(solution)/shard_map/ppermute | solution.py:286
  6.0 2.2 %collective-permute-start.3 = (bf16[128,128]{1,0:T(8,128)(2,1)}, bf16[128,128]{1,0:T(8,128)(2,1)S(1)}, u32[]{:S(2)}, u32[]{:S(2)}) collective-permute-start(bf16[128,128]{1,0:T(8,128)(2,1)} %bitcast.7), channel_id=1, source_target_pairs={{0,4},{1,5},{2,6},{3,7},{4,0},{5,1},{6,2},{7,3},{8,12},{9,13},{10,... | collective-permute-start | bytes 98312 | tf_op jit(solution)/shard_map/ppermute | solution.py:286
  9.4 4.5 %collective-permute-start.5 = (bf16[128,128]{1,0:T(8,128)(2,1)S(1)}, bf16[128,128]{1,0:T(8,128)(2,1)S(1)}, u32[]{:S(2)}, u32[]{:S(2)}) collective-permute-start(bf16[128,128]{1,0:T(8,128)(2,1)S(1)} %shard_map.146.refs_1_), channel_id=1, source_target_pairs={{0,12},{1,13},{2,14},{3,15},{4,8},{5,9},{6,10},{7,11},{8,20},{9,21... | collective-permute-start | bytes 98312 | tf_op jit(solution)/shard_map/ppermute | solution.py:286
  11.0 3.6 %collective-permute-start.6 = (bf16[128,128]{1,0:T(8,128)(2,1)S(1)}, bf16[128,128]{1,0:T(8,128)(2,1)S(1)}, u32[]{:S(2)}, u32[]{:S(2)}) collective-permute-start(bf16[128,128]{1,0:T(8,128)(2,1)S(1)} %shard_map.146.refs_1_), channel_id=1, source_target_pairs={{0,28},{1,29},{2,30},{3,31},{4,24},{5,25},{6,26},{7,27},{8,4},{9,5... | collective-permute-start | bytes 98312 | tf_op jit(solution)/shard_map/ppermute | solution.py:286
  12.0 3.3 %collective-permute-start.7 = (bf16[128,128]{1,0:T(8,128)(2,1)S(1)}, bf16[128,128]{1,0:T(8,128)(2,1)S(1)}, u32[]{:S(2)}, u32[]{:S(2)}) collective-permute-start(bf16[128,128]{1,0:T(8,128)(2,1)S(1)} %shard_map.146.refs_1_), channel_id=1, source_target_pairs={{0,20},{1,21},{2,22},{3,23},{4,16},{5,17},{6,18},{7,19},{8,28},{9,... | collective-permute-start | bytes 98312 | tf_op jit(solution)/shard_map/ppermute | solution.py:286
  13.7 2.2 %collective-permute-start.4 = (bf16[128,128]{1,0:T(8,128)(2,1)S(1)}, bf16[128,128]{1,0:T(8,128)(2,1)S(1)}, u32[]{:S(2)}, u32[]{:S(2)}) collective-permute-start(bf16[128,128]{1,0:T(8,128)(2,1)S(1)} %shard_map.146.refs_1_), channel_id=1, source_target_pairs={{0,4},{1,5},{2,6},{3,7},{4,0},{5,1},{6,2},{7,3},{8,12},{9,13},{10,... | collective-permute-start | bytes 98312 | tf_op jit(solution)/shard_map/ppermute | solution.py:286
  13.9 2.0 %collective-permute-start.8 = (bf16[128,128]{1,0:T(8,128)(2,1)S(1)}, bf16[128,128]{1,0:T(8,128)(2,1)S(1)}, u32[]{:S(2)}, u32[]{:S(2)}) collective-permute-start(bf16[128,128]{1,0:T(8,128)(2,1)S(1)} %collective-permute-done.5.refs_2_), channel_id=1, source_target_pairs={{0,4},{1,5},{2,6},{3,7},{4,0},{5,1},{6,2},{7,3},{8,12},{9,13},{10,... | collective-permute-start | bytes 98312 | tf_op jit(solution)/shard_map/ppermute | solution.py:286
  14.6 1.3 %collective-permute-start.9 = (bf16[128,128]{1,0:T(8,128)(2,1)S(1)}, bf16[128,128]{1,0:T(8,128)(2,1)S(1)}, u32[]{:S(2)}, u32[]{:S(2)}) collective-permute-start(bf16[128,128]{1,0:T(8,128)(2,1)S(1)} %collective-permute-done.6.refs_3_), channel_id=1, source_target_pairs={{0,4},{1,5},{2,6},{3,7},{4,0},{5,1},{6,2},{7,3},{8,12},{9,13},{10,... | collective-permute-start | bytes 98312 | tf_op jit(solution)/shard_map/ppermute | solution.py:286
  15.4 1.3 %collective-permute-start.10 = (bf16[128,128]{1,0:T(8,128)(2,1)S(1)}, bf16[128,128]{1,0:T(8,128)(2,1)S(1)}, u32[]{:S(2)}, u32[]{:S(2)}) collective-permute-start(bf16[128,128]{1,0:T(8,128)(2,1)S(1)} %collective-permute-done.7.refs_4_), channel_id=1, source_target_pairs={{0,4},{1,5},{2,6},{3,7},{4,0},{5,1},{6,2},{7,3},{8,12},{9,13},{10,... | collective-permute-start | bytes 98312 | tf_op jit(solution)/shard_map/ppermute | solution.py:286
